TPU v7x, 512 devices: a whole 4x8x8 slice. The times are simulated.
512 devices in a mesh: vid: 64 (over y_hi, x, z), aud: 4 (over y_lo), tp: 2 (over core).
Axes of the slice: x: 4, y: 8 (y_hi: 2, y_lo: 4; y = y_hi * 4 + y_lo), z: 8, core: 2. Of those that a mesh axis runs over, the one named last changes fastest.
Arguments:
- video_proj: bfloat16 [4, 8192, 3072], P(None, ('vid', 'aud'), 'tp'), may hold values from -125 to 125
- audio_proj: bfloat16 [4, 2048, 3072], P(None, ('vid', 'aud'), 'tp'), may hold values from -125 to 125
- video_gains: float32 [3, 3072], P(None, 'tp'), may hold values from 1.2 to 2
- audio_gains: float32 [3, 3072], P(None, 'tp'), may hold values from 1.2 to 2
- cross_gates: bfloat16 [2, 50, 3072], P(None, None, 'tp'), may hold values from 0.19921875 to 2
- timestep: int32 [1], replicated, may hold values from 0 to 49
- video_counts: int32 [64], replicated, may hold values from 64 to 128, as said below
- audio_counts: int32 [64], replicated, may hold values from 16 to 32, as said below
Outputs:
- video_mixed: bfloat16 [8192, 3072], P(('vid', 'aud'), 'tp')
- audio_mixed: bfloat16 [2048, 3072], P(('vid', 'aud'), 'tp')
Inputs may be any that keep to these rules, and one draw needn't show every extreme that they name: `video_counts`: entry s counts the live video tokens of vid shard s, which are its first ones; the others are padding that no query attends to; some shard is full. `audio_counts`: entry s counts the live audio tokens of vid shard s, which are its first ones; the others are padding that no query attends to; some shard is full.
All inputs are finite; a program needn't handle non-finite values.
Results may differ from a plain program's by a relative error of at most 0.011.
Values may be sent and summed in bfloat16 or wider, within the bound.
No kernel may reach another device: no remote copies, remote signals or barrier semaphores. Data moves between devices by JAX's collectives and lax.ppermute only.
A program may use at most 64 MiB of HBM per device.

v0:
```python
import math

import jax
import jax.numpy as jnp
from jax import lax
from jax.sharding import PartitionSpec as P

D = 3072
HD = 128
VTOK_DEV = 128
ATOK_DEV = 32


EPSILON = 1e-06
FLOOR_SCORE = -1e30


def normalize(raw_rows, mean_square, gain_rows):
    scaled_rows = raw_rows.astype(jnp.float32) * lax.rsqrt(mean_square + EPSILON)[..., None]
    return (scaled_rows * gain_rows[:, None, :]).astype(jnp.bfloat16)


def square_sums(raw_rows):
    values_f = raw_rows[:3].astype(jnp.float32)
    return jnp.sum(values_f * values_f, axis=2)


def live_keys(positions, counts, tok_shard):
    shard_of = positions // tok_shard
    within = positions - shard_of * tok_shard
    shard_ids = jnp.arange(counts.shape[0], dtype=jnp.int32)
    allowed = jnp.sum(
        jnp.where(shard_of[:, None] == shard_ids[None, :], counts[None, :], 0), axis=1
    )
    return within < allowed


def initial_state(query_count, heads_here):
    return (
        jnp.full((heads_here, query_count), FLOOR_SCORE, jnp.float32),
        jnp.zeros((heads_here, query_count), jnp.float32),
        jnp.zeros((heads_here, query_count, HD), jnp.float32),
    )


def fold_keys(queries, counts, tok_shard, running, key_piece):
    key_rows, value_rows = key_piece
    piece_len = key_rows.shape[0]
    block_len = math.gcd(piece_len, 1024)
    heads_here = key_rows.shape[1] // HD
    scale_factor = HD ** (-0.5)
    key_blocks = key_rows.reshape(piece_len // block_len, block_len, heads_here, HD)
    value_blocks = value_rows.reshape(piece_len // block_len, block_len, heads_here, HD)
    offsets = jnp.arange(piece_len // block_len, dtype=jnp.int32) * block_len

    def one_block(state, operands):
        key_block, value_block, offset = operands
        positions = offset + jnp.arange(block_len, dtype=jnp.int32)
        allowed = live_keys(positions, counts, tok_shard)
        scores = (
            jnp.einsum("qhd,khd->hqk", queries, key_block, preferred_element_type=jnp.float32)
            * scale_factor
        )
        scores = jnp.where(allowed[None, None, :], scores, -jnp.inf)
        top_old, total_old, accum = state
        top_new = jnp.maximum(top_old, jnp.max(scores, axis=2))
        rescale = jnp.exp(top_old - top_new)
        weights = jnp.exp(scores - top_new[..., None])
        total_new = total_old * rescale + jnp.sum(weights, axis=2)
        update = jnp.einsum(
            "hqk,khd->hqd",
            weights.astype(jnp.bfloat16),
            value_block,
            preferred_element_type=jnp.float32,
        )
        return ((top_new, total_new, accum * rescale[..., None] + update), None)

    running, ignored = lax.scan(one_block, running, (key_blocks, value_blocks, offsets))
    return running


def finish(running):
    top_new, total_new, accum = running
    outputs = accum / total_new[..., None]
    return outputs.transpose(1, 0, 2).reshape(outputs.shape[1], outputs.shape[0] * HD)


def shards(
    video_proj,
    audio_proj,
    video_gains,
    audio_gains,
    cross_gates,
    timestep,
    video_counts,
    audio_counts,
):
    width_here = video_proj.shape[2] // lax.axis_size("aud")
    heads_here = width_here // HD
    aud_index = lax.axis_index("aud")
    video_square, audio_square = lax.psum((square_sums(video_proj), square_sums(audio_proj)), "tp")
    video_send = jnp.concatenate(
        [normalize(video_proj[:3], video_square / D, video_gains), video_proj[3:]], axis=0
    )
    audio_send = jnp.concatenate(
        [normalize(audio_proj[:3], audio_square / D, audio_gains), audio_proj[3:]], axis=0
    )
    video_heads, audio_heads = (
        lax.all_to_all(video_send, "aud", split_axis=2, concat_axis=1, tiled=True),
        lax.all_to_all(audio_send, "aud", split_axis=2, concat_axis=1, tiled=True),
    )
    video_rows = video_heads.shape[1]

    def split_heads(feature_rows):
        return feature_rows.reshape(feature_rows.shape[0], heads_here, HD)

    video_queries = split_heads(jnp.concatenate([video_heads[0], audio_heads[1]], axis=0))
    audio_queries = split_heads(jnp.concatenate([video_heads[1], audio_heads[0]], axis=0))
    audio_state = fold_keys(
        audio_queries,
        audio_counts,
        ATOK_DEV,
        initial_state(audio_queries.shape[0], heads_here),
        (
            lax.all_gather(audio_heads[2], "vid", axis=0, tiled=True),
            lax.all_gather(audio_heads[3], "vid", axis=0, tiled=True),
        ),
    )
    video_state = fold_keys(
        video_queries,
        video_counts,
        VTOK_DEV,
        initial_state(video_queries.shape[0], heads_here),
        (
            lax.all_gather(video_heads[2], "vid", axis=0, tiled=True),
            lax.all_gather(video_heads[3], "vid", axis=0, tiled=True),
        ),
    )
    video_result = finish(video_state)
    audio_result = finish(audio_state)
    video_self = video_result[:video_rows]
    audio_cross = video_result[video_rows:]
    video_cross = audio_result[:video_rows]
    audio_self = audio_result[video_rows:]
    selector = (jnp.arange(cross_gates.shape[1], dtype=jnp.int32) == timestep[0]).astype(
        jnp.float32
    )
    gate_rows = jnp.einsum("s,tsd->td", selector, cross_gates.astype(jnp.float32))
    gate_here = lax.dynamic_slice_in_dim(gate_rows, aud_index * width_here, width_here, 1)
    video_mixed = (video_self + gate_here[0][None, :] * video_cross).astype(jnp.bfloat16)
    audio_mixed = (audio_self + gate_here[1][None, :] * audio_cross).astype(jnp.bfloat16)
    video_back, audio_back = (
        lax.all_to_all(video_mixed, "aud", split_axis=0, concat_axis=1, tiled=True),
        lax.all_to_all(audio_mixed, "aud", split_axis=0, concat_axis=1, tiled=True),
    )
    return (video_back, audio_back)


def solution(mesh):
    in_specs = (
        P(None, ("vid", "aud"), "tp"),
        P(None, ("vid", "aud"), "tp"),
        P(None, "tp"),
        P(None, "tp"),
        P(None, None, "tp"),
        P(),
        P(),
        P(),
    )
    out_specs = (P(("vid", "aud"), "tp"), P(("vid", "aud"), "tp"))
    return jax.shard_map(shards, mesh=mesh, in_specs=in_specs, out_specs=out_specs, check_vma=False)
```

profile of v0, /device:TPU:1, one launch (start us, length us, event | category | flops | bytes accessed | tf_op | source)
XLA Modules:
  0.0 732.0 jit_solution(8917095012392709767)
XLA Ops:
  10.1 9.0 %all-reduce = (f32[3,32]{1,0:T(4,128)S(1)}, f32[3,8]{1,0:T(4,128)S(1)}) all-reduce(f32[3,32]{1,0:T(4,128)S(1)} %fusion.42, f32[3,8]{1,0:T(4,128)S(1)} %fusion.47), channel_id=1, replica_groups=mesh['vid'=64,'aud'=4,'tp'=2] {'tp'}, use_global_device_ids=true, to_apply=%region_1.0 | all-reduce | flops 120 | bytes 960 | tf_op jit(solution)/shard_map/psum | solution.py:101
  21.1 1.8 reshape.182
  22.9 7.2 all_to_all.62
  30.0 1.8 reshape.183
  37.1 13.2 %all_to_all.63 = bf16[4,2,24576]{2,1,0:T(2,128)(2,1)S(1)} all-to-all(bf16[4,2,24576]{2,1,0:T(2,128)(2,1)S(1)} %reshape.180), channel_id=1, replica_groups=mesh['vid'=64,'aud'=4,'tp'=2] {'aud'}, dimensions={0} | all-to-all | bytes 786432 | tf_op jit(solution)/shard_map/all_to_all | solution.py:109
  55.4 103.5 %all-gather.9.cloned.1.call-done = bf16[2048,384]{1,0:T(8,128)(2,1)} async-done(((bf16[32,384]{1,0:T(8,128)(2,1)}), bf16[2048,384]{1,0:T(8,128)(2,1)}) %all-gather.9.cloned.1.call-update) | async-done | bytes 1572880 | tf_op jit(solution)/shard_map/all_gather | solution.py:125
  158.9 3.9 reshape.176
  164.2 125.1 %all-gather.11.cloned.1.call-done = bf16[2048,384]{1,0:T(8,128)(2,1)} async-done(((bf16[32,384]{1,0:T(8,128)(2,1)}), bf16[2048,384]{1,0:T(8,128)(2,1)}) %all-gather.11.cloned.1.call-update) | async-done | bytes 1572880 | tf_op jit(solution)/shard_map/all_gather | solution.py:126
  289.3 3.9 reshape.177
  294.7 11.5 %while.35 = (s32[]{:T(128)}, f32[3,160]{1,0:T(4,128)S(1)}, f32[3,160]{1,0:T(4,128)S(1)}, f32[3,160,128]{2,1,0:T(8,128)S(1)}, s32[2]{0:T(128)S(1)}, /*index=5*/s3...) while((s32[]{:T(128)}, f32[3,160]{1,0:T(4,128)S(1)}, ...), condition=%wide.region_13.14_spmd.clone, body=%wide.region_9.13_spmd.clone.sunk | while | flops 257483104 | bytes 14433453 | solution.py:78
  306.7 155.8 %all-gather.5.cloned.1.call-done = bf16[8192,384]{1,0:T(8,128)(2,1)} async-done(((bf16[128,384]{1,0:T(8,128)(2,1)}), bf16[8192,384]{1,0:T(8,128)(2,1)}) %all-gather.5.cloned.1.call-update) | async-done | bytes 6291472 | tf_op jit(solution)/shard_map/all_gather | solution.py:135
  462.5 16.7 %reshape.174 = bf16[8,1024,3,128]{3,2,1,0:T(4,128)(2,1)} reshape(bf16[8192,384]{1,0:T(8,128)(2,1)} %all-gather.5.cloned.1.call-done) | data formatting | bytes 12582912 | tf_op jit(solution)/shard_map/reshape | solution.py:52
  479.1 7.6 %copy.173 = bf16[8,1024,3,128]{3,1,2,0:T(8,128)(2,1)} copy(bf16[8,1024,3,128]{3,2,1,0:T(4,128)(2,1)} %reshape.174) | data formatting | bytes 12582912
  486.8 146.7 %all-gather.7.cloned.1.call-done = bf16[8192,384]{1,0:T(8,128)(2,1)} async-done(((bf16[128,384]{1,0:T(8,128)(2,1)}), bf16[8192,384]{1,0:T(8,128)(2,1)}) %all-gather.7.cloned.1.call-update) | async-done | bytes 6291472 | tf_op jit(solution)/shard_map/all_gather | solution.py:136
  633.5 16.7 %reshape.175 = bf16[8,1024,3,128]{3,2,1,0:T(4,128)(2,1)} reshape(bf16[8192,384]{1,0:T(8,128)(2,1)} %all-gather.7.cloned.1.call-done) | data formatting | bytes 12582912 | tf_op jit(solution)/shard_map/reshape | solution.py:53
  650.1 7.7 %copy.175 = bf16[8,1024,3,128]{3,1,2,0:T(8,128)(2,1)} copy(bf16[8,1024,3,128]{3,2,1,0:T(4,128)(2,1)} %reshape.175) | data formatting | bytes 12582912
  657.8 48.6 %while.34 = (s32[]{:T(128)}, f32[3,160]{1,0:T(4,128)S(1)}, f32[3,160]{1,0:T(4,128)S(1)}, f32[3,160,128]{2,1,0:T(8,128)S(1)}, s32[8]{0:T(128)S(1)}, /*index=5*/s3...) while((s32[]{:T(128)}, f32[3,160]{1,0:T(4,128)S(1)}, ...), condition=%wide.region_8.9_spmd.clone, body=%wide.region_4.8_spmd.clone.sunk | while | flops 257483104 | bytes 8138125 | solution.py:78
  662.1 1.8 convolution_add_fusion.4
  665.9 1.7 bitcast_reduce_fusion.4
  668.2 1.8 convolution_add_fusion.4
  672.0 1.7 bitcast_reduce_fusion.4
  674.3 1.8 convolution_add_fusion.4
  678.1 1.7 bitcast_reduce_fusion.4
  680.3 1.8 convolution_add_fusion.4
  686.4 1.8 convolution_add_fusion.4
  692.5 1.8 convolution_add_fusion.4
  698.6 1.8 convolution_add_fusion.4
  704.7 1.8 convolution_add_fusion.4
  707.3 4.4 all-to-all-start.3
  712.7 3.6 all-to-all-done.3
  716.2 3.3 all-to-all-start.2
  719.5 4.6 all-to-all-done.2
  (179 shorter events, 60.9 us)
Async XLA Ops:
  7.2 47.4 %copy-start = (bf16[2,50,1536]{2,0,1:T(2,128)(2,1)S(1)}, bf16[2,50,1536]{2,0,1:T(2,128)(2,1)}, u32[]{:S(2)}) copy-start(bf16[2,50,1536]{2,0,1:T(2,128)(2,1)} %param.16) | copy-start | bytes 921604
  7.2 151.7 %all-gather.9.cloned.1.call-start = ((), (), s32[]{:S(2)}) async-start(), calls=%async_computation.6 | async-start | bytes 1597440 | tf_op jit(solution)/shard_map/all_gather | solution.py:125
  30.0 4.3 copy-start.3
  30.0 4.3 copy-start.4
  30.0 4.4 slice-start
  33.5 255.9 %all-gather.11.cloned.1.call-start = ((), (), s32[]{:S(2)}) async-start(), calls=%async_computation.7 | async-start | bytes 1597440 | tf_op jit(solution)/shard_map/all_gather | solution.py:126
  34.2 428.3 %all-gather.5.cloned.1.call-start = ((), (), s32[]{:S(2)}) async-start(), calls=%async_computation.4 | async-start | bytes 6389760 | tf_op jit(solution)/shard_map/all_gather | solution.py:135
  53.0 580.5 %all-gather.7.cloned.1.call-start = ((), (), s32[]{:S(2)}) async-start(), calls=%async_computation.5 | async-start | bytes 6389760 | tf_op jit(solution)/shard_map/all_gather | solution.py:136
  293.3 1.4 copy-start.5
  298.4 1.4 copy-start.2
  304.1 1.4 copy-start.2
  650.1 7.7 %copy-start.6 = (s32[64]{0:T(128)S(1)}, s32[64]{0:T(128)}, u32[]{:S(2)}) copy-start(s32[64]{0:T(128)} %param.18) | copy-start | bytes 772
  706.5 19.0 %copy-start.1 = (bf16[2,50,1536]{2,0,1:T(2,128)(2,1)S(1)}, bf16[2,50,1536]{2,0,1:T(2,128)(2,1)}, u32[]{:S(2)}) copy-start(bf16[2,50,1536]{2,0,1:T(2,128)(2,1)} %param.16) | copy-start | bytes 921604
  707.3 8.9 %all-to-all-start.3 = ((bf16[4,8,384]{2,1,0:T(8,128)(2,1)}), bf16[4,8,384]{2,1,0:T(8,128)(2,1)S(1)}, u32[]{:S(2)}, u32[]{:S(2)}) async-start(bf16[4,8,384]{2,1,0:T(8,128)(2,1)} %add_convert_fusion.1), calls=%async_computation.3 | async-start | bytes 49152 | tf_op jit(solution)/shard_map/all_to_all | solution.py:154
  716.2 8.0 %all-to-all-start.2 = ((bf16[4,32,384]{2,1,0:T(8,128)(2,1)}), bf16[4,32,384]{2,1,0:T(8,128)(2,1)S(1)}, u32[]{:S(2)}, u32[]{:S(2)}) async-start(bf16[4,32,384]{2,1,0:T(8,128)(2,1)} %add_convert_fusion), calls=%async_computation.2 | async-start | bytes 196608 | tf_op jit(solution)/shard_map/all_to_all | solution.py:153
Sparse Core Ops, SparseCore 0:
  33.6 125.2 all-gather.8
  163.5 125.8 all-gather.10
  294.5 167.9 all-gather.4
  466.9 166.5 all-gather.6
where the time goes:
time: 741 us; the launch traced here: 732 us
  waiting for transfers between devices  539 us (73%)
  local copies, waits for them, and re-layouts  82.3 us (11%)
  matrix products  32.2 us (4%)
  blocking collectives  29.4 us (4%)
  other arithmetic  25.1 us (3%)
  between operations  14.9 us (2%)
  starting transfers between devices  8.05 us (1%)
    all_gather x1, waiting for transfers between devices, shards(): lax.all_gather(video_heads[2], 'vid', axis=0, tiled=True)  156 us
    all_gather x1, waiting for transfers between devices, shards(): lax.all_gather(video_heads[3], 'vid', axis=0, tiled=True)  147 us
    all_gather x1, waiting for transfers between devices, shards(): lax.all_gather(audio_heads[3], 'vid', axis=0, tiled=True)  125 us
    all_gather x1, waiting for transfers between devices, shards(): lax.all_gather(audio_heads[2], 'vid', axis=0, tiled=True)  104 us
    unnamed x23, local copies, waits for them, and re-layouts  24.7 us
    reshape x2, local copies, waits for them, and re-layouts, fold_keys(): key_rows.reshape(piece_len // block_len, block_len, heads_here, HD)  20.6 us
    reshape x2, local copies, waits for them, and re-layouts, fold_keys(): value_rows.reshape(piece_len // block_len, block_len, heads_here, HD)  20.6 us
    dot_general x10, matrix products, one_block(): jnp.einsum('qhd,khd->hqk', queries, key_block, preferred_element_type=jnp...  16.6 us
  transfers between devices with their start and end apart: 6, of which 6 were waited for; matrix products, arithmetic and copies ran while one was open for 7% of the time, Pallas kernels for 0%

commit v1 on v0

v1 whole, which is shorter than its diff:
```python
import math

import jax
import jax.numpy as jnp
import numpy as np
from jax import lax
from jax.experimental import pallas as pl
from jax.experimental.pallas import tpu as pltpu
from jax.sharding import Mesh
from jax.sharding import PartitionSpec as P

D = 3072
HD = 128
VTOK_DEV = 128
ATOK_DEV = 32
EPSILON = 1e-06
MASKED = -1e30

YH = 2
NY = 8
NZ = 8
GROUP = D // NY
HEADS_HERE = GROUP // HD
VROWS = 16
AROWS = 4
BLOCK = 2 * VROWS + 2 * AROWS
OUT_ROWS = 2 * (VTOK_DEV + ATOK_DEV)
STAT_ROWS = OUT_ROWS // 8
BACK_ROWS = VROWS + 8
SCORE_SCALE = HD ** (-0.5) * math.log2(math.e)
VMEM_LIMIT = 48 * 1024 * 1024


def low_rows(shape):
    return lax.broadcasted_iota(jnp.int32, shape, len(shape) - 2) % 8 < 4


def swap_halves(rows):
    return pltpu.roll(rows, 4, axis=rows.ndim - 2)


def norm_kernel(core_ref, video_ref, audio_ref, gains_ref, query_ref, keyval_ref):
    core = core_ref[0]
    first = pl.multiple_of(core * VROWS, VROWS)
    half_groups = NY // 2

    def normed(halves, gain_row, extra):
        values = [half.astype(jnp.float32) for half in halves]
        total = sum(jnp.sum(v * v, axis=1, keepdims=True) for v in values)
        inverse = lax.rsqrt(total / D + EPSILON)
        return [
            v * inverse * (gains_ref[s, gain_row : gain_row + 1, :] * extra)
            for s, v in enumerate(values)
        ]

    def spread(out_ref, row, halves):
        count = halves[0].shape[0]
        for group in range(NY):
            col = (group % half_groups) * GROUP
            out_ref[group, row : row + count, :] = halves[group // half_groups][
                :, col : col + GROUP
            ].astype(jnp.bfloat16)

    def video(array):
        return [video_ref[s, array, pl.ds(first, VROWS), :] for s in range(2)]

    def audio(array):
        return [audio_ref[s, array, :, :] for s in range(2)]

    spread(keyval_ref, 0, normed(video(2), 2, 1.0))
    spread(keyval_ref, VROWS, video(3))
    audio_key = normed(audio(2), 5, 1.0)
    audio_value = [half.astype(jnp.float32) for half in audio(3)]
    spread(
        keyval_ref,
        2 * VROWS,
        [jnp.where(core == 0, k, v) for k, v in zip(audio_key, audio_value)],
    )
    spread(query_ref, 0, normed(video(0), 0, SCORE_SCALE))
    spread(query_ref, VROWS, normed(video(1), 1, SCORE_SCALE))
    audio_self = normed(audio(0), 3, SCORE_SCALE)
    audio_cross = normed(audio(1), 4, SCORE_SCALE)
    mixed = []
    for own, other in zip(audio_self, audio_cross):
        low = low_rows(own.shape)
        mixed.append(
            jnp.where(
                core == 0,
                jnp.where(low, own, swap_halves(other)),
                jnp.where(low, swap_halves(own), other),
            )
        )
    spread(query_ref, 2 * VROWS, mixed)


def attend_kernel(query_ref, keyval_ref, video_bias_ref, audio_bias_ref, out_ref):
    x_count = query_ref.shape[0]
    z_count = keyval_ref.shape[1]
    video_keys = 2 * z_count * NY * VROWS
    audio_keys = z_count * NY * 8
    video_key = keyval_ref[:, :, :, :VROWS, :].reshape(video_keys, HD)
    video_value = keyval_ref[:, :, :, VROWS : 2 * VROWS, :].reshape(video_keys, HD)

    def audio_part(which):
        rows = keyval_ref[which, :, :, 2 * VROWS :, :].astype(jnp.float32)
        return rows.reshape(audio_keys, HD).astype(jnp.bfloat16)

    audio_key, audio_value = audio_part(0), audio_part(1)
    lane = lax.broadcasted_iota(jnp.int32, (1, 8, HD), 2)
    row = lax.broadcasted_iota(jnp.int32, (1, 8, HD), 1)
    in_row = lane // 16 == row
    field = lane % 16

    def attend(queries, key, value, bias_ref):
        scores = lax.dot_general(
            queries, key, (((1,), (1,)), ((), ())), preferred_element_type=jnp.float32
        )
        scores = scores + bias_ref[0:1, :]
        top = jnp.max(scores, axis=1, keepdims=True)
        top = top.astype(jnp.bfloat16).astype(jnp.float32)
        weights = jnp.exp2(scores - top)
        total = jnp.sum(weights, axis=1, keepdims=True)
        sums = jnp.dot(
            weights.astype(jnp.bfloat16), value, preferred_element_type=jnp.float32
        )
        high = total.astype(jnp.bfloat16).astype(jnp.float32)
        groups = top.shape[0] // 8

        def wide(column):
            return jnp.broadcast_to(column, (column.shape[0], HD)).reshape(groups, 8, HD)

        stats = jnp.where(
            field == 0,
            wide(top),
            jnp.where(field == 1, wide(high), wide(total - high)),
        )
        stats = jnp.sum(jnp.where(in_row & (field < 3), stats, 0.0), axis=1)
        return (sums / total).astype(jnp.bfloat16), stats

    audio_rows = query_ref[:, :, 2 * VROWS :, :].astype(jnp.float32)
    audio_rows = audio_rows.reshape(x_count * NY // 2, 2, 8, HD)
    even, odd = audio_rows[:, 0], audio_rows[:, 1]
    low = low_rows(even.shape)
    audio_self = jnp.where(low, even, swap_halves(odd)).reshape(-1, HD).astype(jnp.bfloat16)
    audio_cross = jnp.where(low, swap_halves(even), odd).reshape(-1, HD).astype(jnp.bfloat16)

    for x in range(x_count):
        own = slice(x * ATOK_DEV, (x + 1) * ATOK_DEV)
        video_self = query_ref[x, :, :VROWS, :].reshape(VTOK_DEV, HD)
        video_cross = query_ref[x, :, VROWS : 2 * VROWS, :].reshape(VTOK_DEV, HD)
        on_video, video_stats = attend(
            jnp.concatenate([video_self, audio_cross[own]], axis=0),
            video_key,
            video_value,
            video_bias_ref,
        )
        on_audio, audio_stats = attend(
            jnp.concatenate([video_cross, audio_self[own]], axis=0),
            audio_key,
            audio_value,
            audio_bias_ref,
        )
        tokens = VTOK_DEV + ATOK_DEV
        out_ref[x, :tokens, :] = on_video
        out_ref[x, tokens:OUT_ROWS, :] = on_audio
        out_ref[x, OUT_ROWS:, :] = jnp.concatenate(
            [video_stats, audio_stats], axis=0
        ).astype(jnp.bfloat16)


def combine_kernel(part_ref, gate_ref, out_ref):
    parts = part_ref.shape[0]
    lane = lax.broadcasted_iota(jnp.int32, (1, 8, HD), 2)
    row = lax.broadcasted_iota(jnp.int32, (1, 8, HD), 1)

    def stat(rows, number):
        picked = jnp.where(lane == row * 16 + number, rows, 0.0)
        return jnp.sum(picked.reshape(OUT_ROWS, HD), axis=1, keepdims=True)

    tops, totals = [], []
    for part in range(parts):
        rows = part_ref[part, OUT_ROWS:, :].astype(jnp.float32)
        rows = jnp.broadcast_to(rows[:, None, :], (STAT_ROWS, 8, HD))
        tops.append(stat(rows, 0))
        totals.append(stat(rows, 1) + stat(rows, 2))
    top = tops[0]
    for other in tops[1:]:
        top = jnp.maximum(top, other)
    shares = [jnp.exp2(t - top) * total for t, total in zip(tops, totals)]
    inverse = 1.0 / sum(shares)
    merged = sum(
        part_ref[part, :OUT_ROWS, :].astype(jnp.float32) * (shares[part] * inverse)
        for part in range(parts)
    )
    tokens = VTOK_DEV + ATOK_DEV
    video = merged[:VTOK_DEV] + gate_ref[0:1, :] * merged[tokens : tokens + VTOK_DEV]
    audio = merged[tokens + VTOK_DEV :] + gate_ref[1:2, :] * merged[VTOK_DEV:tokens]
    out_ref[:, :VROWS, :] = video.reshape(NY, VROWS, HD).astype(jnp.bfloat16)
    for pair in range(NY // 2):
        rows = audio[pair * 8 : pair * 8 + 8].astype(jnp.bfloat16)
        out_ref[2 * pair, VROWS:, :] = rows
        out_ref[2 * pair + 1, VROWS:, :] = rows


def place_kernel(place_ref, back_ref, video_ref, audio_ref):
    core = place_ref[0]
    odd = place_ref[1]
    half_groups = NY // 2
    for j in range(half_groups):
        group = core * half_groups + j
        cols = slice(j * GROUP, (j + 1) * GROUP)
        for s in range(2):
            video_ref[s * VROWS : (s + 1) * VROWS, cols] = back_ref[s, group, :VROWS, :]
        first, second = (back_ref[s, group, VROWS:, :].astype(jnp.float32) for s in range(2))
        low = low_rows(first.shape)
        audio_ref[:, cols] = jnp.where(
            odd == 0,
            jnp.where(low, first, swap_halves(second)),
            jnp.where(low, swap_halves(first), second),
        ).astype(jnp.bfloat16)


def whole(memory_space=pltpu.VMEM):
    return pl.BlockSpec(memory_space=memory_space)


def params():
    return pltpu.CompilerParams(vmem_limit_bytes=VMEM_LIMIT)


def shards(
    video_proj,
    audio_proj,
    video_gains,
    audio_gains,
    cross_gates,
    timestep,
    video_counts,
    audio_counts,
):
    core = lax.axis_index("tp")
    ring = ("yh", "aud")
    x_count = lax.axis_size("x")
    z_count = lax.axis_size("z")
    y_index = lax.axis_index(ring)
    gate_rows = lax.dynamic_index_in_dim(cross_gates, timestep[0], 1, keepdims=False)
    small = jnp.concatenate(
        [video_gains, audio_gains, gate_rows.astype(jnp.float32)], axis=0
    )
    video_all = lax.all_gather(video_proj, "tp", axis=0)
    audio_all = lax.all_gather(audio_proj, "tp", axis=0)
    small_all = lax.all_gather(small, "tp", axis=0)
    block = jax.ShapeDtypeStruct((NY, BLOCK, GROUP), jnp.bfloat16)
    queries, keyval = pl.pallas_call(
        norm_kernel,
        out_shape=(block, block),
        in_specs=[whole(pltpu.SMEM), whole(), whole(), whole()],
        out_specs=(whole(), whole()),
        compiler_params=params(),
        name="norm",
    )(core[None], video_all, audio_all, small_all)

    keyval = lax.all_to_all(keyval, ring, split_axis=0, concat_axis=0)
    keyval, queries = lax.optimization_barrier((keyval, queries))
    keyval = lax.all_gather(keyval, "z", axis=0)
    queries = lax.all_to_all(queries, ring, split_axis=0, concat_axis=0)
    queries = lax.all_gather(queries, "x", axis=0)
    keyval = lax.all_gather(keyval, "tp", axis=0)

    shape = (YH, x_count, z_count)
    x_index = lax.axis_index("x")

    aud_of = np.arange(NY) % (NY // YH)
    video_first = (
        aud_of[None, None, :, None] * (2 * VROWS)
        + np.arange(2)[:, None, None, None] * VROWS
        + np.arange(VROWS)[None, None, None, :]
    )
    audio_first = aud_of[None, :, None] * 8 + np.arange(8)[None, None, :]
    video_width = 2 * z_count * NY * VROWS
    audio_width = z_count * NY * 8
    here_v = lax.dynamic_index_in_dim(video_counts.reshape(shape), x_index, 1, keepdims=False)
    here_a = lax.dynamic_index_in_dim(audio_counts.reshape(shape), x_index, 1, keepdims=False)
    allow_v = jnp.repeat(here_v.T, NY // YH, axis=1)
    allow_a = jnp.repeat(here_a.T, NY // YH, axis=1)
    video_bias = jnp.where(video_first < allow_v[None, :, :, None], 0.0, MASKED)
    audio_bias = jnp.where(audio_first < allow_a[:, :, None], 0.0, MASKED)
    video_bias = video_bias.astype(jnp.float32).reshape(1, video_width)
    audio_bias = audio_bias.astype(jnp.float32).reshape(1, audio_width)

    partial = pl.pallas_call(
        attend_kernel,
        grid=(HEADS_HERE,),
        out_shape=jax.ShapeDtypeStruct(
            (x_count, OUT_ROWS + STAT_ROWS, GROUP), jnp.bfloat16
        ),
        in_specs=[
            pl.BlockSpec((x_count, NY, BLOCK, HD), lambda h: (0, 0, 0, h)),
            pl.BlockSpec((2, z_count, NY, BLOCK, HD), lambda h: (0, 0, 0, 0, h)),
            pl.BlockSpec((1, video_width), lambda h: (0, 0)),
            pl.BlockSpec((1, audio_width), lambda h: (0, 0)),
        ],
        out_specs=pl.BlockSpec((x_count, OUT_ROWS + STAT_ROWS, HD), lambda h: (0, 0, h)),
        compiler_params=params(),
        name="attend",
    )(queries, keyval, video_bias, audio_bias)

    partial = lax.all_to_all(partial, "x", split_axis=0, concat_axis=0)
    gates = lax.dynamic_slice(
        small_all,
        (y_index // (NY // 2), 6, (y_index % (NY // 2)) * GROUP),
        (1, 2, GROUP),
    )[0]
    back = pl.pallas_call(
        combine_kernel,
        grid=(HEADS_HERE,),
        out_shape=jax.ShapeDtypeStruct((NY, BACK_ROWS, GROUP), jnp.bfloat16),
        in_specs=[
            pl.BlockSpec((x_count, OUT_ROWS + STAT_ROWS, HD), lambda h: (0, 0, h)),
            pl.BlockSpec((2, HD), lambda h: (0, h)),
        ],
        out_specs=pl.BlockSpec((NY, BACK_ROWS, HD), lambda h: (0, 0, h)),
        compiler_params=params(),
        name="combine",
    )(partial, gates)
    back = lax.all_to_all(back, ring, split_axis=0, concat_axis=0)
    back = lax.all_gather(back, "tp", axis=0)
    return pl.pallas_call(
        place_kernel,
        out_shape=(
            jax.ShapeDtypeStruct((2 * VROWS, D // 2), jnp.bfloat16),
            jax.ShapeDtypeStruct((2 * AROWS, D // 2), jnp.bfloat16),
        ),
        in_specs=[whole(pltpu.SMEM), whole()],
        out_specs=(whole(), whole()),
        compiler_params=params(),
        name="place",
    )(jnp.stack([core, y_index % 2]), back)


def solution(mesh):
    vid = mesh.devices.shape[0]
    cut = (YH, vid // (YH * NZ), NZ)
    fine = Mesh(
        mesh.devices.reshape(cut + mesh.devices.shape[1:]), ("yh", "x", "z", "aud", "tp")
    )
    tokens = ("yh", "x", "z", "aud")
    in_specs = (
        P(None, tokens, "tp"),
        P(None, tokens, "tp"),
        P(None, "tp"),
        P(None, "tp"),
        P(None, None, "tp"),
        P(),
        P(),
        P(),
    )
    out_specs = (P(tokens, "tp"), P(tokens, "tp"))
    return jax.shard_map(
        shards, mesh=fine, in_specs=in_specs, out_specs=out_specs, check_vma=False
    )
```

time: 741 us -> 168 us (0.23); the launches traced: 732 us -> 168 us
  waiting for transfers between devices: 539 us -> 64.6 us
  local copies, waits for them, and re-layouts: 82.3 us -> 2.72 us
  matrix products: 32.2 us -> 0 us
  other arithmetic: 25.1 us -> 1.7 us
  blocking collectives: 29.4 us -> 50.5 us
  Pallas kernels: 0 us -> 17.9 us
  starting transfers between devices: 8.05 us -> 15.5 us
    all_gather x4 -> x2, waiting for transfers between devices: 531 us -> 37.9 us  [the longest x1 37.9 us: shards(): keyval = lax.all_gather(keyval, 'z', axis=0)]
    reshape x4 -> x2, local copies, waits for them, and re-layouts: 41.1 us -> 0.17 us  [the longest x1 0.08 us: shards(): video_counts.reshape(shape)]
    all_gather x0 -> x5, blocking collectives: none -> 35.5 us  [the longest x1 12 us: shards(): queries = lax.all_gather(queries, 'x', axis=0)]
    dot_general x21 -> x0, matrix products: 32.2 us -> none  [the longest x10 16.6 us: one_block(): jnp.einsum('qhd,khd->hqk', queries, key_block, preferred_element_type=jnp...]
    unnamed x23 -> x10, local copies, waits for them, and re-layouts: 24.7 us -> 2.13 us
    all_to_all x2 -> x3, waiting for transfers between devices: 8.21 us -> 26.7 us  [the longest x1 9.9 us: shards(): partial = lax.all_to_all(partial, 'x', split_axis=0, concat_axis=0)]
    pallas_call x0 -> x4, Pallas kernels: none -> 17.9 us  [the longest x1 12.7 us: shards(): pl.pallas_call(attend_kernel, grid=(HEADS_HERE,), out_shape=jax.ShapeDtyp...]
    psum x1 -> x0, blocking collectives: 9 us -> none  [shards(): lax.psum((square_sums(video_proj), square_sums(audio_proj)), 'tp')]
  transfers between devices with their start and end apart: 6 -> 5, of which waited for: 6 -> 4; matrix products, arithmetic and copies ran while one was open for 7% -> 0% of each run, Pallas kernels for 0% -> 0%
where the time goes in v1:
time: 168 us
  waiting for transfers between devices  64.6 us (38%)
  blocking collectives  50.5 us (30%)
  Pallas kernels  17.9 us (11%)
  starting transfers between devices  15.5 us (9%)
  between operations  14.8 us (9%)
  local copies, waits for them, and re-layouts  2.72 us (2%)
  other arithmetic  1.7 us (1%)
    all_gather x1, waiting for transfers between devices, shards(): keyval = lax.all_gather(keyval, 'z', axis=0)  37.9 us
    all_to_all x1, blocking collectives, shards(): keyval = lax.all_to_all(keyval, ring, split_axis=0, concat_axis=0)  15 us
    pallas_call x1, Pallas kernels, shards(): pl.pallas_call(attend_kernel, grid=(HEADS_HERE,), out_shape=jax.ShapeDtyp...  12.7 us
    all_gather x1, blocking collectives, shards(): queries = lax.all_gather(queries, 'x', axis=0)  12 us
    all_gather x1, blocking collectives, shards(): back = lax.all_gather(back, 'tp', axis=0)  10.4 us
    all_to_all x1, waiting for transfers between devices, shards(): partial = lax.all_to_all(partial, 'x', split_axis=0, concat_axis=0)  9.9 us
    all_to_all x1, waiting for transfers between devices, shards(): queries = lax.all_to_all(queries, ring, split_axis=0, concat_axis=0)  8.8 us
    all_gather x1, blocking collectives, shards(): small_all = lax.all_gather(small, 'tp', axis=0)  8.41 us
  transfers between devices with their start and end apart: 5, of which 4 were waited for; matrix products, arithmetic and copies ran while one was open for 0% of the time, Pallas kernels for 0%

profile of v1, /device:TPU:1, one launch (start us, length us, event | category | flops | bytes accessed | tf_op | source)
XLA Modules:
  0.0 167.7 jit_solution(3528970151461639271)
XLA Ops:
  7.2 0.0 all-gather.10.cloned.1.call-start
  7.9 0.7 bitcast_convert_fusion
  8.6 0.8 pad_maximum_fusion
  9.3 8.4 %all-gather.2 = f32[16,1536]{1,0:T(8,128)S(1)} all-gather(f32[8,1536]{1,0:T(8,128)S(1)} %pad_maximum_fusion), channel_id=4, replica_groups=mesh['yh'=2,'x'=4,'z'=8,'aud'=4,'tp'=2] {'tp'}, dimensions={0}, use_global_device_ids=true | all-gather | bytes 147456 | tf_op jit(solution)/shard_map/all_gather | solution.py:252
  17.7 2.1 %all-gather.1 = bf16[8,8,1536]{2,1,0:T(8,128)(2,1)S(1)} all-gather(bf16[4,8,1536]{2,1,0:T(8,128)(2,1)} %param.11), channel_id=3, replica_groups=mesh['yh'=2,'x'=4,'z'=8,'aud'=4,'tp'=2] {'tp'}, dimensions={0}, use_global_device_ids=true | all-gather | bytes 294912 | tf_op jit(solution)/shard_map/all_gather | solution.py:251
  19.9 2.6 %all-gather = bf16[8,32,1536]{2,1,0:T(8,128)(2,1)S(1)} all-gather(bf16[4,32,1536]{2,1,0:T(8,128)(2,1)} %param.10), channel_id=2, replica_groups=mesh['yh'=2,'x'=4,'z'=8,'aud'=4,'tp'=2] {'tp'}, dimensions={0}, use_global_device_ids=true | all-gather | bytes 1179648 | tf_op jit(solution)/shard_map/all_gather | solution.py:250
  22.5 0.9 norm.1
  23.4 15.0 %all_to_all.20 = bf16[8,40,384]{2,1,0:T(8,128)(2,1)} all-to-all(bf16[8,40,384]{2,1,0:T(8,128)(2,1)S(1)} %get-tuple-element.6), channel_id=1, replica_groups=mesh['yh'=2,'x'=4,'z'=8,'aud'=4,'tp'=2] {'yh','aud'}, dimensions={0} | all-to-all | bytes 491520 | tf_op jit(solution)/shard_map/all_to_all | solution.py:263
  38.5 0.0 all-gather.12.cloned.1.call-start
  38.5 37.9 %all-gather.10.cloned.1.call-done = bf16[64,40,384]{2,1,0:T(8,128)(2,1)} async-done(((bf16[8,40,384]{2,1,0:T(8,128)(2,1)}), bf16[64,40,384]{2,1,0:T(8,128)(2,1)}) %all-gather.10.cloned.1.call-update) | async-done | bytes 1966096 | tf_op jit(solution)/shard_map/all_gather | solution.py:265
  76.4 0.1 reshape.72
  76.5 0.1 reshape.73
  76.6 0.1 copy.14
  76.7 0.1 copy.15
  76.8 6.5 %all-to-all-start.1 = ((bf16[8,40,384]{2,1,0:T(8,128)(2,1)}), bf16[8,40,384]{2,1,0:T(8,128)(2,1)S(1)}, u32[]{:S(2)}, u32[]{:S(2)}) async-start(bf16[8,40,384]{2,1,0:T(8,128)(2,1)} %get-tuple-element.8), calls=%async_computation.1 | async-start | bytes 491520 | tf_op jit(solution)/shard_map/all_to_all | solution.py:266
  83.2 0.1 compare_select_fusion.1
  83.3 0.1 select_n.64.audio_bias_ref
  83.4 0.1 compare_select_fusion
  83.5 0.1 select_n.62.video_bias_ref
  83.6 8.8 %all-to-all-done.1 = bf16[8,40,384]{2,1,0:T(8,128)(2,1)S(1)} async-done(((bf16[8,40,384]{2,1,0:T(8,128)(2,1)}), bf16[8,40,384]{2,1,0:T(8,128)(2,1)S(1)}, u32[]{:S(2)}, u32[]{:S(2)}) %all-to-all-start.1) | async-done | bytes 245792 | tf_op jit(solution)/shard_map/all_to_all | solution.py:266
  92.4 12.0 %all-gather.3 = bf16[32,40,384]{2,1,0:T(8,128)(2,1)S(1)} all-gather(bf16[8,40,384]{2,1,0:T(8,128)(2,1)S(1)} %all-to-all-done.1), channel_id=5, replica_groups=mesh['yh'=2,'x'=4,'z'=8,'aud'=4,'tp'=2] {'x'}, dimensions={0}, use_global_device_ids=true | all-gather | bytes 1228800 | tf_op jit(solution)/shard_map/all_gather | solution.py:267
  104.4 2.1 %copy-done = bf16[16,8,40,384]{3,2,1,0:T(8,128)(2,1)S(1)} copy-done((bf16[16,8,40,384]{3,2,1,0:T(8,128)(2,1)S(1)}, bf16[16,8,40,384]{3,2,1,0:T(8,128)(2,1)}, u32[]{:S(2)}) %copy-start) | copy-done | bytes 3932184
  106.5 12.7 %attend.1 = bf16[4,360,384]{2,1,0:T(8,128)(2,1)} custom-call(bf16[4,8,40,384]{3,2,1,0:T(8,128)(2,1)S(1)} %bitcast.29, bf16[2,8,8,40,384]{4,3,2,1,0:T(8,128)(2,1)S(1)} %bitcast.28, f32[1,2048]{1,0:T(1,128)S(1)} %select_n.62.video_bias_ref, f32[1,512]{1,0:T(1,128)S(1)} %select_n.64.audio_bias_ref), custom_call_target="tpu_custom_call" | custom-call | tf_op jit(solution)/shard_map/attend/pallas_call | solution.py:291
  119.3 3.5 %all-to-all-start.2 = ((bf16[4,360,384]{2,1,0:T(8,128)(2,1)}), bf16[4,360,384]{2,1,0:T(8,128)(2,1)S(1)}, u32[]{:S(2)}, u32[]{:S(2)}) async-start(bf16[4,360,384]{2,1,0:T(8,128)(2,1)} %attend.1), calls=%async_computation.2 | async-start | bytes 2211840 | tf_op jit(solution)/shard_map/all_to_all | solution.py:308
  122.8 0.1 dynamic-slice_bitcast_fusion.gate_ref
  122.9 9.9 %all-to-all-done.2.part_ref = bf16[4,360,384]{2,1,0:T(8,128)(2,1)S(1)} async-done(((bf16[4,360,384]{2,1,0:T(8,128)(2,1)}), bf16[4,360,384]{2,1,0:T(8,128)(2,1)S(1)}, u32[]{:S(2)}, u32[]{:S(2)}) %all-to-all-start.2) | async-done | bytes 1105952 | tf_op jit(solution)/shard_map/all_to_all | solution.py:308
  132.8 3.0 %combine.1 = bf16[8,24,384]{2,1,0:T(8,128)(2,1)} custom-call(bf16[4,360,384]{2,1,0:T(8,128)(2,1)S(1)} %all-to-all-done.2.part_ref, f32[2,384]{1,0:T(2,128)S(1)} %dynamic-slice_bitcast_fusion.gate_ref), custom_call_target="tpu_custom_call" | custom-call | tf_op jit(solution)/shard_map/combine/pallas_call | solution.py:314
  135.8 5.4 %all-to-all-start.3 = ((bf16[8,24,384]{2,1,0:T(8,128)(2,1)}), bf16[8,24,384]{2,1,0:T(8,128)(2,1)S(1)}, u32[]{:S(2)}, u32[]{:S(2)}) async-start(bf16[8,24,384]{2,1,0:T(8,128)(2,1)} %combine.1), calls=%async_computation.3 | async-start | bytes 294912 | tf_op jit(solution)/shard_map/all_to_all | solution.py:326
  141.2 0.1 pad_add_fusion.place_ref
  141.3 8.0 %all-to-all-done.3 = bf16[8,24,384]{2,1,0:T(8,128)(2,1)S(1)} async-done(((bf16[8,24,384]{2,1,0:T(8,128)(2,1)}), bf16[8,24,384]{2,1,0:T(8,128)(2,1)S(1)}, u32[]{:S(2)}, u32[]{:S(2)}) %all-to-all-start.3) | async-done | bytes 147488 | tf_op jit(solution)/shard_map/all_to_all | solution.py:326
  149.3 10.4 %all-gather.6 = bf16[16,24,384]{2,1,0:T(8,128)(2,1)S(1)} all-gather(bf16[8,24,384]{2,1,0:T(8,128)(2,1)S(1)} %all-to-all-done.3), channel_id=8, replica_groups=mesh['yh'=2,'x'=4,'z'=8,'aud'=4,'tp'=2] {'tp'}, dimensions={0}, use_global_device_ids=true | all-gather | bytes 442368 | tf_op jit(solution)/shard_map/all_gather | solution.py:327
  159.7 1.2 place.1
  (15 shorter events, 0.1 us)
Async XLA Ops:
  7.2 69.2 %all-gather.10.cloned.1.call-start = ((), (), s32[]{:S(2)}) async-start(), calls=%async_computation.4 | async-start | bytes 2211840 | tf_op jit(solution)/shard_map/all_gather | solution.py:265
  22.5 54.0 %copy-start.3 = (s32[64]{0:T(128)S(1)}, s32[64]{0:T(128)}, u32[]{:S(2)}) copy-start(s32[64]{0:T(128)} %param.16) | copy-start | bytes 772
  22.5 54.1 %copy-start.4 = (s32[64]{0:T(128)S(1)}, s32[64]{0:T(128)}, u32[]{:S(2)}) copy-start(s32[64]{0:T(128)} %param.17) | copy-start | bytes 772
  22.5 60.8 %copy-start.2 = (s32[8,8]{1,0:T(8,128)S(1)}, s32[8,8]{1,0:T(8,128)}, u32[]{:S(2)}) copy-start(s32[8,8]{1,0:T(8,128)} %constant.81) | copy-start | bytes 772
  22.5 60.9 %copy-start.1 = (s32[2,8,16]{2,1,0:T(8,128)S(1)}, s32[2,8,16]{2,1,0:T(8,128)}, u32[]{:S(2)}) copy-start(s32[2,8,16]{2,1,0:T(8,128)} %constant.80) | copy-start | bytes 3076
  38.5 65.9 %all-gather.12.cloned.1.call-start = ((), (), s32[]{:S(2)}) async-start(), calls=%async_computation.5 | async-start | bytes 5898240 | tf_op jit(solution)/shard_map/all_gather | solution.py:268
  76.8 15.6 %all-to-all-start.1 = ((bf16[8,40,384]{2,1,0:T(8,128)(2,1)}), bf16[8,40,384]{2,1,0:T(8,128)(2,1)S(1)}, u32[]{:S(2)}, u32[]{:S(2)}) async-start(bf16[8,40,384]{2,1,0:T(8,128)(2,1)} %get-tuple-element.8), calls=%async_computation.1 | async-start | bytes 491520 | tf_op jit(solution)/shard_map/all_to_all | solution.py:266
  104.4 2.1 %copy-start = (bf16[16,8,40,384]{3,2,1,0:T(8,128)(2,1)S(1)}, bf16[16,8,40,384]{3,2,1,0:T(8,128)(2,1)}, u32[]{:S(2)}) copy-start(bf16[16,8,40,384]{3,2,1,0:T(8,128)(2,1)} %all-gather.12.cloned.1.call-done) | copy-start | bytes 11796484
  119.3 13.5 %all-to-all-start.2 = ((bf16[4,360,384]{2,1,0:T(8,128)(2,1)}), bf16[4,360,384]{2,1,0:T(8,128)(2,1)S(1)}, u32[]{:S(2)}, u32[]{:S(2)}) async-start(bf16[4,360,384]{2,1,0:T(8,128)(2,1)} %attend.1), calls=%async_computation.2 | async-start | bytes 2211840 | tf_op jit(solution)/shard_map/all_to_all | solution.py:308
  135.8 13.5 %all-to-all-start.3 = ((bf16[8,24,384]{2,1,0:T(8,128)(2,1)}), bf16[8,24,384]{2,1,0:T(8,128)(2,1)S(1)}, u32[]{:S(2)}, u32[]{:S(2)}) async-start(bf16[8,24,384]{2,1,0:T(8,128)(2,1)} %combine.1), calls=%async_computation.3 | async-start | bytes 294912 | tf_op jit(solution)/shard_map/all_to_all | solution.py:326
Sparse Core Ops, SparseCore 0:
  38.6 37.7 all-gather.9
  78.5 24.9 all-gather.11

commit v2 on v1

v2 whole, which is shorter than its diff:
```python
import math

import jax
import jax.numpy as jnp
import numpy as np
from jax import lax
from jax.experimental import pallas as pl
from jax.experimental.pallas import tpu as pltpu
from jax.sharding import Mesh
from jax.sharding import PartitionSpec as P

D = 3072
HD = 128
VTOK_DEV = 128
ATOK_DEV = 32
EPSILON = 1e-06
MASKED = -1e30

YH = 2
NY = 8
NZ = 8
GROUP = D // NY
HEADS_HERE = GROUP // HD
VROWS = 16
AROWS = 4
BLOCK = 2 * VROWS + 2 * AROWS
OUT_ROWS = 2 * (VTOK_DEV + ATOK_DEV)
STAT_ROWS = OUT_ROWS // 8
BACK_ROWS = VROWS + 8
AUDIO_ROW = 4 * VROWS
SMALL_ROW = AUDIO_ROW + 4 * 2 * AROWS
PACK_ROWS = SMALL_ROW + 32
KEY_STEP = 256
SCORE_SCALE = HD ** (-0.5) * math.log2(math.e)
VMEM_LIMIT = 48 * 1024 * 1024
ATTEND_VMEM = 60 * 1024 * 1024


def low_rows(shape):
    return lax.broadcasted_iota(jnp.int32, shape, len(shape) - 2) % 8 < 4


def swap_halves(rows):
    return pltpu.roll(rows, 4, axis=rows.ndim - 2)


def pack_kernel(core_ref, video_ref, audio_ref, video_gains_ref, audio_gains_ref, out_ref):
    first = pl.multiple_of((1 - core_ref[0]) * VROWS, VROWS)
    for array in range(4):
        row = array * VROWS
        out_ref[row : row + VROWS, :] = video_ref[array, pl.ds(first, VROWS), :]
        row = AUDIO_ROW + array * 8
        out_ref[row : row + 8, :] = audio_ref[array]
    gains = [video_gains_ref[...], audio_gains_ref[...]]
    rest = jnp.concatenate(gains + [jnp.zeros_like(gains[0][:2])], axis=0)
    pieces = []
    for _ in range(3):
        piece = rest.astype(jnp.bfloat16).astype(jnp.float32)
        pieces.append(piece)
        rest = rest - piece
    pieces.append(jnp.zeros_like(rest))
    out_ref[SMALL_ROW:, :] = jnp.concatenate(pieces, axis=0).astype(jnp.bfloat16)


def norm_kernel(
    core_ref,
    video_ref,
    audio_ref,
    video_gains_ref,
    audio_gains_ref,
    packed_ref,
    query_ref,
    keyval_ref,
):
    core = core_ref[0]
    at_zero = core == 0
    own_first = pl.multiple_of(core * VROWS, VROWS)
    small = packed_ref[1 - core, SMALL_ROW:, :].astype(jnp.float32)
    other_gains = small[0:8] + small[8:16] + small[16:24]
    own_gains = jnp.concatenate([video_gains_ref[...], audio_gains_ref[...]], axis=0)

    def ordered(own, other):
        return [jnp.where(at_zero, own, other), jnp.where(at_zero, other, own)]

    gains = ordered(own_gains, other_gains[:6])
    half_groups = NY // 2

    def normed(halves, gain_row, extra):
        total = sum(jnp.sum(v * v, axis=1, keepdims=True) for v in halves)
        inverse = lax.rsqrt(total / D + EPSILON)
        return [
            v * inverse * (gains[s][gain_row : gain_row + 1, :] * extra)
            for s, v in enumerate(halves)
        ]

    def spread(out_ref, row, halves):
        count = halves[0].shape[0]
        for group in range(NY):
            col = (group % half_groups) * GROUP
            out_ref[group, row : row + count, :] = halves[group // half_groups][
                :, col : col + GROUP
            ].astype(jnp.bfloat16)

    def video(array):
        first = array * VROWS
        return ordered(
            video_ref[array, pl.ds(own_first, VROWS), :].astype(jnp.float32),
            packed_ref[1 - core, first : first + VROWS, :].astype(jnp.float32),
        )

    def audio(array):
        first = AUDIO_ROW + array * 8
        return ordered(
            audio_ref[array].astype(jnp.float32),
            packed_ref[1 - core, first : first + 8, :].astype(jnp.float32),
        )

    spread(keyval_ref, 0, normed(video(2), 2, 1.0))
    spread(keyval_ref, VROWS, video(3))
    audio_key = normed(audio(2), 5, 1.0)
    audio_value = audio(3)
    spread(
        keyval_ref,
        2 * VROWS,
        [jnp.where(at_zero, k, v) for k, v in zip(audio_key, audio_value)],
    )
    spread(query_ref, 0, normed(video(0), 0, SCORE_SCALE))
    spread(query_ref, VROWS, normed(video(1), 1, SCORE_SCALE))
    audio_self = normed(audio(0), 3, SCORE_SCALE)
    audio_cross = normed(audio(1), 4, SCORE_SCALE)
    mixed = []
    for own, other in zip(audio_self, audio_cross):
        low = low_rows(own.shape)
        mixed.append(
            jnp.where(
                at_zero,
                jnp.where(low, own, swap_halves(other)),
                jnp.where(low, swap_halves(own), other),
            )
        )
    spread(query_ref, 2 * VROWS, mixed)


def attend_kernel(query_ref, keyval_ref, video_bias_ref, audio_bias_ref, out_ref):
    x_count = query_ref.shape[0]
    z_count = keyval_ref.shape[0]
    video_keys = z_count * 2 * NY * VROWS
    audio_keys = z_count * NY * 8
    video_key = keyval_ref[:, :, :, :VROWS, :].reshape(video_keys, HD)
    video_value = keyval_ref[:, :, :, VROWS : 2 * VROWS, :].reshape(video_keys, HD)

    def audio_part(which):
        rows = keyval_ref[:, which, :, 2 * VROWS :, :].astype(jnp.float32)
        return rows.reshape(audio_keys, HD).astype(jnp.bfloat16)

    audio_key, audio_value = audio_part(0), audio_part(1)
    lane = lax.broadcasted_iota(jnp.int32, (1, 8, HD), 2)
    row = lax.broadcasted_iota(jnp.int32, (1, 8, HD), 1)
    in_row = lane // 16 == row
    field = lane % 16

    def attend(queries, key, value, bias_ref):
        top = None
        for first in range(0, key.shape[0], KEY_STEP):
            keys = slice(first, first + KEY_STEP)
            scores = lax.dot_general(
                queries,
                key[keys],
                (((1,), (1,)), ((), ())),
                preferred_element_type=jnp.float32,
            )
            scores = scores + bias_ref[0:1, keys]
            here = jnp.max(scores, axis=1, keepdims=True)
            here = here.astype(jnp.bfloat16).astype(jnp.float32)
            new_top = here if top is None else jnp.maximum(top, here)
            weights = jnp.exp2(scores - new_top)
            new_total = jnp.sum(weights, axis=1, keepdims=True)
            new_sums = jnp.dot(
                weights.astype(jnp.bfloat16), value[keys], preferred_element_type=jnp.float32
            )
            if top is not None:
                keep = jnp.exp2(top - new_top)
                new_total = new_total + total * keep
                new_sums = new_sums + sums * keep
            top, total, sums = new_top, new_total, new_sums
        high = total.astype(jnp.bfloat16).astype(jnp.float32)
        groups = top.shape[0] // 8

        def wide(column):
            return jnp.broadcast_to(column, (column.shape[0], HD)).reshape(groups, 8, HD)

        stats = jnp.where(
            field == 0,
            wide(top),
            jnp.where(field == 1, wide(high), wide(total - high)),
        )
        stats = jnp.sum(jnp.where(in_row & (field < 3), stats, 0.0), axis=1)
        return (sums / total).astype(jnp.bfloat16), stats

    audio_rows = query_ref[:, :, 2 * VROWS :, :].astype(jnp.float32)
    audio_rows = audio_rows.reshape(x_count * NY // 2, 2, 8, HD)
    even, odd = audio_rows[:, 0], audio_rows[:, 1]
    low = low_rows(even.shape)
    audio_self = jnp.where(low, even, swap_halves(odd)).reshape(-1, HD).astype(jnp.bfloat16)
    audio_cross = jnp.where(low, swap_halves(even), odd).reshape(-1, HD).astype(jnp.bfloat16)
    video_self = query_ref[:, :, :VROWS, :].reshape(x_count * VTOK_DEV, HD)
    video_cross = query_ref[:, :, VROWS : 2 * VROWS, :].reshape(x_count * VTOK_DEV, HD)
    stats = []
    for kind, (video, audio, key, value, bias_ref) in enumerate(
        (
            (video_self, audio_cross, video_key, video_value, video_bias_ref),
            (video_cross, audio_self, audio_key, audio_value, audio_bias_ref),
        )
    ):
        rows, stat = attend(jnp.concatenate([video, audio], axis=0), key, value, bias_ref)
        stats.append(stat)
        start = kind * (VTOK_DEV + ATOK_DEV)
        for x in range(x_count):
            first = x * VTOK_DEV
            out_ref[x, start : start + VTOK_DEV, :] = rows[first : first + VTOK_DEV]
            first = x_count * VTOK_DEV + x * ATOK_DEV
            out_ref[x, start + VTOK_DEV : start + VTOK_DEV + ATOK_DEV, :] = rows[
                first : first + ATOK_DEV
            ]
    wide_stat, narrow_stat = VTOK_DEV // 8, ATOK_DEV // 8
    for x in range(x_count):
        picked = []
        for stat in stats:
            first = x * wide_stat
            picked.append(stat[first : first + wide_stat])
            first = x_count * wide_stat + x * narrow_stat
            picked.append(stat[first : first + narrow_stat])
        out_ref[x, OUT_ROWS:, :] = jnp.concatenate(picked, axis=0).astype(jnp.bfloat16)


def combine_kernel(part_ref, gate_ref, out_ref):
    parts = part_ref.shape[0]
    lane = lax.broadcasted_iota(jnp.int32, (1, 8, HD), 2)
    row = lax.broadcasted_iota(jnp.int32, (1, 8, HD), 1)
    in_row = lane // 16 == row
    source = lax.broadcasted_iota(jnp.int32, (HD, 2 * HD), 0) % 16
    target = lax.broadcasted_iota(jnp.int32, (HD, 2 * HD), 1) // HD
    source = jnp.where(source < 3, (source + 1) // 2, 2)
    pick = jnp.where(source == target, 1.0, 0.0).astype(jnp.bfloat16)
    tokens = VTOK_DEV + ATOK_DEV
    for head in range(HEADS_HERE):
        cols = slice(head * HD, (head + 1) * HD)
        tops, totals = [], []
        for part in range(parts):
            rows = part_ref[part, OUT_ROWS:, cols].astype(jnp.float32)
            rows = jnp.broadcast_to(rows[:, None, :], (STAT_ROWS, 8, HD))
            rows = jnp.where(in_row, rows, 0.0).reshape(OUT_ROWS, HD)
            fields = jnp.dot(
                rows.astype(jnp.bfloat16), pick, preferred_element_type=jnp.float32
            )
            tops.append(fields[:, :HD])
            totals.append(fields[:, HD:])
        top = tops[0]
        for other in tops[1:]:
            top = jnp.maximum(top, other)
        shares = [jnp.exp2(t - top) * total for t, total in zip(tops, totals)]
        inverse = 1.0 / sum(shares)
        merged = sum(
            part_ref[part, :OUT_ROWS, cols].astype(jnp.float32) * (shares[part] * inverse)
            for part in range(parts)
        )
        video = merged[:VTOK_DEV] + gate_ref[0:1, cols] * merged[tokens : tokens + VTOK_DEV]
        audio = merged[tokens + VTOK_DEV :] + gate_ref[1:2, cols] * merged[VTOK_DEV:tokens]
        out_ref[:, :VROWS, cols] = video.reshape(NY, VROWS, HD).astype(jnp.bfloat16)
        for pair in range(NY // 2):
            rows = audio[pair * 8 : pair * 8 + 8].astype(jnp.bfloat16)
            out_ref[2 * pair, VROWS:, cols] = rows
            out_ref[2 * pair + 1, VROWS:, cols] = rows


def place_kernel(place_ref, back_ref, video_ref, audio_ref):
    core = place_ref[0]
    odd = place_ref[1]
    half_groups = NY // 2
    for j in range(half_groups):
        group = core * half_groups + j
        cols = slice(j * GROUP, (j + 1) * GROUP)
        for s in range(2):
            video_ref[s * VROWS : (s + 1) * VROWS, cols] = back_ref[s, group, :VROWS, :]
        first, second = (back_ref[s, group, VROWS:, :].astype(jnp.float32) for s in range(2))
        low = low_rows(first.shape)
        audio_ref[:, cols] = jnp.where(
            odd == 0,
            jnp.where(low, first, swap_halves(second)),
            jnp.where(low, swap_halves(first), second),
        ).astype(jnp.bfloat16)


def whole(memory_space=pltpu.VMEM):
    return pl.BlockSpec(memory_space=memory_space)


def params():
    return pltpu.CompilerParams(vmem_limit_bytes=VMEM_LIMIT)


def shards(
    video_proj,
    audio_proj,
    video_gains,
    audio_gains,
    cross_gates,
    timestep,
    video_counts,
    audio_counts,
):
    core = lax.axis_index("tp")
    ring = ("yh", "aud")
    x_count = lax.axis_size("x")
    z_count = lax.axis_size("z")
    y_index = lax.axis_index(ring)
    packed = pl.pallas_call(
        pack_kernel,
        grid=(1,),
        out_shape=jax.ShapeDtypeStruct((PACK_ROWS, D // 2), jnp.bfloat16),
        in_specs=[
            whole(pltpu.SMEM),
            pl.BlockSpec(video_proj.shape, lambda i: (0, 0, 0)),
            pl.BlockSpec(audio_proj.shape, lambda i: (0, 0, 0)),
            pl.BlockSpec(video_gains.shape, lambda i: (0, 0)),
            pl.BlockSpec(audio_gains.shape, lambda i: (0, 0)),
        ],
        out_specs=pl.BlockSpec((PACK_ROWS, D // 2), lambda i: (0, 0)),
        compiler_params=pltpu.CompilerParams(vmem_limit_bytes=ATTEND_VMEM),
        name="pack",
    )(core[None], video_proj, audio_proj, video_gains, audio_gains)
    packed = lax.all_gather(packed, "tp", axis=0)
    block = jax.ShapeDtypeStruct((NY, BLOCK, GROUP), jnp.bfloat16)
    queries, keyval = pl.pallas_call(
        norm_kernel,
        out_shape=(block, block),
        in_specs=[whole(pltpu.SMEM)] + [whole()] * 5,
        out_specs=(whole(), whole()),
        compiler_params=params(),
        name="norm",
    )(core[None], video_proj, audio_proj, video_gains, audio_gains, packed)

    keyval = lax.all_to_all(keyval, ring, split_axis=0, concat_axis=0)
    keyval, queries = lax.optimization_barrier((keyval, queries))
    keyval = lax.all_gather(keyval, ("z", "tp"), axis=0)
    keyval = keyval.reshape(z_count, 2, NY, BLOCK, GROUP)
    queries = lax.all_to_all(queries, ring, split_axis=0, concat_axis=0)
    queries = lax.all_gather(queries, "x", axis=0)

    shape = (YH, x_count, z_count)
    x_index = lax.axis_index("x")

    aud_of = np.arange(NY) % (NY // YH)
    video_first = (
        aud_of[None, None, :, None] * (2 * VROWS)
        + np.arange(2)[None, :, None, None] * VROWS
        + np.arange(VROWS)[None, None, None, :]
    )
    audio_first = aud_of[None, :, None] * 8 + np.arange(8)[None, None, :]
    video_width = z_count * 2 * NY * VROWS
    audio_width = z_count * NY * 8

    def allowed(counts):
        here = lax.dynamic_index_in_dim(counts.reshape(shape), x_index, 1, keepdims=False)
        return jnp.repeat(here.T, NY // YH, axis=1)

    video_bias = jnp.where(
        video_first < allowed(video_counts)[:, None, :, None], 0.0, MASKED
    )
    audio_bias = jnp.where(audio_first < allowed(audio_counts)[:, :, None], 0.0, MASKED)
    video_bias = video_bias.astype(jnp.float32).reshape(1, video_width)
    audio_bias = audio_bias.astype(jnp.float32).reshape(1, audio_width)
    queries, video_bias, audio_bias, step = lax.optimization_barrier(
        (queries, video_bias, audio_bias, timestep)
    )
    gates = lax.dynamic_index_in_dim(cross_gates, step[0], 1, keepdims=False)
    gates = lax.all_gather(gates, "tp", axis=0)
    gates = lax.dynamic_slice(
        gates,
        (y_index // (NY // 2), 0, (y_index % (NY // 2)) * GROUP),
        (1, 2, GROUP),
    )[0].astype(jnp.float32)
    queries, gates = lax.optimization_barrier((queries, gates))

    partial = pl.pallas_call(
        attend_kernel,
        grid=(HEADS_HERE,),
        out_shape=jax.ShapeDtypeStruct(
            (x_count, OUT_ROWS + STAT_ROWS, GROUP), jnp.bfloat16
        ),
        in_specs=[
            pl.BlockSpec((x_count, NY, BLOCK, HD), lambda h: (0, 0, 0, h)),
            pl.BlockSpec((z_count, 2, NY, BLOCK, HD), lambda h: (0, 0, 0, 0, h)),
            pl.BlockSpec((1, video_width), lambda h: (0, 0)),
            pl.BlockSpec((1, audio_width), lambda h: (0, 0)),
        ],
        out_specs=pl.BlockSpec((x_count, OUT_ROWS + STAT_ROWS, HD), lambda h: (0, 0, h)),
        compiler_params=pltpu.CompilerParams(vmem_limit_bytes=ATTEND_VMEM),
        name="attend",
    )(queries, keyval, video_bias, audio_bias)

    partial = lax.all_to_all(partial, "x", split_axis=0, concat_axis=0)
    back = pl.pallas_call(
        combine_kernel,
        out_shape=jax.ShapeDtypeStruct((NY, BACK_ROWS, GROUP), jnp.bfloat16),
        in_specs=[whole(), whole()],
        out_specs=whole(),
        compiler_params=params(),
        name="combine",
    )(partial, gates)
    back = lax.all_to_all(back, ring, split_axis=0, concat_axis=0)
    back = lax.all_gather(back, "tp", axis=0)
    return pl.pallas_call(
        place_kernel,
        out_shape=(
            jax.ShapeDtypeStruct((2 * VROWS, D // 2), jnp.bfloat16),
            jax.ShapeDtypeStruct((2 * AROWS, D // 2), jnp.bfloat16),
        ),
        in_specs=[whole(pltpu.SMEM), whole()],
        out_specs=(whole(), whole()),
        compiler_params=params(),
        name="place",
    )(jnp.stack([core, y_index % 2]), back)


def solution(mesh):
    vid = mesh.devices.shape[0]
    cut = (YH, vid // (YH * NZ), NZ)
    fine = Mesh(
        mesh.devices.reshape(cut + mesh.devices.shape[1:]), ("yh", "x", "z", "aud", "tp")
    )
    tokens = ("yh", "x", "z", "aud")
    in_specs = (
        P(None, tokens, "tp"),
        P(None, tokens, "tp"),
        P(None, "tp"),
        P(None, "tp"),
        P(None, None, "tp"),
        P(),
        P(),
        P(),
    )
    out_specs = (P(tokens, "tp"), P(tokens, "tp"))
    return jax.shard_map(
        shards, mesh=fine, in_specs=in_specs, out_specs=out_specs, check_vma=False
    )
```

time: 168 us -> 137 us (0.82)
  waiting for transfers between devices: 64.6 us -> 31 us
  blocking collectives: 50.5 us -> 62.3 us
  starting transfers between devices: 15.5 us -> 9.92 us
    all_gather x2 -> x1, waiting for transfers between devices: 37.9 us -> 15.3 us  [shards(): keyval = lax.all_gather(keyval, ('z', 'tp'), axis=0)]
    all_to_all x0 -> x1, blocking collectives: none -> 19.2 us  [shards(): partial = lax.all_to_all(partial, 'x', split_axis=0, concat_axis=0)]
    all_to_all x1 -> x0, waiting for transfers between devices: 9.9 us -> none  [shards(): partial = lax.all_to_all(partial, 'x', split_axis=0, concat_axis=0)]
    all_gather x1, blocking collectives: 10.4 us -> 4.45 us  [shards(): back = lax.all_gather(back, 'tp', axis=0)]
    all_to_all x1 -> x0, starting transfers between devices: 3.52 us -> none  [shards(): partial = lax.all_to_all(partial, 'x', split_axis=0, concat_axis=0)]
    all_to_all x1, starting transfers between devices: 6.46 us -> 3.42 us  [shards(): queries = lax.all_to_all(queries, ring, split_axis=0, concat_axis=0)]
    pallas_call x1, Pallas kernels: 12.7 us -> 10.4 us  [shards(): pl.pallas_call(attend_kernel, grid=(HEADS_HERE,), out_shape=jax.ShapeDtyp...]
    unnamed x10 -> x19, local copies, waits for them, and re-layouts: 2.13 us -> 0.05 us
  transfers between devices with their start and end apart: 5 -> 3, of which waited for: 4 -> 3; matrix products, arithmetic and copies ran while one was open for 0% -> 1% of each run, Pallas kernels for 0% -> 0%
where the time goes in v2:
time: 137 us; the launch traced here: 136 us
  blocking collectives  62.3 us (45%)
  waiting for transfers between devices  31 us (23%)
  Pallas kernels  16.3 us (12%)
  between operations  14.9 us (11%)
  starting transfers between devices  9.92 us (7%)
  local copies, waits for them, and re-layouts  1.77 us (1%)
    all_to_all x1, blocking collectives, shards(): partial = lax.all_to_all(partial, 'x', split_axis=0, concat_axis=0)  19.2 us
    all_gather x1, waiting for transfers between devices, shards(): keyval = lax.all_gather(keyval, ('z', 'tp'), axis=0)  15.3 us
    all_to_all x1, blocking collectives, shards(): keyval = lax.all_to_all(keyval, ring, split_axis=0, concat_axis=0)  15.1 us
    all_gather x1, blocking collectives, shards(): queries = lax.all_gather(queries, 'x', axis=0)  12.4 us
    pallas_call x1, Pallas kernels, shards(): pl.pallas_call(attend_kernel, grid=(HEADS_HERE,), out_shape=jax.ShapeDtyp...  10.4 us
    all_gather x1, blocking collectives, shards(): packed = lax.all_gather(packed, 'tp', axis=0)  9.07 us
    all_to_all x1, waiting for transfers between devices, shards(): back = lax.all_to_all(back, ring, split_axis=0, concat_axis=0)  8.06 us
    all_to_all x1, waiting for transfers between devices, shards(): queries = lax.all_to_all(queries, ring, split_axis=0, concat_axis=0)  7.62 us
  transfers between devices with their start and end apart: 3, of which 3 were waited for; matrix products, arithmetic and copies ran while one was open for 1% of the time, Pallas kernels for 0%

profile of v2, /device:TPU:1, one launch (start us, length us, event | category | flops | bytes accessed | tf_op | source)
XLA Modules:
  0.0 136.4 jit_solution(1677429416275839566)
XLA Ops:
  7.2 0.0 copy-start
  7.2 0.0 copy-start.4
  7.2 0.0 copy-start.3
  7.2 0.0 copy-start.2
  7.2 0.0 all-gather.7.cloned.1.call-start
  7.3 1.9 %pack.1 = bf16[128,1536]{1,0:T(8,128)(2,1)} custom-call(s32[1]{0:T(128)} %bitcast.core_ref, bf16[4,32,1536]{2,1,0:T(8,128)(2,1)} %video_ref.3, bf16[4,8,1536]{2,1,0:T(8,128)(2,1)} %audio_ref.3, f32[3,1536]{1,0:T(4,128)} %video_gains_ref.3, f32[3,1536]{1,0:T(4,128)} %audio_gains_ref.3), custom_call_target="tpu_custom_call" | custom-call | tf_op jit(solution)/shard_map/pack/pallas_call | solution.py:317
  9.2 9.1 %all-gather = bf16[256,1536]{1,0:T(8,128)(2,1)S(1)} all-gather(bf16[128,1536]{1,0:T(8,128)(2,1)} %pack.1), channel_id=2, replica_groups=mesh['yh'=2,'x'=4,'z'=8,'aud'=4,'tp'=2] {'tp'}, dimensions={0}, use_global_device_ids=true | all-gather | bytes 1179648 | tf_op jit(solution)/shard_map/all_gather | solution.py:332
  18.3 1.1 norm.1
  19.4 15.1 %all_to_all.20 = bf16[8,40,384]{2,1,0:T(8,128)(2,1)} all-to-all(bf16[8,40,384]{2,1,0:T(8,128)(2,1)S(1)} %get-tuple-element.12), channel_id=1, replica_groups=mesh['yh'=2,'x'=4,'z'=8,'aud'=4,'tp'=2] {'yh','aud'}, dimensions={0} | all-to-all | bytes 491520 | tf_op jit(solution)/shard_map/all_to_all | solution.py:343
  34.5 0.0 all-gather.7.cloned.1.call-update
  35.2 0.1 reshape.76
  35.3 0.1 reshape.77
  35.4 0.1 copy.18
  35.5 0.1 compare_select_fusion.1
  35.5 3.4 %all-to-all-start.1 = ((bf16[8,40,384]{2,1,0:T(8,128)(2,1)}), bf16[8,40,384]{2,1,0:T(8,128)(2,1)S(1)}, u32[]{:S(2)}, u32[]{:S(2)}) async-start(bf16[8,40,384]{2,1,0:T(8,128)(2,1)} %get-tuple-element.14), calls=%async_computation.1 | async-start | bytes 491520 | tf_op jit(solution)/shard_map/all_to_all | solution.py:347
  39.0 0.1 copy.17
  39.1 2.0 %all-gather.2 = bf16[4,1,1536]{2,1,0:T(2,128)(2,1)S(1)} all-gather(bf16[2,1,1536]{2,1,0:T(2,128)(2,1)S(1)} %copy.21), channel_id=4, replica_groups=mesh['yh'=2,'x'=4,'z'=8,'aud'=4,'tp'=2] {'tp'}, dimensions={0}, use_global_device_ids=true | all-gather | bytes 18432 | tf_op jit(solution)/shard_map/all_gather | solution.py:377
  41.1 0.1 reduce
  41.2 0.7 select_n.63.audio_bias_ref
  41.9 0.1 compare_select_fusion
  42.0 0.7 select_n.61.video_bias_ref
  42.7 7.6 %all-to-all-done.1 = bf16[8,40,384]{2,1,0:T(8,128)(2,1)S(1)} async-done(((bf16[8,40,384]{2,1,0:T(8,128)(2,1)}), bf16[8,40,384]{2,1,0:T(8,128)(2,1)S(1)}, u32[]{:S(2)}, u32[]{:S(2)}) %all-to-all-start.1) | async-done | bytes 245792 | tf_op jit(solution)/shard_map/all_to_all | solution.py:347
  50.3 12.4 %all-gather.1 = bf16[32,40,384]{2,1,0:T(8,128)(2,1)} all-gather(bf16[8,40,384]{2,1,0:T(8,128)(2,1)S(1)} %all-to-all-done.1), channel_id=3, replica_groups=mesh['yh'=2,'x'=4,'z'=8,'aud'=4,'tp'=2] {'x'}, dimensions={0}, use_global_device_ids=true | all-gather | bytes 1228800 | tf_op jit(solution)/shard_map/all_gather | solution.py:348
  62.7 15.3 %all-gather.7.cloned.1.call-done = bf16[128,40,384]{2,1,0:T(8,128)(2,1)} async-done(((bf16[8,40,384]{2,1,0:T(8,128)(2,1)}), bf16[128,40,384]{2,1,0:T(8,128)(2,1)}) %all-gather.7.cloned.1.call-update) | async-done | bytes 3932176 | tf_op jit(solution)/shard_map/all_gather | solution.py:345
  78.0 10.4 %attend.1 = bf16[4,360,384]{2,1,0:T(8,128)(2,1)} custom-call(bf16[4,8,40,384]{3,2,1,0:T(8,128)(2,1)} %bitcast.26, bf16[8,2,8,40,384]{4,3,2,1,0:T(8,128)(2,1)} %bitcast.25, f32[1,2048]{1,0:T(1,128)} %select_n.61.video_bias_ref, f32[1,512]{1,0:T(1,128)} %select_n.63.audio_bias_ref), custom_call_target="tpu_custom_call" | custom-call | tf_op jit(solution)/shard_map/attend/pallas_call | solution.py:385
  88.3 19.2 %all_to_all.21.part_ref = bf16[4,360,384]{2,1,0:T(8,128)(2,1)S(1)} all-to-all(bf16[4,360,384]{2,1,0:T(8,128)(2,1)} %attend.1), channel_id=1, replica_groups=mesh['yh'=2,'x'=4,'z'=8,'aud'=4,'tp'=2] {'x'}, dimensions={0} | all-to-all | bytes 2211840 | tf_op jit(solution)/shard_map/all_to_all | solution.py:402
  107.6 1.7 %combine.1 = bf16[8,24,384]{2,1,0:T(8,128)(2,1)} custom-call(bf16[4,360,384]{2,1,0:T(8,128)(2,1)S(1)} %all_to_all.21.part_ref, f32[2,384]{1,0:T(2,128)S(1)} %bitcast_convert_fusion.gate_ref), custom_call_target="tpu_custom_call" | custom-call | tf_op jit(solution)/shard_map/combine/pallas_call | solution.py:403
  109.3 6.5 %all-to-all-start.3 = ((bf16[8,24,384]{2,1,0:T(8,128)(2,1)}), bf16[8,24,384]{2,1,0:T(8,128)(2,1)S(1)}, u32[]{:S(2)}, u32[]{:S(2)}) async-start(bf16[8,24,384]{2,1,0:T(8,128)(2,1)} %combine.1), calls=%async_computation.3 | async-start | bytes 294912 | tf_op jit(solution)/shard_map/all_to_all | solution.py:411
  115.7 0.1 pad_add_fusion.place_ref
  115.8 8.1 %all-to-all-done.3 = bf16[8,24,384]{2,1,0:T(8,128)(2,1)S(1)} async-done(((bf16[8,24,384]{2,1,0:T(8,128)(2,1)}), bf16[8,24,384]{2,1,0:T(8,128)(2,1)S(1)}, u32[]{:S(2)}, u32[]{:S(2)}) %all-to-all-start.3) | async-done | bytes 147488 | tf_op jit(solution)/shard_map/all_to_all | solution.py:411
  123.9 4.5 %all-gather.4 = bf16[16,24,384]{2,1,0:T(8,128)(2,1)S(1)} all-gather(bf16[8,24,384]{2,1,0:T(8,128)(2,1)S(1)} %all-to-all-done.3), channel_id=6, replica_groups=mesh['yh'=2,'x'=4,'z'=8,'aud'=4,'tp'=2] {'tp'}, dimensions={0}, use_global_device_ids=true | all-gather | bytes 442368 | tf_op jit(solution)/shard_map/all_gather | solution.py:412
  128.3 1.2 place.1
  (21 shorter events, 0.1 us)
Async XLA Ops:
  7.2 31.8 %copy-start = (bf16[2,50,1536]{2,0,1:T(2,128)(2,1)S(1)}, bf16[2,50,1536]{2,0,1:T(2,128)(2,1)}, u32[]{:S(2)}) copy-start(bf16[2,50,1536]{2,0,1:T(2,128)(2,1)} %param.14) | copy-start | bytes 921604
  7.2 11.1 %copy-start.4 = (f32[3,1536]{1,0:T(4,128)S(1)}, f32[3,1536]{1,0:T(4,128)}, u32[]{:S(2)}) copy-start(f32[3,1536]{1,0:T(4,128)} %audio_gains_ref.3) | copy-start | bytes 55300
  7.2 11.1 %copy-start.3 = (f32[3,1536]{1,0:T(4,128)S(1)}, f32[3,1536]{1,0:T(4,128)}, u32[]{:S(2)}) copy-start(f32[3,1536]{1,0:T(4,128)} %video_gains_ref.3) | copy-start | bytes 55300
  7.2 11.1 %copy-start.2 = (bf16[4,8,1536]{2,1,0:T(8,128)(2,1)S(1)}, bf16[4,8,1536]{2,1,0:T(8,128)(2,1)}, u32[]{:S(2)}) copy-start(bf16[4,8,1536]{2,1,0:T(8,128)(2,1)} %audio_ref.3) | copy-start | bytes 294916
  7.2 11.1 %copy-start.1 = (bf16[4,32,1536]{2,1,0:T(8,128)(2,1)S(1)}, bf16[4,32,1536]{2,1,0:T(8,128)(2,1)}, u32[]{:S(2)}) copy-start(bf16[4,32,1536]{2,1,0:T(8,128)(2,1)} %video_ref.3) | copy-start | bytes 1179652
  7.2 70.8 %all-gather.7.cloned.1.call-start = ((), (), s32[]{:S(2)}) async-start(), calls=%async_computation.4 | async-start | bytes 4177920 | tf_op jit(solution)/shard_map/all_gather | solution.py:345
  18.3 16.9 %copy-start.7 = (s32[64]{0:T(128)S(1)}, s32[64]{0:T(128)}, u32[]{:S(2)}) copy-start(s32[64]{0:T(128)} %param.16) | copy-start | bytes 772
  18.3 17.0 %copy-start.8 = (s32[64]{0:T(128)S(1)}, s32[64]{0:T(128)}, u32[]{:S(2)}) copy-start(s32[64]{0:T(128)} %param.17) | copy-start | bytes 772
  18.3 17.2 %copy-start.6 = (s32[8,8]{1,0:T(8,128)S(1)}, s32[8,8]{1,0:T(8,128)}, u32[]{:S(2)}) copy-start(s32[8,8]{1,0:T(8,128)} %constant.79) | copy-start | bytes 772
  19.4 22.5 %copy-start.5 = (s32[2,8,16]{2,1,0:T(8,128)S(1)}, s32[2,8,16]{2,1,0:T(8,128)}, u32[]{:S(2)}) copy-start(s32[2,8,16]{2,1,0:T(8,128)} %constant.78) | copy-start | bytes 3076
  35.5 14.8 %all-to-all-start.1 = ((bf16[8,40,384]{2,1,0:T(8,128)(2,1)}), bf16[8,40,384]{2,1,0:T(8,128)(2,1)S(1)}, u32[]{:S(2)}, u32[]{:S(2)}) async-start(bf16[8,40,384]{2,1,0:T(8,128)(2,1)} %get-tuple-element.14), calls=%async_computation.1 | async-start | bytes 491520 | tf_op jit(solution)/shard_map/all_to_all | solution.py:347
  109.3 14.6 %all-to-all-start.3 = ((bf16[8,24,384]{2,1,0:T(8,128)(2,1)}), bf16[8,24,384]{2,1,0:T(8,128)(2,1)S(1)}, u32[]{:S(2)}, u32[]{:S(2)}) async-start(bf16[8,24,384]{2,1,0:T(8,128)(2,1)} %combine.1), calls=%async_computation.3 | async-start | bytes 294912 | tf_op jit(solution)/shard_map/all_to_all | solution.py:411
Sparse Core Ops, SparseCore 0:
  34.6 43.2 all-gather.6

commit v3 on v2

--- a/solution.py
+++ b/solution.py
@@ -1,3 +1,4 @@
+import functools
 import math
 
 import jax
@@ -18,7 +19,8 @@
 
 YH = 2
 NY = 8
-NZ = 8
+ZP = 2
+ZQ = 4
 GROUP = D // NY
 HEADS_HERE = GROUP // HD
 VROWS = 16
@@ -33,7 +35,7 @@
 KEY_STEP = 256
 SCORE_SCALE = HD ** (-0.5) * math.log2(math.e)
 VMEM_LIMIT = 48 * 1024 * 1024
-ATTEND_VMEM = 60 * 1024 * 1024
+PACK_VMEM = 60 * 1024 * 1024
 
 
 def low_rows(shape):
@@ -63,14 +65,14 @@
 
 
 def norm_kernel(
+    for_queries,
     core_ref,
     video_ref,
     audio_ref,
     video_gains_ref,
     audio_gains_ref,
     packed_ref,
-    query_ref,
-    keyval_ref,
+    out_ref,
 ):
     core = core_ref[0]
     at_zero = core == 0
@@ -93,13 +95,17 @@
             for s, v in enumerate(halves)
         ]
 
-    def spread(out_ref, row, halves):
+    def spread(row, halves):
         count = halves[0].shape[0]
         for group in range(NY):
             col = (group % half_groups) * GROUP
-            out_ref[group, row : row + count, :] = halves[group // half_groups][
-                :, col : col + GROUP
-            ].astype(jnp.bfloat16)
+            rows = halves[group // half_groups][:, col : col + GROUP].astype(jnp.bfloat16)
+            if for_queries:
+                out_ref[group, row : row + count, :] = rows
+            else:
+                yh, aud = divmod(group, NY // YH)
+                for zq in range(out_ref.shape[1]):
+                    out_ref[yh, zq, aud, row : row + count, :] = rows
 
     def video(array):
         first = array * VROWS
@@ -115,17 +121,18 @@
             packed_ref[1 - core, first : first + 8, :].astype(jnp.float32),
         )
 
-    spread(keyval_ref, 0, normed(video(2), 2, 1.0))
-    spread(keyval_ref, VROWS, video(3))
-    audio_key = normed(audio(2), 5, 1.0)
-    audio_value = audio(3)
-    spread(
-        keyval_ref,
-        2 * VROWS,
-        [jnp.where(at_zero, k, v) for k, v in zip(audio_key, audio_value)],
-    )
-    spread(query_ref, 0, normed(video(0), 0, SCORE_SCALE))
-    spread(query_ref, VROWS, normed(video(1), 1, SCORE_SCALE))
+    if not for_queries:
+        spread(0, normed(video(2), 2, 1.0))
+        spread(VROWS, video(3))
+        audio_key = normed(audio(2), 5, 1.0)
+        audio_value = audio(3)
+        spread(
+            2 * VROWS,
+            [jnp.where(at_zero, k, v) for k, v in zip(audio_key, audio_value)],
+        )
+        return
+    spread(0, normed(video(0), 0, SCORE_SCALE))
+    spread(VROWS, normed(video(1), 1, SCORE_SCALE))
     audio_self = normed(audio(0), 3, SCORE_SCALE)
     audio_cross = normed(audio(1), 4, SCORE_SCALE)
     mixed = []
@@ -138,51 +145,67 @@
                 jnp.where(low, swap_halves(own), other),
             )
         )
-    spread(query_ref, 2 * VROWS, mixed)
-
-
-def attend_kernel(query_ref, keyval_ref, video_bias_ref, audio_bias_ref, out_ref):
+    spread(2 * VROWS, mixed)
+
+
+def attend_kernel(parities, begins, ends, core_ref, query_ref, *refs):
     x_count = query_ref.shape[0]
-    z_count = keyval_ref.shape[0]
-    video_keys = z_count * 2 * NY * VROWS
-    audio_keys = z_count * NY * 8
-    video_key = keyval_ref[:, :, :, :VROWS, :].reshape(video_keys, HD)
-    video_value = keyval_ref[:, :, :, VROWS : 2 * VROWS, :].reshape(video_keys, HD)
-
-    def audio_part(which):
-        rows = keyval_ref[:, which, :, 2 * VROWS :, :].astype(jnp.float32)
-        return rows.reshape(audio_keys, HD).astype(jnp.bfloat16)
-
-    audio_key, audio_value = audio_part(0), audio_part(1)
+    keyval_refs = refs[: 2 * parities]
+    video_bias_ref, audio_bias_ref, *rest = refs[2 * parities :]
+    holds_keys = core_ref[0] == 0
+
+    def rows_of(ref, first, last):
+        rows = ref[:, :, :, first:last, :]
+        if last - first == 8:
+            rows = rows.astype(jnp.float32)
+        return rows.reshape(-1, HD)
+
+    video_pieces, audio_pieces = [], []
+    for own, other in zip(keyval_refs[::2], keyval_refs[1::2]):
+        for ref in (own, other):
+            key = rows_of(ref, 0, VROWS)
+            value = rows_of(ref, VROWS, 2 * VROWS)
+            for first in range(0, key.shape[0], KEY_STEP):
+                keys = slice(first, first + KEY_STEP)
+                video_pieces.append((key[keys], value[keys]))
+        own, other = (rows_of(ref, 2 * VROWS, BLOCK) for ref in (own, other))
+        audio_pieces.append(
+            (
+                jnp.where(holds_keys, own, other).astype(jnp.bfloat16),
+                jnp.where(holds_keys, other, own).astype(jnp.bfloat16),
+            )
+        )
     lane = lax.broadcasted_iota(jnp.int32, (1, 8, HD), 2)
     row = lax.broadcasted_iota(jnp.int32, (1, 8, HD), 1)
     in_row = lane // 16 == row
     field = lane % 16
 
-    def attend(queries, key, value, bias_ref):
-        top = None
-        for first in range(0, key.shape[0], KEY_STEP):
-            keys = slice(first, first + KEY_STEP)
+    def attend(queries, pieces, bias_ref, state):
+        first = 0
+        for key, value in pieces:
+            keys = slice(first, first + key.shape[0])
+            first = keys.stop
             scores = lax.dot_general(
-                queries,
-                key[keys],
-                (((1,), (1,)), ((), ())),
-                preferred_element_type=jnp.float32,
+                queries, key, (((1,), (1,)), ((), ())), preferred_element_type=jnp.float32
             )
             scores = scores + bias_ref[0:1, keys]
-            here = jnp.max(scores, axis=1, keepdims=True)
-            here = here.astype(jnp.bfloat16).astype(jnp.float32)
-            new_top = here if top is None else jnp.maximum(top, here)
-            weights = jnp.exp2(scores - new_top)
-            new_total = jnp.sum(weights, axis=1, keepdims=True)
-            new_sums = jnp.dot(
-                weights.astype(jnp.bfloat16), value[keys], preferred_element_type=jnp.float32
-            )
-            if top is not None:
-                keep = jnp.exp2(top - new_top)
-                new_total = new_total + total * keep
-                new_sums = new_sums + sums * keep
-            top, total, sums = new_top, new_total, new_sums
+            top = jnp.max(scores, axis=1, keepdims=True)
+            top = top.astype(jnp.bfloat16).astype(jnp.float32)
+            if state is not None:
+                top = jnp.maximum(top, state[0])
+            weights = jnp.exp2(scores - top)
+            total = jnp.sum(weights, axis=1, keepdims=True)
+            sums = jnp.dot(
+                weights.astype(jnp.bfloat16), value, preferred_element_type=jnp.float32
+            )
+            if state is not None:
+                keep = jnp.exp2(state[0] - top)
+                total = total + state[1] * keep
+                sums = sums + state[2] * keep
+            state = top, total, sums
+        return state
+
+    def finish(top, total, sums):
         high = total.astype(jnp.bfloat16).astype(jnp.float32)
         groups = top.shape[0] // 8
 
@@ -205,14 +228,33 @@
     audio_cross = jnp.where(low, swap_halves(even), odd).reshape(-1, HD).astype(jnp.bfloat16)
     video_self = query_ref[:, :, :VROWS, :].reshape(x_count * VTOK_DEV, HD)
     video_cross = query_ref[:, :, VROWS : 2 * VROWS, :].reshape(x_count * VTOK_DEV, HD)
+    queries = (
+        jnp.concatenate([video_self, audio_cross], axis=0),
+        jnp.concatenate([video_cross, audio_self], axis=0),
+    )
+    pieces = (video_pieces, audio_pieces)
+    biases = (video_bias_ref, audio_bias_ref)
+    count = queries[0].shape[0]
     stats = []
-    for kind, (video, audio, key, value, bias_ref) in enumerate(
-        (
-            (video_self, audio_cross, video_key, video_value, video_bias_ref),
-            (video_cross, audio_self, audio_key, audio_value, audio_bias_ref),
-        )
-    ):
-        rows, stat = attend(jnp.concatenate([video, audio], axis=0), key, value, bias_ref)
+    for kind in range(2):
+        rows = slice(kind * count, (kind + 1) * count)
+        state = attend(queries[kind], pieces[kind], biases[kind], None)
+        top, total, sums = state
+        if not ends:
+            sums_ref, level_ref = rest
+            sums_ref[rows, :] = (sums / total).astype(jnp.bfloat16)
+            level_ref[rows, :] = jnp.broadcast_to(top + jnp.log2(total), (count, HD))
+            continue
+        if not begins:
+            old_sums_ref, old_level_ref, _ = rest
+            old_level = old_level_ref[rows, :]
+            new_top = jnp.maximum(top, old_level.astype(jnp.bfloat16).astype(jnp.float32))
+            keep, old_share = jnp.exp2(top - new_top), jnp.exp2(old_level - new_top)
+            total = total * keep + old_share
+            sums = sums * keep + old_sums_ref[rows, :].astype(jnp.float32) * old_share
+            state = new_top, total, sums
+        out_ref = rest[-1]
+        rows, stat = finish(*state)
         stats.append(stat)
         start = kind * (VTOK_DEV + ATOK_DEV)
         for x in range(x_count):
@@ -222,6 +264,8 @@
             out_ref[x, start + VTOK_DEV : start + VTOK_DEV + ATOK_DEV, :] = rows[
                 first : first + ATOK_DEV
             ]
+    if not ends:
+        return
     wide_stat, narrow_stat = VTOK_DEV // 8, ATOK_DEV // 8
     for x in range(x_count):
         picked = []
@@ -312,7 +356,8 @@
     core = lax.axis_index("tp")
     ring = ("yh", "aud")
     x_count = lax.axis_size("x")
-    z_count = lax.axis_size("z")
+    zq_count = lax.axis_size("zq")
+    z_parity = lax.axis_index("zp")
     y_index = lax.axis_index(ring)
     packed = pl.pallas_call(
         pack_kernel,
@@ -326,79 +371,120 @@
             pl.BlockSpec(audio_gains.shape, lambda i: (0, 0)),
         ],
         out_specs=pl.BlockSpec((PACK_ROWS, D // 2), lambda i: (0, 0)),
-        compiler_params=pltpu.CompilerParams(vmem_limit_bytes=ATTEND_VMEM),
+        compiler_params=pltpu.CompilerParams(vmem_limit_bytes=PACK_VMEM),
         name="pack",
     )(core[None], video_proj, audio_proj, video_gains, audio_gains)
     packed = lax.all_gather(packed, "tp", axis=0)
-    block = jax.ShapeDtypeStruct((NY, BLOCK, GROUP), jnp.bfloat16)
-    queries, keyval = pl.pallas_call(
-        norm_kernel,
-        out_shape=(block, block),
-        in_specs=[whole(pltpu.SMEM)] + [whole()] * 5,
-        out_specs=(whole(), whole()),
-        compiler_params=params(),
-        name="norm",
-    )(core[None], video_proj, audio_proj, video_gains, audio_gains, packed)
-
-    keyval = lax.all_to_all(keyval, ring, split_axis=0, concat_axis=0)
-    keyval, queries = lax.optimization_barrier((keyval, queries))
-    keyval = lax.all_gather(keyval, ("z", "tp"), axis=0)
-    keyval = keyval.reshape(z_count, 2, NY, BLOCK, GROUP)
+    def norm(for_queries, shape):
+        return pl.pallas_call(
+            functools.partial(norm_kernel, for_queries),
+            out_shape=jax.ShapeDtypeStruct(shape + (BLOCK, GROUP), jnp.bfloat16),
+            in_specs=[whole(pltpu.SMEM)] + [whole()] * 5,
+            out_specs=whole(),
+            compiler_params=params(),
+            name="norm_queries" if for_queries else "norm_keys",
+        )(core[None], video_proj, audio_proj, video_gains, audio_gains, packed)
+
+    queries = norm(True, (NY,))
+    keyval = norm(False, (YH, zq_count, NY // YH))
+
+    full_shape = keyval.shape
+    keyval = keyval.reshape((YH * zq_count * (NY // YH),) + full_shape[3:])
+    keyval = lax.all_to_all(keyval, ("yh", "zq", "aud"), split_axis=0, concat_axis=0)
     queries = lax.all_to_all(queries, ring, split_axis=0, concat_axis=0)
     queries = lax.all_gather(queries, "x", axis=0)
 
-    shape = (YH, x_count, z_count)
     x_index = lax.axis_index("x")
-
-    aud_of = np.arange(NY) % (NY // YH)
+    aud_first = np.arange(NY // YH)
+    parities = jnp.stack([z_parity, 1 - z_parity])
+    halves = jnp.stack([core, 1 - core])
+
+    def allowed(counts):
+        here = counts.reshape(YH, x_count, zq_count, ZP)
+        here = lax.dynamic_index_in_dim(here, x_index, 1, keepdims=False)
+        here = jnp.moveaxis(here, 2, 0)
+        return jnp.where(z_parity == 0, here, here[::-1])
+
+    def bias(live):
+        return jnp.where(live, 0.0, MASKED).astype(jnp.float32).reshape(1, -1)
+
     video_first = (
-        aud_of[None, None, :, None] * (2 * VROWS)
-        + np.arange(2)[None, :, None, None] * VROWS
-        + np.arange(VROWS)[None, None, None, :]
+        aud_first[None, :, None] * (2 * VROWS)
+        + halves[:, None, None] * VROWS
+        + np.arange(VROWS)[None, None, :]
     )
-    audio_first = aud_of[None, :, None] * 8 + np.arange(8)[None, None, :]
-    video_width = z_count * 2 * NY * VROWS
-    audio_width = z_count * NY * 8
-
-    def allowed(counts):
-        here = lax.dynamic_index_in_dim(counts.reshape(shape), x_index, 1, keepdims=False)
-        return jnp.repeat(here.T, NY // YH, axis=1)
-
-    video_bias = jnp.where(
-        video_first < allowed(video_counts)[:, None, :, None], 0.0, MASKED
-    )
-    audio_bias = jnp.where(audio_first < allowed(audio_counts)[:, :, None], 0.0, MASKED)
-    video_bias = video_bias.astype(jnp.float32).reshape(1, video_width)
-    audio_bias = audio_bias.astype(jnp.float32).reshape(1, audio_width)
-    queries, video_bias, audio_bias, step = lax.optimization_barrier(
-        (queries, video_bias, audio_bias, timestep)
-    )
-    gates = lax.dynamic_index_in_dim(cross_gates, step[0], 1, keepdims=False)
+    audio_first = aud_first[:, None] * 8 + np.arange(8)[None, :]
+    allowed_video, allowed_audio = allowed(video_counts), allowed(audio_counts)
+    biases = [
+        (
+            bias(video_first[:, None, None] < allowed_video[parity][None, :, :, None, None]),
+            bias(audio_first < allowed_audio[parity][..., None, None]),
+        )
+        for parity in range(ZP)
+    ]
+    places = jnp.stack([core, y_index % 2])
+    gates = lax.dynamic_index_in_dim(cross_gates, timestep[0], 1, keepdims=False)
+    gates, packed = lax.optimization_barrier((gates, packed))
     gates = lax.all_gather(gates, "tp", axis=0)
     gates = lax.dynamic_slice(
         gates,
         (y_index // (NY // 2), 0, (y_index % (NY // 2)) * GROUP),
         (1, 2, GROUP),
     )[0].astype(jnp.float32)
-    queries, gates = lax.optimization_barrier((queries, gates))
-
-    partial = pl.pallas_call(
-        attend_kernel,
-        grid=(HEADS_HERE,),
-        out_shape=jax.ShapeDtypeStruct(
-            (x_count, OUT_ROWS + STAT_ROWS, GROUP), jnp.bfloat16
-        ),
-        in_specs=[
-            pl.BlockSpec((x_count, NY, BLOCK, HD), lambda h: (0, 0, 0, h)),
-            pl.BlockSpec((z_count, 2, NY, BLOCK, HD), lambda h: (0, 0, 0, 0, h)),
-            pl.BlockSpec((1, video_width), lambda h: (0, 0)),
-            pl.BlockSpec((1, audio_width), lambda h: (0, 0)),
-        ],
-        out_specs=pl.BlockSpec((x_count, OUT_ROWS + STAT_ROWS, HD), lambda h: (0, 0, h)),
-        compiler_params=pltpu.CompilerParams(vmem_limit_bytes=ATTEND_VMEM),
-        name="attend",
-    )(queries, keyval, video_bias, audio_bias)
-
+    queries, gates, biases, keyval, places = lax.optimization_barrier(
+        (queries, gates, biases, keyval, places)
+    )
+
+    ways = [
+        (z * 2 + c, (z + 1 - 2 * c) % (ZP * zq_count) * 2 + c)
+        for z in range(ZP * zq_count)
+        for c in range(2)
+    ]
+    swap = [(0, 1), (1, 0)]
+    far = lax.ppermute(keyval, ("zq", "zp", "tp"), ways)
+    keyval_other = lax.ppermute(keyval, "tp", swap)
+    near = [keyval.reshape(full_shape), keyval_other.reshape(full_shape)]
+
+    def attend(keyvals, video_bias, audio_bias, state, ends):
+        parities = len(keyvals) // 2
+        rows = 2 * x_count * (VTOK_DEV + ATOK_DEV)
+        state_spec = pl.BlockSpec((rows, HD), lambda h: (0, h))
+        if ends:
+            out_shape = jax.ShapeDtypeStruct(
+                (x_count, OUT_ROWS + STAT_ROWS, GROUP), jnp.bfloat16
+            )
+            out_specs = pl.BlockSpec(
+                (x_count, OUT_ROWS + STAT_ROWS, HD), lambda h: (0, 0, h)
+            )
+        else:
+            out_shape = tuple(
+                jax.ShapeDtypeStruct((rows, GROUP), dtype)
+                for dtype in (jnp.bfloat16, jnp.float32)
+            )
+            out_specs = (state_spec,) * 2
+        keyval_spec = pl.BlockSpec(full_shape[:-1] + (HD,), lambda h: (0, 0, 0, 0, h))
+        return pl.pallas_call(
+            functools.partial(attend_kernel, parities, not state, ends),
+            grid=(HEADS_HERE,),
+            out_shape=out_shape,
+            in_specs=[
+                whole(pltpu.SMEM),
+                pl.BlockSpec((x_count, NY, BLOCK, HD), lambda h: (0, 0, 0, h)),
+                *[keyval_spec] * len(keyvals),
+                pl.BlockSpec(video_bias.shape, lambda h: (0, 0)),
+                pl.BlockSpec(audio_bias.shape, lambda h: (0, 0)),
+                *[state_spec] * len(state),
+            ],
+            out_specs=out_specs,
+            compiler_params=params(),
+            name="attend_near" if not ends else "attend",
+        )(core[None], queries, *keyvals, video_bias, audio_bias, *state)
+
+    state = attend(near, *biases[0], (), False)
+    far, *state = lax.optimization_barrier((far, *state))
+    far_other = lax.ppermute(far, "tp", swap)
+    far = [far.reshape(full_shape), far_other.reshape(full_shape)]
+    partial = attend(far, *biases[1], state, True)
     partial = lax.all_to_all(partial, "x", split_axis=0, concat_axis=0)
     back = pl.pallas_call(
         combine_kernel,
@@ -420,16 +506,15 @@
         out_specs=(whole(), whole()),
         compiler_params=params(),
         name="place",
-    )(jnp.stack([core, y_index % 2]), back)
+    )(places, back)
 
 
 def solution(mesh):
     vid = mesh.devices.shape[0]
-    cut = (YH, vid // (YH * NZ), NZ)
-    fine = Mesh(
-        mesh.devices.reshape(cut + mesh.devices.shape[1:]), ("yh", "x", "z", "aud", "tp")
-    )
-    tokens = ("yh", "x", "z", "aud")
+    cut = (YH, vid // (YH * ZQ * ZP), ZQ, ZP)
+    axes = ("yh", "x", "zq", "zp", "aud", "tp")
+    fine = Mesh(mesh.devices.reshape(cut + mesh.devices.shape[1:]), axes)
+    tokens = axes[:-1]
     in_specs = (
         P(None, tokens, "tp"),
         P(None, tokens, "tp"),

time: 137 us -> 134 us (0.978)
  between operations: 14.9 us -> 1.58 us
  starting transfers between devices: 9.92 us -> 21.7 us
  blocking collectives: 62.3 us -> 59.3 us
  Pallas kernels: 16.3 us -> 18.6 us
    all_gather x1 -> x0, waiting for transfers between devices: 15.3 us -> none  [shards(): keyval = lax.all_gather(keyval, ('z', 'tp'), axis=0)]
    ppermute x0 -> x3, starting transfers between devices: none -> 10.5 us  [the longest x1 4.61 us: shards(): keyval_other = lax.ppermute(keyval, 'tp', swap)]
    ppermute x0 -> x3, waiting for transfers between devices: none -> 9.05 us  [the longest x1 6.63 us: shards(): far = lax.ppermute(keyval, ('zq', 'zp', 'tp'), ways)]
    all_to_all x1, blocking collectives: 15.1 us -> 10.5 us  [shards(): back = lax.all_to_all(back, ring, split_axis=0, concat_axis=0)]
    all_to_all x1, waiting for transfers between devices: 8.06 us -> 12 us  [shards(): lax.all_to_all(keyval, ('yh', 'zq', 'aud'), split_axis=0, concat_axis=0)]
    pallas_call x2 -> x4, Pallas kernels: 11.4 us -> 14.4 us  [the longest x2 12.3 us: attend(): pl.pallas_call(functools.partial(attend_kernel, parities, not state, ends...]
    all_to_all x1, waiting for transfers between devices: 7.62 us -> 9.07 us  [shards(): queries = lax.all_to_all(queries, ring, split_axis=0, concat_axis=0)]
  transfers between devices with their start and end apart: 3 -> 5, of which waited for: 3 -> 5; matrix products, arithmetic and copies ran while one was open for 1% -> 1% of each run, Pallas kernels for 0% -> 5%
where the time goes in v3:
time: 134 us
  blocking collectives  59.3 us (44%)
  waiting for transfers between devices  30.1 us (22%)
  starting transfers between devices  21.7 us (16%)
  Pallas kernels  18.6 us (14%)
  local copies, waits for them, and re-layouts  2.21 us (2%)
  between operations  1.58 us (1%)
    all_to_all x1, blocking collectives, shards(): partial = lax.all_to_all(partial, 'x', split_axis=0, concat_axis=0)  19 us
    all_gather x1, blocking collectives, shards(): queries = lax.all_gather(queries, 'x', axis=0)  13.1 us
    pallas_call x2, Pallas kernels, attend(): pl.pallas_call(functools.partial(attend_kernel, parities, not state, ends...  12.3 us
    all_to_all x1, waiting for transfers between devices, shards(): lax.all_to_all(keyval, ('yh', 'zq', 'aud'), split_axis=0, concat_axis=0)  12 us
    all_to_all x1, blocking collectives, shards(): back = lax.all_to_all(back, ring, split_axis=0, concat_axis=0)  10.5 us
    all_gather x1, blocking collectives, shards(): packed = lax.all_gather(packed, 'tp', axis=0)  9.07 us
    all_to_all x1, waiting for transfers between devices, shards(): queries = lax.all_to_all(queries, ring, split_axis=0, concat_axis=0)  9.07 us
    all_to_all x1, starting transfers between devices, shards(): lax.all_to_all(keyval, ('yh', 'zq', 'aud'), split_axis=0, concat_axis=0)  7.76 us
  transfers between devices with their start and end apart: 5, of which 5 were waited for; matrix products, arithmetic and copies ran while one was open for 1% of the time, Pallas kernels for 5%

profile of v3, /device:TPU:1, one launch (start us, length us, event | category | flops | bytes accessed | tf_op | source)
XLA Modules:
  0.0 133.9 jit_solution(16637624960675856600)
XLA Ops:
  0.7 1.9 %pack.1 = bf16[128,1536]{1,0:T(8,128)(2,1)} custom-call(s32[1]{0:T(128)} %bitcast.core_ref, bf16[4,32,1536]{2,1,0:T(8,128)(2,1)} %video_ref.5, bf16[4,8,1536]{2,1,0:T(8,128)(2,1)} %audio_ref.5, f32[3,1536]{1,0:T(4,128)} %video_gains_ref.5, f32[3,1536]{1,0:T(4,128)} %audio_gains_ref.5), custom_call_target="tpu_custom_call" | custom-call | tf_op jit(solution)/shard_map/pack/pallas_call | solution.py:362
  2.6 9.1 %all-gather = bf16[256,1536]{1,0:T(8,128)(2,1)S(1)} all-gather(bf16[128,1536]{1,0:T(8,128)(2,1)} %pack.1), channel_id=2, replica_groups=mesh['yh'=2,'x'=4,'zq'=4,'zp'=2,'aud'=4,'tp'=2] {'tp'}, dimensions={0}, use_global_device_ids=true | all-gather | bytes 1179648 | tf_op jit(solution)/shard_map/all_gather | solution.py:377
  11.7 1.0 norm_queries.1
  12.6 3.4 %all-to-all-start = ((bf16[8,40,384]{2,1,0:T(8,128)(2,1)}), bf16[8,40,384]{2,1,0:T(8,128)(2,1)S(1)}, u32[]{:S(2)}, u32[]{:S(2)}) async-start(bf16[8,40,384]{2,1,0:T(8,128)(2,1)} %norm_queries.1), calls=%async_computation | async-start | bytes 491520 | tf_op jit(solution)/shard_map/all_to_all | solution.py:394
  16.1 1.2 norm_keys.1
  18.0 0.1 reshape.200
  18.1 0.1 reshape.201
  18.2 0.1 copy.18
  18.3 0.1 copy.17
  18.6 0.1 select_n.112.refs_3_
  18.7 0.1 select_n.108.refs_3_
  18.9 9.1 %all-to-all-done = bf16[8,40,384]{2,1,0:T(8,128)(2,1)S(1)} async-done(((bf16[8,40,384]{2,1,0:T(8,128)(2,1)}), bf16[8,40,384]{2,1,0:T(8,128)(2,1)S(1)}, u32[]{:S(2)}, u32[]{:S(2)}) %all-to-all-start) | async-done | bytes 245792 | tf_op jit(solution)/shard_map/all_to_all | solution.py:394
  27.9 7.8 %all-to-all-start.1 = ((bf16[32,40,384]{2,1,0:T(8,128)(2,1)}), bf16[32,40,384]{2,1,0:T(8,128)(2,1)S(1)}, u32[]{:S(2)}, u32[]{:S(2)}) async-start(bf16[32,40,384]{2,1,0:T(8,128)(2,1)} %bitcast.18), calls=%async_computation.1 | async-start | bytes 1966080 | tf_op jit(solution)/shard_map/all_to_all | solution.py:393
  36.0 0.1 select_n.110.refs_2_
  36.0 0.1 select_n.105.refs_2_
  36.2 3.1 %all-gather.4 = bf16[2,2,1536]{2,1,0:T(2,128)(2,1)S(1)} all-gather(bf16[1,2,1536]{2,1,0:T(2,128)(2,1)S(1)} %bitcast.42), channel_id=4, replica_groups=mesh['yh'=2,'x'=4,'zq'=4,'zp'=2,'aud'=4,'tp'=2] {'tp'}, dimensions={0}, use_global_device_ids=true | all-gather | bytes 18432 | tf_op jit(solution)/shard_map/all_gather | solution.py:428
  39.3 13.1 %all-gather.1 = bf16[32,40,384]{2,1,0:T(8,128)(2,1)S(1)} all-gather(bf16[8,40,384]{2,1,0:T(8,128)(2,1)S(1)} %all-to-all-done), channel_id=3, replica_groups=mesh['yh'=2,'x'=4,'zq'=4,'zp'=2,'aud'=4,'tp'=2] {'x'}, dimensions={0}, use_global_device_ids=true | all-gather | bytes 1228800 | tf_op jit(solution)/shard_map/all_gather | solution.py:395
  52.5 12.0 %all-to-all-done.1 = bf16[32,40,384]{2,1,0:T(8,128)(2,1)S(1)} async-done(((bf16[32,40,384]{2,1,0:T(8,128)(2,1)}), bf16[32,40,384]{2,1,0:T(8,128)(2,1)S(1)}, u32[]{:S(2)}, u32[]{:S(2)}) %all-to-all-start.1) | async-done | bytes 983072 | tf_op jit(solution)/shard_map/all_to_all | solution.py:393
  64.4 4.6 %collective-permute-start.1 = (bf16[32,40,384]{2,1,0:T(8,128)(2,1)S(1)}, bf16[32,40,384]{2,1,0:T(8,128)(2,1)S(1)}, u32[]{:S(2)}, u32[]{:S(2)}) collective-permute-start(bf16[32,40,384]{2,1,0:T(8,128)(2,1)S(1)} %all-to-all-done.1), channel_id=1, source_target_pairs={{0,1},{1,0},{2,3},{3,2},{4,5},{5,4},{6,7},{7,6},{8,9},{9,8},{10,11... | collective-permute-start | bytes 2949128 | tf_op jit(solution)/shard_map/ppermute | solution.py:445
  69.0 1.9 %collective-permute-start = (bf16[32,40,384]{2,1,0:T(8,128)(2,1)S(1)}, bf16[32,40,384]{2,1,0:T(8,128)(2,1)S(1)}, u32[]{:S(2)}, u32[]{:S(2)}) collective-permute-start(bf16[32,40,384]{2,1,0:T(8,128)(2,1)S(1)} %all-to-all-done.1), channel_id=1, source_target_pairs={{0,8},{1,57},{8,16},{9,1},{16,24},{17,9},{24,32},{25,17},{32,40},{... | collective-permute-start | bytes 2949128 | tf_op jit(solution)/shard_map/ppermute | solution.py:444
  71.0 0.2 collective-permute-done.1
  71.2 5.0 %attend_near.1 = (bf16[1280,384]{1,0:T(8,128)(2,1)S(1)}, f32[1280,384]{1,0:T(8,128)S(1)}) custom-call(s32[1]{0:T(128)} %bitcast.core_ref, bf16[4,8,40,384]{3,2,1,0:T(8,128)(2,1)S(1)} %bitcast.33, bf16[2,4,4,40,384]{4,3,2,1,0:T(8,128)(2,1)S(1)} %bitcast.37, bf16[2,4,4,40,384]{4,3,2,1,0:T(8,128)(2,1)S(1)} %bitcast.40, f32[1,1024]{1,0:T(1,128)S(1)} %select_n.105.refs_2_, ...), custom_call_target="tpu_custom_call" | custom-call | tf_op jit(solution)/shard_map/attend_near/pallas_call | solution.py:466
  76.3 1.3 copy-done.2
  77.5 6.6 %collective-permute-done = bf16[32,40,384]{2,1,0:T(8,128)(2,1)S(1)} collective-permute-done((bf16[32,40,384]{2,1,0:T(8,128)(2,1)S(1)}, bf16[32,40,384]{2,1,0:T(8,128)(2,1)S(1)}, u32[]{:S(2)}, u32[]{:S(2)}) %collective-permute-start) | collective-permute-done | bytes 983072 | tf_op jit(solution)/shard_map/ppermute | solution.py:444
  84.2 4.0 %collective-permute-start.2 = (bf16[32,40,384]{2,1,0:T(8,128)(2,1)S(1)}, bf16[32,40,384]{2,1,0:T(8,128)(2,1)S(1)}, u32[]{:S(2)}, u32[]{:S(2)}) collective-permute-start(bf16[32,40,384]{2,1,0:T(8,128)(2,1)S(1)} %collective-permute-done), channel_id=1, source_target_pairs={{0,1},{1,0},{2,3},{3,2},{4,5},{5,4},{6,7},{7,6},{8,9},{9,8},{10,11... | collective-permute-start | bytes 2949128 | tf_op jit(solution)/shard_map/ppermute | solution.py:485
  88.2 2.2 %collective-permute-done.2 = bf16[32,40,384]{2,1,0:T(8,128)(2,1)S(1)} collective-permute-done((bf16[32,40,384]{2,1,0:T(8,128)(2,1)S(1)}, bf16[32,40,384]{2,1,0:T(8,128)(2,1)S(1)}, u32[]{:S(2)}, u32[]{:S(2)}) %collective-permute-start.2) | collective-permute-done | bytes 983072 | tf_op jit(solution)/shard_map/ppermute | solution.py:485
  90.3 7.3 %attend.1 = bf16[4,360,384]{2,1,0:T(8,128)(2,1)S(1)} custom-call(s32[1]{0:T(128)} %bitcast.core_ref, bf16[4,8,40,384]{3,2,1,0:T(8,128)(2,1)S(1)} %bitcast.34, bf16[2,4,4,40,384]{4,3,2,1,0:T(8,128)(2,1)S(1)} %bitcast.39, bf16[2,4,4,40,384]{4,3,2,1,0:T(8,128)(2,1)S(1)} %bitcast.41, f32[1,1024]{1,0:T(1,128)S(1)} %select_n.110.refs_2_, ...), custom_call_target="tpu_custom_call" | custom-call | tf_op jit(solution)/shard_map/attend/pallas_call | solution.py:466
  97.6 19.0 %all_to_all.20.part_ref = bf16[4,360,384]{2,1,0:T(8,128)(2,1)S(1)} all-to-all(bf16[4,360,384]{2,1,0:T(8,128)(2,1)S(1)} %attend.1), channel_id=1, replica_groups=mesh['yh'=2,'x'=4,'zq'=4,'zp'=2,'aud'=4,'tp'=2] {'x'}, dimensions={0} | all-to-all | bytes 2211840 | tf_op jit(solution)/shard_map/all_to_all | solution.py:488
  116.6 1.1 combine.1
  117.6 10.5 %all_to_all.21 = bf16[8,24,384]{2,1,0:T(8,128)(2,1)S(1)} all-to-all(bf16[8,24,384]{2,1,0:T(8,128)(2,1)S(1)} %combine.1), channel_id=1, replica_groups=mesh['yh'=2,'x'=4,'zq'=4,'zp'=2,'aud'=4,'tp'=2] {'yh','aud'}, dimensions={0} | all-to-all | bytes 294912 | tf_op jit(solution)/shard_map/all_to_all | solution.py:497
  128.1 4.5 %all-gather.3 = bf16[16,24,384]{2,1,0:T(8,128)(2,1)S(1)} all-gather(bf16[8,24,384]{2,1,0:T(8,128)(2,1)S(1)} %all_to_all.21), channel_id=5, replica_groups=mesh['yh'=2,'x'=4,'zq'=4,'zp'=2,'aud'=4,'tp'=2] {'tp'}, dimensions={0}, use_global_device_ids=true | all-gather | bytes 442368 | tf_op jit(solution)/shard_map/all_gather | solution.py:498
  132.7 1.2 place.1
  (33 shorter events, 0.6 us)
Async XLA Ops:
  0.6 35.5 %copy-start = (bf16[2,50,1536]{2,0,1:T(2,128)(2,1)S(1)}, bf16[2,50,1536]{2,0,1:T(2,128)(2,1)}, u32[]{:S(2)}) copy-start(bf16[2,50,1536]{2,0,1:T(2,128)(2,1)} %param.15) | copy-start | bytes 921604
  0.6 11.0 %copy-start.5 = (f32[3,1536]{1,0:T(4,128)S(1)}, f32[3,1536]{1,0:T(4,128)}, u32[]{:S(2)}) copy-start(f32[3,1536]{1,0:T(4,128)} %audio_gains_ref.5) | copy-start | bytes 55300
  0.7 11.0 %copy-start.4 = (f32[3,1536]{1,0:T(4,128)S(1)}, f32[3,1536]{1,0:T(4,128)}, u32[]{:S(2)}) copy-start(f32[3,1536]{1,0:T(4,128)} %video_gains_ref.5) | copy-start | bytes 55300
  0.7 11.0 %copy-start.3 = (bf16[4,8,1536]{2,1,0:T(8,128)(2,1)S(1)}, bf16[4,8,1536]{2,1,0:T(8,128)(2,1)}, u32[]{:S(2)}) copy-start(bf16[4,8,1536]{2,1,0:T(8,128)(2,1)} %audio_ref.5) | copy-start | bytes 294916
  0.7 11.0 %copy-start.1 = (bf16[4,32,1536]{2,1,0:T(8,128)(2,1)S(1)}, bf16[4,32,1536]{2,1,0:T(8,128)(2,1)}, u32[]{:S(2)}) copy-start(bf16[4,32,1536]{2,1,0:T(8,128)(2,1)} %video_ref.5) | copy-start | bytes 1179652
  12.6 15.3 %all-to-all-start = ((bf16[8,40,384]{2,1,0:T(8,128)(2,1)}), bf16[8,40,384]{2,1,0:T(8,128)(2,1)S(1)}, u32[]{:S(2)}, u32[]{:S(2)}) async-start(bf16[8,40,384]{2,1,0:T(8,128)(2,1)} %norm_queries.1), calls=%async_computation | async-start | bytes 491520 | tf_op jit(solution)/shard_map/all_to_all | solution.py:394
  16.1 1.9 %copy-start.7 = (s32[64]{0:T(128)S(1)}, s32[64]{0:T(128)}, u32[]{:S(2)}) copy-start(s32[64]{0:T(128)} %param.17) | copy-start | bytes 772
  16.1 2.0 %copy-start.8 = (s32[64]{0:T(128)S(1)}, s32[64]{0:T(128)}, u32[]{:S(2)}) copy-start(s32[64]{0:T(128)} %param.18) | copy-start | bytes 772
  16.1 2.4 %copy-start.6 = (s32[4,8]{1,0:T(4,128)S(1)}, s32[4,8]{1,0:T(4,128)}, u32[]{:S(2)}) copy-start(s32[4,8]{1,0:T(4,128)} %constant.84.clone) | copy-start | bytes 388
  27.9 36.5 %all-to-all-start.1 = ((bf16[32,40,384]{2,1,0:T(8,128)(2,1)}), bf16[32,40,384]{2,1,0:T(8,128)(2,1)S(1)}, u32[]{:S(2)}, u32[]{:S(2)}) async-start(bf16[32,40,384]{2,1,0:T(8,128)(2,1)} %bitcast.18), calls=%async_computation.1 | async-start | bytes 1966080 | tf_op jit(solution)/shard_map/all_to_all | solution.py:393
  64.4 6.8 %collective-permute-start.1 = (bf16[32,40,384]{2,1,0:T(8,128)(2,1)S(1)}, bf16[32,40,384]{2,1,0:T(8,128)(2,1)S(1)}, u32[]{:S(2)}, u32[]{:S(2)}) collective-permute-start(bf16[32,40,384]{2,1,0:T(8,128)(2,1)S(1)} %all-to-all-done.1), channel_id=1, source_target_pairs={{0,1},{1,0},{2,3},{3,2},{4,5},{5,4},{6,7},{7,6},{8,9},{9,8},{10,11... | collective-permute-start | bytes 2949128 | tf_op jit(solution)/shard_map/ppermute | solution.py:445
  69.0 15.1 %collective-permute-start = (bf16[32,40,384]{2,1,0:T(8,128)(2,1)S(1)}, bf16[32,40,384]{2,1,0:T(8,128)(2,1)S(1)}, u32[]{:S(2)}, u32[]{:S(2)}) collective-permute-start(bf16[32,40,384]{2,1,0:T(8,128)(2,1)S(1)} %all-to-all-done.1), channel_id=1, source_target_pairs={{0,8},{1,57},{8,16},{9,1},{16,24},{17,9},{24,32},{25,17},{32,40},{... | collective-permute-start | bytes 2949128 | tf_op jit(solution)/shard_map/ppermute | solution.py:444
  76.3 1.3 copy-start.2
  84.2 6.2 %collective-permute-start.2 = (bf16[32,40,384]{2,1,0:T(8,128)(2,1)S(1)}, bf16[32,40,384]{2,1,0:T(8,128)(2,1)S(1)}, u32[]{:S(2)}, u32[]{:S(2)}) collective-permute-start(bf16[32,40,384]{2,1,0:T(8,128)(2,1)S(1)} %collective-permute-done), channel_id=1, source_target_pairs={{0,1},{1,0},{2,3},{3,2},{4,5},{5,4},{6,7},{7,6},{8,9},{9,8},{10,11... | collective-permute-start | bytes 2949128 | tf_op jit(solution)/shard_map/ppermute | solution.py:485

commit v4 on v3

--- a/solution.py
+++ b/solution.py
@@ -65,7 +65,6 @@
 
 
 def norm_kernel(
-    for_queries,
     core_ref,
     video_ref,
     audio_ref,
@@ -99,13 +98,9 @@
         count = halves[0].shape[0]
         for group in range(NY):
             col = (group % half_groups) * GROUP
-            rows = halves[group // half_groups][:, col : col + GROUP].astype(jnp.bfloat16)
-            if for_queries:
-                out_ref[group, row : row + count, :] = rows
-            else:
-                yh, aud = divmod(group, NY // YH)
-                for zq in range(out_ref.shape[1]):
-                    out_ref[yh, zq, aud, row : row + count, :] = rows
+            out_ref[group, row : row + count, :] = halves[group // half_groups][
+                :, col : col + GROUP
+            ].astype(jnp.bfloat16)
 
     def video(array):
         first = array * VROWS
@@ -121,18 +116,16 @@
             packed_ref[1 - core, first : first + 8, :].astype(jnp.float32),
         )
 
-    if not for_queries:
-        spread(0, normed(video(2), 2, 1.0))
-        spread(VROWS, video(3))
-        audio_key = normed(audio(2), 5, 1.0)
-        audio_value = audio(3)
-        spread(
-            2 * VROWS,
-            [jnp.where(at_zero, k, v) for k, v in zip(audio_key, audio_value)],
-        )
-        return
-    spread(0, normed(video(0), 0, SCORE_SCALE))
-    spread(VROWS, normed(video(1), 1, SCORE_SCALE))
+    spread(0, normed(video(2), 2, 1.0))
+    spread(VROWS, video(3))
+    audio_key = normed(audio(2), 5, 1.0)
+    audio_value = audio(3)
+    spread(
+        2 * VROWS,
+        [jnp.where(at_zero, k, v) for k, v in zip(audio_key, audio_value)],
+    )
+    spread(BLOCK, normed(video(0), 0, SCORE_SCALE))
+    spread(BLOCK + VROWS, normed(video(1), 1, SCORE_SCALE))
     audio_self = normed(audio(0), 3, SCORE_SCALE)
     audio_cross = normed(audio(1), 4, SCORE_SCALE)
     mixed = []
@@ -145,7 +138,7 @@
                 jnp.where(low, swap_halves(own), other),
             )
         )
-    spread(2 * VROWS, mixed)
+    spread(BLOCK + 2 * VROWS, mixed)
 
 
 def attend_kernel(parities, begins, ends, core_ref, query_ref, *refs):
@@ -218,7 +211,7 @@
             jnp.where(field == 1, wide(high), wide(total - high)),
         )
         stats = jnp.sum(jnp.where(in_row & (field < 3), stats, 0.0), axis=1)
-        return (sums / total).astype(jnp.bfloat16), stats
+        return (sums * pl.reciprocal(total)).astype(jnp.bfloat16), stats
 
     audio_rows = query_ref[:, :, 2 * VROWS :, :].astype(jnp.float32)
     audio_rows = audio_rows.reshape(x_count * NY // 2, 2, 8, HD)
@@ -242,7 +235,7 @@
         top, total, sums = state
         if not ends:
             sums_ref, level_ref = rest
-            sums_ref[rows, :] = (sums / total).astype(jnp.bfloat16)
+            sums_ref[rows, :] = (sums * pl.reciprocal(total)).astype(jnp.bfloat16)
             level_ref[rows, :] = jnp.broadcast_to(top + jnp.log2(total), (count, HD))
             continue
         if not begins:
@@ -375,24 +368,14 @@
         name="pack",
     )(core[None], video_proj, audio_proj, video_gains, audio_gains)
     packed = lax.all_gather(packed, "tp", axis=0)
-    def norm(for_queries, shape):
-        return pl.pallas_call(
-            functools.partial(norm_kernel, for_queries),
-            out_shape=jax.ShapeDtypeStruct(shape + (BLOCK, GROUP), jnp.bfloat16),
-            in_specs=[whole(pltpu.SMEM)] + [whole()] * 5,
-            out_specs=whole(),
-            compiler_params=params(),
-            name="norm_queries" if for_queries else "norm_keys",
-        )(core[None], video_proj, audio_proj, video_gains, audio_gains, packed)
-
-    queries = norm(True, (NY,))
-    keyval = norm(False, (YH, zq_count, NY // YH))
-
-    full_shape = keyval.shape
-    keyval = keyval.reshape((YH * zq_count * (NY // YH),) + full_shape[3:])
-    keyval = lax.all_to_all(keyval, ("yh", "zq", "aud"), split_axis=0, concat_axis=0)
-    queries = lax.all_to_all(queries, ring, split_axis=0, concat_axis=0)
-    queries = lax.all_gather(queries, "x", axis=0)
+    blocks = pl.pallas_call(
+        norm_kernel,
+        out_shape=jax.ShapeDtypeStruct((NY, 2 * BLOCK, GROUP), jnp.bfloat16),
+        in_specs=[whole(pltpu.SMEM)] + [whole()] * 5,
+        out_specs=whole(),
+        compiler_params=params(),
+        name="norm",
+    )(core[None], video_proj, audio_proj, video_gains, audio_gains, packed)
 
     x_index = lax.axis_index("x")
     aud_first = np.arange(NY // YH)
@@ -402,7 +385,7 @@
     def allowed(counts):
         here = counts.reshape(YH, x_count, zq_count, ZP)
         here = lax.dynamic_index_in_dim(here, x_index, 1, keepdims=False)
-        here = jnp.moveaxis(here, 2, 0)
+        here = here.transpose(2, 1, 0)
         return jnp.where(z_parity == 0, here, here[::-1])
 
     def bias(live):
@@ -431,9 +414,16 @@
         (y_index // (NY // 2), 0, (y_index % (NY // 2)) * GROUP),
         (1, 2, GROUP),
     )[0].astype(jnp.float32)
-    queries, gates, biases, keyval, places = lax.optimization_barrier(
-        (queries, gates, biases, keyval, places)
+    blocks = lax.all_to_all(blocks, ring, split_axis=0, concat_axis=0)
+    keyval, queries = blocks[:, :BLOCK], blocks[:, BLOCK:]
+    biases = [jnp.concatenate(part, axis=1) for part in zip(*biases)]
+    keyval, queries, gates, biases, places = lax.optimization_barrier(
+        (keyval, queries, gates, biases, places)
     )
+    keyval = lax.all_gather(keyval, "zq", axis=0, tiled=True)
+    keyval, queries = lax.optimization_barrier((keyval, queries))
+    queries = lax.all_gather(queries, "x", axis=0)
+    full_shape = (zq_count, YH, NY // YH, BLOCK, GROUP)
 
     ways = [
         (z * 2 + c, (z + 1 - 2 * c) % (ZP * zq_count) * 2 + c)
@@ -443,7 +433,10 @@
     swap = [(0, 1), (1, 0)]
     far = lax.ppermute(keyval, ("zq", "zp", "tp"), ways)
     keyval_other = lax.ppermute(keyval, "tp", swap)
+    far, queries = lax.optimization_barrier((far, queries))
+    far_other = lax.ppermute(far, "tp", swap)
     near = [keyval.reshape(full_shape), keyval_other.reshape(full_shape)]
+    far = [far.reshape(full_shape), far_other.reshape(full_shape)]
 
     def attend(keyvals, video_bias, audio_bias, state, ends):
         parities = len(keyvals) // 2
@@ -480,11 +473,7 @@
             name="attend_near" if not ends else "attend",
         )(core[None], queries, *keyvals, video_bias, audio_bias, *state)
 
-    state = attend(near, *biases[0], (), False)
-    far, *state = lax.optimization_barrier((far, *state))
-    far_other = lax.ppermute(far, "tp", swap)
-    far = [far.reshape(full_shape), far_other.reshape(full_shape)]
-    partial = attend(far, *biases[1], state, True)
+    partial = attend(near + far, *biases, (), True)
     partial = lax.all_to_all(partial, "x", split_axis=0, concat_axis=0)
     back = pl.pallas_call(
         combine_kernel,

time: 134 us -> 130 us (0.970)
  blocking collectives: 59.3 us -> 81.7 us
  waiting for transfers between devices: 30.1 us -> 14.9 us
  starting transfers between devices: 21.7 us -> 14.6 us
  Pallas kernels: 18.6 us -> 14.8 us
    all_gather x0 -> x1, blocking collectives: none -> 23.5 us  [shards(): keyval = lax.all_gather(keyval, 'zq', axis=0, tiled=True)]
    all_to_all x2 -> x1, waiting for transfers between devices: 21 us -> 12.7 us  [shards(): blocks = lax.all_to_all(blocks, ring, split_axis=0, concat_axis=0)]
    all_to_all x2 -> x1, starting transfers between devices: 11.2 us -> 3.48 us  [shards(): blocks = lax.all_to_all(blocks, ring, split_axis=0, concat_axis=0)]
    ppermute x1, waiting for transfers between devices: 6.63 us -> 0.01 us  [shards(): far = lax.ppermute(keyval, ('zq', 'zp', 'tp'), ways)]
    ppermute x1, starting transfers between devices: 1.92 us -> 5.32 us  [shards(): far = lax.ppermute(keyval, ('zq', 'zp', 'tp'), ways)]
    pallas_call x2 -> x1, Pallas kernels: 12.3 us -> 9.47 us  [attend(): pl.pallas_call(functools.partial(attend_kernel, parities, not state, ends...]
    ppermute x1, starting transfers between devices: 4.61 us -> 2.34 us  [shards(): keyval_other = lax.ppermute(keyval, 'tp', swap)]
  transfers between devices with their start and end apart: 5 -> 4, of which waited for: 5 -> 2; matrix products, arithmetic and copies ran while one was open for 1% -> 1% of each run, Pallas kernels for 5% -> 0%
where the time goes in v4:
time: 130 us; the launch traced here: 129 us
  blocking collectives  81.7 us (63%)
  waiting for transfers between devices  14.9 us (11%)
  Pallas kernels  14.8 us (11%)
  starting transfers between devices  14.6 us (11%)
  between operations  1.58 us (1%)
  local copies, waits for them, and re-layouts  1.36 us (1%)
    all_gather x1, blocking collectives, shards(): keyval = lax.all_gather(keyval, 'zq', axis=0, tiled=True)  23.5 us
    all_to_all x1, blocking collectives, shards(): partial = lax.all_to_all(partial, 'x', split_axis=0, concat_axis=0)  19.1 us
    all_gather x1, blocking collectives, shards(): queries = lax.all_gather(queries, 'x', axis=0)  13.3 us
    all_to_all x1, waiting for transfers between devices, shards(): blocks = lax.all_to_all(blocks, ring, split_axis=0, concat_axis=0)  12.7 us
    all_to_all x1, blocking collectives, shards(): back = lax.all_to_all(back, ring, split_axis=0, concat_axis=0)  10.6 us
    pallas_call x1, Pallas kernels, attend(): pl.pallas_call(functools.partial(attend_kernel, parities, not state, ends...  9.47 us
    all_gather x1, blocking collectives, shards(): packed = lax.all_gather(packed, 'tp', axis=0)  9.07 us
    ppermute x1, starting transfers between devices, shards(): far = lax.ppermute(keyval, ('zq', 'zp', 'tp'), ways)  5.32 us
  transfers between devices with their start and end apart: 4, of which 2 were waited for; matrix products, arithmetic and copies ran while one was open for 1% of the time, Pallas kernels for 0%

profile of v4, /device:TPU:1, one launch (start us, length us, event | category | flops | bytes accessed | tf_op | source)
XLA Modules:
  0.0 129.4 jit_solution(15641438176042408186)
XLA Ops:
  0.7 1.9 %pack.1 = bf16[128,1536]{1,0:T(8,128)(2,1)} custom-call(s32[1]{0:T(128)} %bitcast.core_ref, bf16[4,32,1536]{2,1,0:T(8,128)(2,1)} %video_ref.3, bf16[4,8,1536]{2,1,0:T(8,128)(2,1)} %audio_ref.3, f32[3,1536]{1,0:T(4,128)} %video_gains_ref.3, f32[3,1536]{1,0:T(4,128)} %audio_gains_ref.3), custom_call_target="tpu_custom_call" | custom-call | tf_op jit(solution)/shard_map/pack/pallas_call | solution.py:355
  2.6 9.1 %all-gather = bf16[256,1536]{1,0:T(8,128)(2,1)S(1)} all-gather(bf16[128,1536]{1,0:T(8,128)(2,1)} %pack.1), channel_id=2, replica_groups=mesh['yh'=2,'x'=4,'zq'=4,'zp'=2,'aud'=4,'tp'=2] {'tp'}, dimensions={0}, use_global_device_ids=true | all-gather | bytes 1179648 | tf_op jit(solution)/shard_map/all_gather | solution.py:370
  11.7 1.2 norm.1
  12.9 3.5 %all-to-all-start = ((bf16[8,80,384]{2,1,0:T(8,128)(2,1)}), bf16[8,80,384]{2,1,0:T(8,128)(2,1)S(1)}, u32[]{:S(2)}, u32[]{:S(2)}) async-start(bf16[8,80,384]{2,1,0:T(8,128)(2,1)} %norm.1), calls=%async_computation | async-start | bytes 983040 | tf_op jit(solution)/shard_map/all_to_all | solution.py:417
  16.6 0.1 reshape.197
  16.7 0.1 reshape.198
  16.9 0.1 copy.28
  17.0 0.1 copy.25
  17.1 0.1 copy.27
  17.2 0.1 copy.26
  17.4 0.1 copy.30
  17.5 0.1 copy.29
  17.5 0.1 compare_select_fusion.1
  17.6 0.1 compare_select_fusion.3
  18.4 0.1 select_n.110
  18.5 0.1 select_n.112
  18.6 0.1 select_n.105
  18.7 0.1 select_n.107
  18.8 1.9 %all-gather.4 = bf16[2,2,1536]{2,1,0:T(2,128)(2,1)S(1)} all-gather(bf16[1,2,1536]{2,1,0:T(2,128)(2,1)S(1)} %bitcast.39), channel_id=3, replica_groups=mesh['yh'=2,'x'=4,'zq'=4,'zp'=2,'aud'=4,'tp'=2] {'tp'}, dimensions={0}, use_global_device_ids=true | all-gather | bytes 18432 | tf_op jit(solution)/shard_map/all_gather | solution.py:411
  20.8 12.7 %all-to-all-done = bf16[8,80,384]{2,1,0:T(8,128)(2,1)S(1)} async-done(((bf16[8,80,384]{2,1,0:T(8,128)(2,1)}), bf16[8,80,384]{2,1,0:T(8,128)(2,1)S(1)}, u32[]{:S(2)}, u32[]{:S(2)}) %all-to-all-start) | async-done | bytes 491552 | tf_op jit(solution)/shard_map/all_to_all | solution.py:417
  33.6 23.5 %all_gather.31 = bf16[32,40,384]{2,1,0:T(8,128)(2,1)S(1)} all-gather(bf16[8,40,384]{2,1,0:T(8,128)(2,1)S(1)} %get-tuple-element.15), channel_id=1, replica_groups=mesh['yh'=2,'x'=4,'zq'=4,'zp'=2,'aud'=4,'tp'=2] {'zq'}, dimensions={0}, use_global_device_ids=true | all-gather | bytes 1228800 | tf_op jit(solution)/shard_map/all_gather | solution.py:423
  57.1 5.3 %collective-permute-start = (bf16[32,40,384]{2,1,0:T(8,128)(2,1)S(1)}, bf16[32,40,384]{2,1,0:T(8,128)(2,1)S(1)}, u32[]{:S(2)}, u32[]{:S(2)}) collective-permute-start(bf16[32,40,384]{2,1,0:T(8,128)(2,1)S(1)} %all_gather.31), channel_id=1, source_target_pairs={{0,8},{1,57},{8,16},{9,1},{16,24},{17,9},{24,32},{25,17},{32,40},{... | collective-permute-start | bytes 2949128 | tf_op jit(solution)/shard_map/ppermute | solution.py:434
  62.4 2.3 %collective-permute-start.1 = (bf16[32,40,384]{2,1,0:T(8,128)(2,1)S(1)}, bf16[32,40,384]{2,1,0:T(8,128)(2,1)S(1)}, u32[]{:S(2)}, u32[]{:S(2)}) collective-permute-start(bf16[32,40,384]{2,1,0:T(8,128)(2,1)S(1)} %all_gather.31), channel_id=1, source_target_pairs={{0,1},{1,0},{2,3},{3,2},{4,5},{5,4},{6,7},{7,6},{8,9},{9,8},{10,11... | collective-permute-start | bytes 2949128 | tf_op jit(solution)/shard_map/ppermute | solution.py:435
  64.8 13.3 %all-gather.2 = bf16[32,40,384]{2,1,0:T(8,128)(2,1)S(1)} all-gather(bf16[8,40,384]{2,1,0:T(8,128)(2,1)S(1)} %get-tuple-element.18), channel_id=4, replica_groups=mesh['yh'=2,'x'=4,'zq'=4,'zp'=2,'aud'=4,'tp'=2] {'x'}, dimensions={0}, use_global_device_ids=true | all-gather | bytes 1228800 | tf_op jit(solution)/shard_map/all_gather | solution.py:425
  78.1 3.5 %collective-permute-start.2 = (bf16[32,40,384]{2,1,0:T(8,128)(2,1)S(1)}, bf16[32,40,384]{2,1,0:T(8,128)(2,1)S(1)}, u32[]{:S(2)}, u32[]{:S(2)}) collective-permute-start(bf16[32,40,384]{2,1,0:T(8,128)(2,1)S(1)} %collective-permute-done), channel_id=1, source_target_pairs={{0,1},{1,0},{2,3},{3,2},{4,5},{5,4},{6,7},{7,6},{8,9},{9,8},{10,11... | collective-permute-start | bytes 2949128 | tf_op jit(solution)/shard_map/ppermute | solution.py:437
  81.6 2.2 %collective-permute-done.2 = bf16[32,40,384]{2,1,0:T(8,128)(2,1)S(1)} collective-permute-done((bf16[32,40,384]{2,1,0:T(8,128)(2,1)S(1)}, bf16[32,40,384]{2,1,0:T(8,128)(2,1)S(1)}, u32[]{:S(2)}, u32[]{:S(2)}) %collective-permute-start.2) | collective-permute-done | bytes 983072 | tf_op jit(solution)/shard_map/ppermute | solution.py:437
  83.8 9.5 %attend.1 = bf16[4,360,384]{2,1,0:T(8,128)(2,1)S(1)} custom-call(s32[1]{0:T(128)} %bitcast.core_ref, bf16[4,8,40,384]{3,2,1,0:T(8,128)(2,1)S(1)} %bitcast.33, bf16[4,2,4,40,384]{4,3,2,1,0:T(8,128)(2,1)S(1)} %bitcast.32, bf16[4,2,4,40,384]{4,3,2,1,0:T(8,128)(2,1)S(1)} %bitcast.37, bf16[4,2,4,40,384]{4,3,2,1,0:T(8,128)(2,1)S(1)} %bitcast.36, ...), custom_call_target="tpu_custom_call" | custom-call | tf_op jit(solution)/shard_map/attend/pallas_call | solution.py:459
  93.3 19.1 %all_to_all.15.part_ref = bf16[4,360,384]{2,1,0:T(8,128)(2,1)S(1)} all-to-all(bf16[4,360,384]{2,1,0:T(8,128)(2,1)S(1)} %attend.1), channel_id=1, replica_groups=mesh['yh'=2,'x'=4,'zq'=4,'zp'=2,'aud'=4,'tp'=2] {'x'}, dimensions={0} | all-to-all | bytes 2211840 | tf_op jit(solution)/shard_map/all_to_all | solution.py:477
  112.4 1.1 combine.1
  113.4 10.6 %all_to_all.16 = bf16[8,24,384]{2,1,0:T(8,128)(2,1)S(1)} all-to-all(bf16[8,24,384]{2,1,0:T(8,128)(2,1)S(1)} %combine.1), channel_id=1, replica_groups=mesh['yh'=2,'x'=4,'zq'=4,'zp'=2,'aud'=4,'tp'=2] {'yh','aud'}, dimensions={0} | all-to-all | bytes 294912 | tf_op jit(solution)/shard_map/all_to_all | solution.py:486
  124.0 4.2 %all-gather.3 = bf16[16,24,384]{2,1,0:T(8,128)(2,1)S(1)} all-gather(bf16[8,24,384]{2,1,0:T(8,128)(2,1)S(1)} %all_to_all.16), channel_id=5, replica_groups=mesh['yh'=2,'x'=4,'zq'=4,'zp'=2,'aud'=4,'tp'=2] {'tp'}, dimensions={0}, use_global_device_ids=true | all-gather | bytes 442368 | tf_op jit(solution)/shard_map/all_gather | solution.py:487
  128.2 1.2 place.1
  (35 shorter events, 0.5 us)
Async XLA Ops:
  0.6 18.2 %copy-start = (bf16[2,50,1536]{2,0,1:T(2,128)(2,1)S(1)}, bf16[2,50,1536]{2,0,1:T(2,128)(2,1)}, u32[]{:S(2)}) copy-start(bf16[2,50,1536]{2,0,1:T(2,128)(2,1)} %param.15) | copy-start | bytes 921604
  0.6 11.0 %copy-start.4 = (f32[3,1536]{1,0:T(4,128)S(1)}, f32[3,1536]{1,0:T(4,128)}, u32[]{:S(2)}) copy-start(f32[3,1536]{1,0:T(4,128)} %audio_gains_ref.3) | copy-start | bytes 55300
  0.7 11.0 %copy-start.3 = (f32[3,1536]{1,0:T(4,128)S(1)}, f32[3,1536]{1,0:T(4,128)}, u32[]{:S(2)}) copy-start(f32[3,1536]{1,0:T(4,128)} %video_gains_ref.3) | copy-start | bytes 55300
  0.7 11.0 %copy-start.2 = (bf16[4,8,1536]{2,1,0:T(8,128)(2,1)S(1)}, bf16[4,8,1536]{2,1,0:T(8,128)(2,1)}, u32[]{:S(2)}) copy-start(bf16[4,8,1536]{2,1,0:T(8,128)(2,1)} %audio_ref.3) | copy-start | bytes 294916
  0.7 11.0 %copy-start.1 = (bf16[4,32,1536]{2,1,0:T(8,128)(2,1)S(1)}, bf16[4,32,1536]{2,1,0:T(8,128)(2,1)}, u32[]{:S(2)}) copy-start(bf16[4,32,1536]{2,1,0:T(8,128)(2,1)} %video_ref.3) | copy-start | bytes 1179652
  11.7 4.9 %copy-start.6 = (s32[64]{0:T(128)S(1)}, s32[64]{0:T(128)}, u32[]{:S(2)}) copy-start(s32[64]{0:T(128)} %param.17) | copy-start | bytes 772
  11.7 5.0 %copy-start.7 = (s32[64]{0:T(128)S(1)}, s32[64]{0:T(128)}, u32[]{:S(2)}) copy-start(s32[64]{0:T(128)} %param.18) | copy-start | bytes 772
  11.7 5.9 %copy-start.5 = (s32[4,8]{1,0:T(4,128)S(1)}, s32[4,8]{1,0:T(4,128)}, u32[]{:S(2)}) copy-start(s32[4,8]{1,0:T(4,128)} %constant.84.clone) | copy-start | bytes 388
  12.9 20.7 %all-to-all-start = ((bf16[8,80,384]{2,1,0:T(8,128)(2,1)}), bf16[8,80,384]{2,1,0:T(8,128)(2,1)S(1)}, u32[]{:S(2)}, u32[]{:S(2)}) async-start(bf16[8,80,384]{2,1,0:T(8,128)(2,1)} %norm.1), calls=%async_computation | async-start | bytes 983040 | tf_op jit(solution)/shard_map/all_to_all | solution.py:417
  57.1 21.0 %collective-permute-start = (bf16[32,40,384]{2,1,0:T(8,128)(2,1)S(1)}, bf16[32,40,384]{2,1,0:T(8,128)(2,1)S(1)}, u32[]{:S(2)}, u32[]{:S(2)}) collective-permute-start(bf16[32,40,384]{2,1,0:T(8,128)(2,1)S(1)} %all_gather.31), channel_id=1, source_target_pairs={{0,8},{1,57},{8,16},{9,1},{16,24},{17,9},{24,32},{25,17},{32,40},{... | collective-permute-start | bytes 2949128 | tf_op jit(solution)/shard_map/ppermute | solution.py:434
  62.4 19.2 %collective-permute-start.1 = (bf16[32,40,384]{2,1,0:T(8,128)(2,1)S(1)}, bf16[32,40,384]{2,1,0:T(8,128)(2,1)S(1)}, u32[]{:S(2)}, u32[]{:S(2)}) collective-permute-start(bf16[32,40,384]{2,1,0:T(8,128)(2,1)S(1)} %all_gather.31), channel_id=1, source_target_pairs={{0,1},{1,0},{2,3},{3,2},{4,5},{5,4},{6,7},{7,6},{8,9},{9,8},{10,11... | collective-permute-start | bytes 2949128 | tf_op jit(solution)/shard_map/ppermute | solution.py:435
  78.1 5.7 %collective-permute-start.2 = (bf16[32,40,384]{2,1,0:T(8,128)(2,1)S(1)}, bf16[32,40,384]{2,1,0:T(8,128)(2,1)S(1)}, u32[]{:S(2)}, u32[]{:S(2)}) collective-permute-start(bf16[32,40,384]{2,1,0:T(8,128)(2,1)S(1)} %collective-permute-done), channel_id=1, source_target_pairs={{0,1},{1,0},{2,3},{3,2},{4,5},{5,4},{6,7},{7,6},{8,9},{9,8},{10,11... | collective-permute-start | bytes 2949128 | tf_op jit(solution)/shard_map/ppermute | solution.py:437

commit v5 on v4

--- a/solution.py
+++ b/solution.py
@@ -1,4 +1,3 @@
-import functools
 import math
 
 import jax
@@ -27,7 +26,10 @@
 AROWS = 4
 BLOCK = 2 * VROWS + 2 * AROWS
 OUT_ROWS = 2 * (VTOK_DEV + ATOK_DEV)
-STAT_ROWS = OUT_ROWS // 8
+STAT_FIELDS = 4
+STATS_PER_ROW = HD // STAT_FIELDS
+STAT_USED = OUT_ROWS // STATS_PER_ROW
+STAT_ROWS = 16
 BACK_ROWS = VROWS + 8
 AUDIO_ROW = 4 * VROWS
 SMALL_ROW = AUDIO_ROW + 4 * 2 * AROWS
@@ -141,10 +143,15 @@
     spread(BLOCK + 2 * VROWS, mixed)
 
 
-def attend_kernel(parities, begins, ends, core_ref, query_ref, *refs):
+def stat_places():
+    shape = (1, STATS_PER_ROW // 8, 8, HD)
+    tile, row, lane = (lax.broadcasted_iota(jnp.int32, shape, i) for i in (1, 2, 3))
+    return lane // STAT_FIELDS == tile * 8 + row, lane % STAT_FIELDS
+
+
+def attend_kernel(core_ref, query_ref, *refs):
     x_count = query_ref.shape[0]
-    keyval_refs = refs[: 2 * parities]
-    video_bias_ref, audio_bias_ref, *rest = refs[2 * parities :]
+    *keyval_refs, video_bias_ref, audio_bias_ref, out_ref = refs
     holds_keys = core_ref[0] == 0
 
     def rows_of(ref, first, last):
@@ -168,13 +175,10 @@
                 jnp.where(holds_keys, other, own).astype(jnp.bfloat16),
             )
         )
-    lane = lax.broadcasted_iota(jnp.int32, (1, 8, HD), 2)
-    row = lax.broadcasted_iota(jnp.int32, (1, 8, HD), 1)
-    in_row = lane // 16 == row
-    field = lane % 16
-
-    def attend(queries, pieces, bias_ref, state):
-        first = 0
+    in_place, field = stat_places()
+
+    def attend(queries, pieces, bias_ref):
+        state, first = None, 0
         for key, value in pieces:
             keys = slice(first, first + key.shape[0])
             first = keys.stop
@@ -187,7 +191,7 @@
             if state is not None:
                 top = jnp.maximum(top, state[0])
             weights = jnp.exp2(scores - top)
-            total = jnp.sum(weights, axis=1, keepdims=True)
+            total = sum(weights[:, i : i + HD] for i in range(0, weights.shape[1], HD))
             sums = jnp.dot(
                 weights.astype(jnp.bfloat16), value, preferred_element_type=jnp.float32
             )
@@ -196,22 +200,23 @@
                 total = total + state[1] * keep
                 sums = sums + state[2] * keep
             state = top, total, sums
-        return state
+        top, total, sums = state
+        return top, jnp.sum(total, axis=1, keepdims=True), sums
 
     def finish(top, total, sums):
         high = total.astype(jnp.bfloat16).astype(jnp.float32)
-        groups = top.shape[0] // 8
 
         def wide(column):
-            return jnp.broadcast_to(column, (column.shape[0], HD)).reshape(groups, 8, HD)
+            wide_column = jnp.broadcast_to(column, (column.shape[0], HD))
+            return wide_column.reshape(-1, STATS_PER_ROW // 8, 8, HD)
 
         stats = jnp.where(
             field == 0,
             wide(top),
             jnp.where(field == 1, wide(high), wide(total - high)),
         )
-        stats = jnp.sum(jnp.where(in_row & (field < 3), stats, 0.0), axis=1)
-        return (sums * pl.reciprocal(total)).astype(jnp.bfloat16), stats
+        stats = jnp.sum(jnp.where(in_place & (field < 3), stats, 0.0), axis=(1, 2))
+        return (sums * (1.0 / total)).astype(jnp.bfloat16), stats
 
     audio_rows = query_ref[:, :, 2 * VROWS :, :].astype(jnp.float32)
     audio_rows = audio_rows.reshape(x_count * NY // 2, 2, 8, HD)
@@ -227,27 +232,9 @@
     )
     pieces = (video_pieces, audio_pieces)
     biases = (video_bias_ref, audio_bias_ref)
-    count = queries[0].shape[0]
     stats = []
     for kind in range(2):
-        rows = slice(kind * count, (kind + 1) * count)
-        state = attend(queries[kind], pieces[kind], biases[kind], None)
-        top, total, sums = state
-        if not ends:
-            sums_ref, level_ref = rest
-            sums_ref[rows, :] = (sums * pl.reciprocal(total)).astype(jnp.bfloat16)
-            level_ref[rows, :] = jnp.broadcast_to(top + jnp.log2(total), (count, HD))
-            continue
-        if not begins:
-            old_sums_ref, old_level_ref, _ = rest
-            old_level = old_level_ref[rows, :]
-            new_top = jnp.maximum(top, old_level.astype(jnp.bfloat16).astype(jnp.float32))
-            keep, old_share = jnp.exp2(top - new_top), jnp.exp2(old_level - new_top)
-            total = total * keep + old_share
-            sums = sums * keep + old_sums_ref[rows, :].astype(jnp.float32) * old_share
-            state = new_top, total, sums
-        out_ref = rest[-1]
-        rows, stat = finish(*state)
+        rows, stat = finish(*attend(queries[kind], pieces[kind], biases[kind]))
         stats.append(stat)
         start = kind * (VTOK_DEV + ATOK_DEV)
         for x in range(x_count):
@@ -257,9 +244,7 @@
             out_ref[x, start + VTOK_DEV : start + VTOK_DEV + ATOK_DEV, :] = rows[
                 first : first + ATOK_DEV
             ]
-    if not ends:
-        return
-    wide_stat, narrow_stat = VTOK_DEV // 8, ATOK_DEV // 8
+    wide_stat, narrow_stat = VTOK_DEV // STATS_PER_ROW, ATOK_DEV // STATS_PER_ROW
     for x in range(x_count):
         picked = []
         for stat in stats:
@@ -267,15 +252,14 @@
             picked.append(stat[first : first + wide_stat])
             first = x_count * wide_stat + x * narrow_stat
             picked.append(stat[first : first + narrow_stat])
+        picked.append(jnp.zeros((STAT_ROWS - STAT_USED, HD), jnp.float32))
         out_ref[x, OUT_ROWS:, :] = jnp.concatenate(picked, axis=0).astype(jnp.bfloat16)
 
 
 def combine_kernel(part_ref, gate_ref, out_ref):
     parts = part_ref.shape[0]
-    lane = lax.broadcasted_iota(jnp.int32, (1, 8, HD), 2)
-    row = lax.broadcasted_iota(jnp.int32, (1, 8, HD), 1)
-    in_row = lane // 16 == row
-    source = lax.broadcasted_iota(jnp.int32, (HD, 2 * HD), 0) % 16
+    in_place, _ = stat_places()
+    source = lax.broadcasted_iota(jnp.int32, (HD, 2 * HD), 0) % STAT_FIELDS
     target = lax.broadcasted_iota(jnp.int32, (HD, 2 * HD), 1) // HD
     source = jnp.where(source < 3, (source + 1) // 2, 2)
     pick = jnp.where(source == target, 1.0, 0.0).astype(jnp.bfloat16)
@@ -284,9 +268,11 @@
         cols = slice(head * HD, (head + 1) * HD)
         tops, totals = [], []
         for part in range(parts):
-            rows = part_ref[part, OUT_ROWS:, cols].astype(jnp.float32)
-            rows = jnp.broadcast_to(rows[:, None, :], (STAT_ROWS, 8, HD))
-            rows = jnp.where(in_row, rows, 0.0).reshape(OUT_ROWS, HD)
+            rows = part_ref[part, OUT_ROWS:, cols].astype(jnp.float32)[:STAT_USED]
+            rows = jnp.broadcast_to(
+                rows[:, None, None, :], (STAT_USED, STATS_PER_ROW // 8, 8, HD)
+            )
+            rows = jnp.where(in_place, rows, 0.0).reshape(OUT_ROWS, HD)
             fields = jnp.dot(
                 rows.astype(jnp.bfloat16), pick, preferred_element_type=jnp.float32
             )
@@ -438,42 +424,23 @@
     near = [keyval.reshape(full_shape), keyval_other.reshape(full_shape)]
     far = [far.reshape(full_shape), far_other.reshape(full_shape)]
 
-    def attend(keyvals, video_bias, audio_bias, state, ends):
-        parities = len(keyvals) // 2
-        rows = 2 * x_count * (VTOK_DEV + ATOK_DEV)
-        state_spec = pl.BlockSpec((rows, HD), lambda h: (0, h))
-        if ends:
-            out_shape = jax.ShapeDtypeStruct(
-                (x_count, OUT_ROWS + STAT_ROWS, GROUP), jnp.bfloat16
-            )
-            out_specs = pl.BlockSpec(
-                (x_count, OUT_ROWS + STAT_ROWS, HD), lambda h: (0, 0, h)
-            )
-        else:
-            out_shape = tuple(
-                jax.ShapeDtypeStruct((rows, GROUP), dtype)
-                for dtype in (jnp.bfloat16, jnp.float32)
-            )
-            out_specs = (state_spec,) * 2
-        keyval_spec = pl.BlockSpec(full_shape[:-1] + (HD,), lambda h: (0, 0, 0, 0, h))
-        return pl.pallas_call(
-            functools.partial(attend_kernel, parities, not state, ends),
-            grid=(HEADS_HERE,),
-            out_shape=out_shape,
-            in_specs=[
-                whole(pltpu.SMEM),
-                pl.BlockSpec((x_count, NY, BLOCK, HD), lambda h: (0, 0, 0, h)),
-                *[keyval_spec] * len(keyvals),
-                pl.BlockSpec(video_bias.shape, lambda h: (0, 0)),
-                pl.BlockSpec(audio_bias.shape, lambda h: (0, 0)),
-                *[state_spec] * len(state),
-            ],
-            out_specs=out_specs,
-            compiler_params=params(),
-            name="attend_near" if not ends else "attend",
-        )(core[None], queries, *keyvals, video_bias, audio_bias, *state)
-
-    partial = attend(near + far, *biases, (), True)
+    keyval_spec = pl.BlockSpec(full_shape[:-1] + (HD,), lambda h: (0, 0, 0, 0, h))
+    partial = pl.pallas_call(
+        attend_kernel,
+        grid=(HEADS_HERE,),
+        out_shape=jax.ShapeDtypeStruct(
+            (x_count, OUT_ROWS + STAT_ROWS, GROUP), jnp.bfloat16
+        ),
+        in_specs=[
+            whole(pltpu.SMEM),
+            pl.BlockSpec((x_count, NY, BLOCK, HD), lambda h: (0, 0, 0, h)),
+            *[keyval_spec] * 4,
+            *[pl.BlockSpec(bias.shape, lambda h: (0, 0)) for bias in biases],
+        ],
+        out_specs=pl.BlockSpec((x_count, OUT_ROWS + STAT_ROWS, HD), lambda h: (0, 0, h)),
+        compiler_params=params(),
+        name="attend",
+    )(core[None], queries, *near, *far, *biases)
     partial = lax.all_to_all(partial, "x", split_axis=0, concat_axis=0)
     back = pl.pallas_call(
         combine_kernel,

time: 130 us -> 128 us (0.985)
  waiting for transfers between devices: 14.9 us -> 13.2 us
  local copies, waits for them, and re-layouts: 1.36 us -> 3.05 us
    unnamed x16, local copies, waits for them, and re-layouts: 0.05 us -> 1.74 us
    all_to_all x1, waiting for transfers between devices: 12.7 us -> 11.1 us  [shards(): blocks = lax.all_to_all(blocks, ring, split_axis=0, concat_axis=0)]
where the time goes in v5:
time: 128 us
  blocking collectives  81 us (63%)
  starting transfers between devices  14.6 us (11%)
  Pallas kernels  14 us (11%)
  waiting for transfers between devices  13.2 us (10%)
  local copies, waits for them, and re-layouts  3.05 us (2%)
  between operations  1.51 us (1%)
    all_gather x1, blocking collectives, shards(): keyval = lax.all_gather(keyval, 'zq', axis=0, tiled=True)  23.5 us
    all_to_all x1, blocking collectives, shards(): partial = lax.all_to_all(partial, 'x', split_axis=0, concat_axis=0)  18 us
    all_gather x1, blocking collectives, shards(): queries = lax.all_gather(queries, 'x', axis=0)  13.3 us
    all_to_all x1, waiting for transfers between devices, shards(): blocks = lax.all_to_all(blocks, ring, split_axis=0, concat_axis=0)  11.1 us
    all_to_all x1, blocking collectives, shards(): back = lax.all_to_all(back, ring, split_axis=0, concat_axis=0)  10.5 us
    all_gather x1, blocking collectives, shards(): packed = lax.all_gather(packed, 'tp', axis=0)  9.22 us
    pallas_call x1, Pallas kernels, shards(): pl.pallas_call(attend_kernel, grid=(HEADS_HERE,), out_shape=jax.ShapeDtyp...  8.66 us
    ppermute x1, starting transfers between devices, shards(): far = lax.ppermute(keyval, ('zq', 'zp', 'tp'), ways)  5.32 us
  transfers between devices with their start and end apart: 4, of which 2 were waited for; matrix products, arithmetic and copies ran while one was open for 1% of the time, Pallas kernels for 0%

profile of v5, /device:TPU:1, one launch (start us, length us, event | category | flops | bytes accessed | tf_op | source)
XLA Modules:
  0.0 127.9 jit_solution(9576991850437606882)
XLA Ops:
  0.6 1.9 %pack.1 = bf16[128,1536]{1,0:T(8,128)(2,1)} custom-call(s32[1]{0:T(128)} %bitcast.core_ref, bf16[4,32,1536]{2,1,0:T(8,128)(2,1)} %video_ref.3, bf16[4,8,1536]{2,1,0:T(8,128)(2,1)} %audio_ref.3, f32[3,1536]{1,0:T(4,128)} %video_gains_ref.3, f32[3,1536]{1,0:T(4,128)} %audio_gains_ref.3), custom_call_target="tpu_custom_call" | custom-call | tf_op jit(solution)/shard_map/pack/pallas_call | solution.py:341
  2.5 9.2 %all-gather = bf16[256,1536]{1,0:T(8,128)(2,1)S(1)} all-gather(bf16[128,1536]{1,0:T(8,128)(2,1)} %pack.1), channel_id=2, replica_groups=mesh['yh'=2,'x'=4,'zq'=4,'zp'=2,'aud'=4,'tp'=2] {'tp'}, dimensions={0}, use_global_device_ids=true | all-gather | bytes 1179648 | tf_op jit(solution)/shard_map/all_gather | solution.py:356
  11.8 1.2 norm.1
  12.9 3.5 %all-to-all-start = ((bf16[8,80,384]{2,1,0:T(8,128)(2,1)}), bf16[8,80,384]{2,1,0:T(8,128)(2,1)S(1)}, u32[]{:S(2)}, u32[]{:S(2)}) async-start(bf16[8,80,384]{2,1,0:T(8,128)(2,1)} %norm.1), calls=%async_computation | async-start | bytes 983040 | tf_op jit(solution)/shard_map/all_to_all | solution.py:403
  16.7 0.6 copy-done.6
  17.3 0.1 reshape.197
  17.4 0.5 copy-done.7
  17.9 0.1 reshape.198
  18.1 0.1 copy.28
  18.1 0.1 copy.25
  18.3 0.1 copy.27
  18.4 0.1 copy.26
  18.5 0.1 copy.30
  18.6 0.1 copy.29
  18.8 0.6 copy-done.5
  20.3 0.1 select_n.112
  20.4 0.1 select_n.105
  20.5 0.1 select_n.107
  20.6 1.9 %all-gather.4 = bf16[2,2,1536]{2,1,0:T(2,128)(2,1)S(1)} all-gather(bf16[1,2,1536]{2,1,0:T(2,128)(2,1)S(1)} %bitcast.39), channel_id=3, replica_groups=mesh['yh'=2,'x'=4,'zq'=4,'zp'=2,'aud'=4,'tp'=2] {'tp'}, dimensions={0}, use_global_device_ids=true | all-gather | bytes 18432 | tf_op jit(solution)/shard_map/all_gather | solution.py:397
  22.6 11.1 %all-to-all-done = bf16[8,80,384]{2,1,0:T(8,128)(2,1)S(1)} async-done(((bf16[8,80,384]{2,1,0:T(8,128)(2,1)}), bf16[8,80,384]{2,1,0:T(8,128)(2,1)S(1)}, u32[]{:S(2)}, u32[]{:S(2)}) %all-to-all-start) | async-done | bytes 491552 | tf_op jit(solution)/shard_map/all_to_all | solution.py:403
  33.7 23.5 %all_gather.31 = bf16[32,40,384]{2,1,0:T(8,128)(2,1)S(1)} all-gather(bf16[8,40,384]{2,1,0:T(8,128)(2,1)S(1)} %get-tuple-element.15), channel_id=1, replica_groups=mesh['yh'=2,'x'=4,'zq'=4,'zp'=2,'aud'=4,'tp'=2] {'zq'}, dimensions={0}, use_global_device_ids=true | all-gather | bytes 1228800 | tf_op jit(solution)/shard_map/all_gather | solution.py:409
  57.2 5.3 %collective-permute-start = (bf16[32,40,384]{2,1,0:T(8,128)(2,1)S(1)}, bf16[32,40,384]{2,1,0:T(8,128)(2,1)S(1)}, u32[]{:S(2)}, u32[]{:S(2)}) collective-permute-start(bf16[32,40,384]{2,1,0:T(8,128)(2,1)S(1)} %all_gather.31), channel_id=1, source_target_pairs={{0,8},{1,57},{8,16},{9,1},{16,24},{17,9},{24,32},{25,17},{32,40},{... | collective-permute-start | bytes 2949128 | tf_op jit(solution)/shard_map/ppermute | solution.py:420
  62.5 2.3 %collective-permute-start.1 = (bf16[32,40,384]{2,1,0:T(8,128)(2,1)S(1)}, bf16[32,40,384]{2,1,0:T(8,128)(2,1)S(1)}, u32[]{:S(2)}, u32[]{:S(2)}) collective-permute-start(bf16[32,40,384]{2,1,0:T(8,128)(2,1)S(1)} %all_gather.31), channel_id=1, source_target_pairs={{0,1},{1,0},{2,3},{3,2},{4,5},{5,4},{6,7},{7,6},{8,9},{9,8},{10,11... | collective-permute-start | bytes 2949128 | tf_op jit(solution)/shard_map/ppermute | solution.py:421
  64.8 13.3 %all-gather.2 = bf16[32,40,384]{2,1,0:T(8,128)(2,1)S(1)} all-gather(bf16[8,40,384]{2,1,0:T(8,128)(2,1)S(1)} %get-tuple-element.18), channel_id=4, replica_groups=mesh['yh'=2,'x'=4,'zq'=4,'zp'=2,'aud'=4,'tp'=2] {'x'}, dimensions={0}, use_global_device_ids=true | all-gather | bytes 1228800 | tf_op jit(solution)/shard_map/all_gather | solution.py:411
  78.2 3.5 %collective-permute-start.2 = (bf16[32,40,384]{2,1,0:T(8,128)(2,1)S(1)}, bf16[32,40,384]{2,1,0:T(8,128)(2,1)S(1)}, u32[]{:S(2)}, u32[]{:S(2)}) collective-permute-start(bf16[32,40,384]{2,1,0:T(8,128)(2,1)S(1)} %collective-permute-done), channel_id=1, source_target_pairs={{0,1},{1,0},{2,3},{3,2},{4,5},{5,4},{6,7},{7,6},{8,9},{9,8},{10,11... | collective-permute-start | bytes 2949128 | tf_op jit(solution)/shard_map/ppermute | solution.py:423
  81.7 2.2 %collective-permute-done.2 = bf16[32,40,384]{2,1,0:T(8,128)(2,1)S(1)} collective-permute-done((bf16[32,40,384]{2,1,0:T(8,128)(2,1)S(1)}, bf16[32,40,384]{2,1,0:T(8,128)(2,1)S(1)}, u32[]{:S(2)}, u32[]{:S(2)}) %collective-permute-start.2) | collective-permute-done | bytes 983072 | tf_op jit(solution)/shard_map/ppermute | solution.py:423
  83.8 8.7 %attend.1 = bf16[4,336,384]{2,1,0:T(8,128)(2,1)S(1)} custom-call(s32[1]{0:T(128)} %bitcast.core_ref, bf16[4,8,40,384]{3,2,1,0:T(8,128)(2,1)S(1)} %bitcast.33, bf16[4,2,4,40,384]{4,3,2,1,0:T(8,128)(2,1)S(1)} %bitcast.32, bf16[4,2,4,40,384]{4,3,2,1,0:T(8,128)(2,1)S(1)} %bitcast.37, bf16[4,2,4,40,384]{4,3,2,1,0:T(8,128)(2,1)S(1)} %bitcast.36, ...), custom_call_target="tpu_custom_call" | custom-call | tf_op jit(solution)/shard_map/attend/pallas_call | solution.py:428
  92.5 18.0 %all_to_all.15.part_ref = bf16[4,336,384]{2,1,0:T(8,128)(2,1)S(1)} all-to-all(bf16[4,336,384]{2,1,0:T(8,128)(2,1)S(1)} %attend.1), channel_id=1, replica_groups=mesh['yh'=2,'x'=4,'zq'=4,'zp'=2,'aud'=4,'tp'=2] {'x'}, dimensions={0} | all-to-all | bytes 2064384 | tf_op jit(solution)/shard_map/all_to_all | solution.py:444
  110.6 1.1 combine.1
  111.7 10.5 %all_to_all.16 = bf16[8,24,384]{2,1,0:T(8,128)(2,1)S(1)} all-to-all(bf16[8,24,384]{2,1,0:T(8,128)(2,1)S(1)} %combine.1), channel_id=1, replica_groups=mesh['yh'=2,'x'=4,'zq'=4,'zp'=2,'aud'=4,'tp'=2] {'yh','aud'}, dimensions={0} | all-to-all | bytes 294912 | tf_op jit(solution)/shard_map/all_to_all | solution.py:453
  122.2 4.6 %all-gather.3 = bf16[16,24,384]{2,1,0:T(8,128)(2,1)S(1)} all-gather(bf16[8,24,384]{2,1,0:T(8,128)(2,1)S(1)} %all_to_all.16), channel_id=5, replica_groups=mesh['yh'=2,'x'=4,'zq'=4,'zp'=2,'aud'=4,'tp'=2] {'tp'}, dimensions={0}, use_global_device_ids=true | all-gather | bytes 442368 | tf_op jit(solution)/shard_map/all_gather | solution.py:454
  126.7 1.2 place.1
  (35 shorter events, 0.8 us)
Async XLA Ops:
  0.6 19.9 %copy-start = (bf16[2,50,1536]{2,0,1:T(2,128)(2,1)S(1)}, bf16[2,50,1536]{2,0,1:T(2,128)(2,1)}, u32[]{:S(2)}) copy-start(bf16[2,50,1536]{2,0,1:T(2,128)(2,1)} %param.15) | copy-start | bytes 921604
  2.5 9.2 %copy-start.1 = (bf16[4,32,1536]{2,1,0:T(8,128)(2,1)S(1)}, bf16[4,32,1536]{2,1,0:T(8,128)(2,1)}, u32[]{:S(2)}) copy-start(bf16[4,32,1536]{2,1,0:T(8,128)(2,1)} %video_ref.3) | copy-start | bytes 1179652
  2.5 9.2 %copy-start.2 = (bf16[4,8,1536]{2,1,0:T(8,128)(2,1)S(1)}, bf16[4,8,1536]{2,1,0:T(8,128)(2,1)}, u32[]{:S(2)}) copy-start(bf16[4,8,1536]{2,1,0:T(8,128)(2,1)} %audio_ref.3) | copy-start | bytes 294916
  2.5 9.2 %copy-start.3 = (f32[3,1536]{1,0:T(4,128)S(1)}, f32[3,1536]{1,0:T(4,128)}, u32[]{:S(2)}) copy-start(f32[3,1536]{1,0:T(4,128)} %video_gains_ref.3) | copy-start | bytes 55300
  2.5 9.2 %copy-start.4 = (f32[3,1536]{1,0:T(4,128)S(1)}, f32[3,1536]{1,0:T(4,128)}, u32[]{:S(2)}) copy-start(f32[3,1536]{1,0:T(4,128)} %audio_gains_ref.3) | copy-start | bytes 55300
  12.9 20.7 %all-to-all-start = ((bf16[8,80,384]{2,1,0:T(8,128)(2,1)}), bf16[8,80,384]{2,1,0:T(8,128)(2,1)S(1)}, u32[]{:S(2)}, u32[]{:S(2)}) async-start(bf16[8,80,384]{2,1,0:T(8,128)(2,1)} %norm.1), calls=%async_computation | async-start | bytes 983040 | tf_op jit(solution)/shard_map/all_to_all | solution.py:403
  16.6 0.7 copy-start.6
  17.3 0.7 copy-start.7
  18.7 0.7 copy-start.5
  57.2 21.0 %collective-permute-start = (bf16[32,40,384]{2,1,0:T(8,128)(2,1)S(1)}, bf16[32,40,384]{2,1,0:T(8,128)(2,1)S(1)}, u32[]{:S(2)}, u32[]{:S(2)}) collective-permute-start(bf16[32,40,384]{2,1,0:T(8,128)(2,1)S(1)} %all_gather.31), channel_id=1, source_target_pairs={{0,8},{1,57},{8,16},{9,1},{16,24},{17,9},{24,32},{25,17},{32,40},{... | collective-permute-start | bytes 2949128 | tf_op jit(solution)/shard_map/ppermute | solution.py:420
  62.5 19.2 %collective-permute-start.1 = (bf16[32,40,384]{2,1,0:T(8,128)(2,1)S(1)}, bf16[32,40,384]{2,1,0:T(8,128)(2,1)S(1)}, u32[]{:S(2)}, u32[]{:S(2)}) collective-permute-start(bf16[32,40,384]{2,1,0:T(8,128)(2,1)S(1)} %all_gather.31), channel_id=1, source_target_pairs={{0,1},{1,0},{2,3},{3,2},{4,5},{5,4},{6,7},{7,6},{8,9},{9,8},{10,11... | collective-permute-start | bytes 2949128 | tf_op jit(solution)/shard_map/ppermute | solution.py:421
  78.2 5.7 %collective-permute-start.2 = (bf16[32,40,384]{2,1,0:T(8,128)(2,1)S(1)}, bf16[32,40,384]{2,1,0:T(8,128)(2,1)S(1)}, u32[]{:S(2)}, u32[]{:S(2)}) collective-permute-start(bf16[32,40,384]{2,1,0:T(8,128)(2,1)S(1)} %collective-permute-done), channel_id=1, source_target_pairs={{0,1},{1,0},{2,3},{3,2},{4,5},{5,4},{6,7},{7,6},{8,9},{9,8},{10,11... | collective-permute-start | bytes 2949128 | tf_op jit(solution)/shard_map/ppermute | solution.py:423

commit v6 on v5

--- a/solution.py
+++ b/solution.py
@@ -17,10 +17,10 @@
 MASKED = -1e30
 
 YH = 2
-NY = 8
-ZP = 2
-ZQ = 4
-GROUP = D // NY
+AH = 2
+AL = 2
+RING = 8
+GROUP = D // RING
 HEADS_HERE = GROUP // HD
 VROWS = 16
 AROWS = 4
@@ -86,7 +86,7 @@
         return [jnp.where(at_zero, own, other), jnp.where(at_zero, other, own)]
 
     gains = ordered(own_gains, other_gains[:6])
-    half_groups = NY // 2
+    half_groups = RING // 2
 
     def normed(halves, gain_row, extra):
         total = sum(jnp.sum(v * v, axis=1, keepdims=True) for v in halves)
@@ -98,7 +98,7 @@
 
     def spread(row, halves):
         count = halves[0].shape[0]
-        for group in range(NY):
+        for group in range(RING):
             col = (group % half_groups) * GROUP
             out_ref[group, row : row + count, :] = halves[group // half_groups][
                 :, col : col + GROUP
@@ -219,7 +219,7 @@
         return (sums * (1.0 / total)).astype(jnp.bfloat16), stats
 
     audio_rows = query_ref[:, :, 2 * VROWS :, :].astype(jnp.float32)
-    audio_rows = audio_rows.reshape(x_count * NY // 2, 2, 8, HD)
+    audio_rows = audio_rows.reshape(x_count * RING // 2, 2, 8, HD)
     even, odd = audio_rows[:, 0], audio_rows[:, 1]
     low = low_rows(even.shape)
     audio_self = jnp.where(low, even, swap_halves(odd)).reshape(-1, HD).astype(jnp.bfloat16)
@@ -289,8 +289,8 @@
         )
         video = merged[:VTOK_DEV] + gate_ref[0:1, cols] * merged[tokens : tokens + VTOK_DEV]
         audio = merged[tokens + VTOK_DEV :] + gate_ref[1:2, cols] * merged[VTOK_DEV:tokens]
-        out_ref[:, :VROWS, cols] = video.reshape(NY, VROWS, HD).astype(jnp.bfloat16)
-        for pair in range(NY // 2):
+        out_ref[:, :VROWS, cols] = video.reshape(RING, VROWS, HD).astype(jnp.bfloat16)
+        for pair in range(RING // 2):
             rows = audio[pair * 8 : pair * 8 + 8].astype(jnp.bfloat16)
             out_ref[2 * pair, VROWS:, cols] = rows
             out_ref[2 * pair + 1, VROWS:, cols] = rows
@@ -299,7 +299,7 @@
 def place_kernel(place_ref, back_ref, video_ref, audio_ref):
     core = place_ref[0]
     odd = place_ref[1]
-    half_groups = NY // 2
+    half_groups = RING // 2
     for j in range(half_groups):
         group = core * half_groups + j
         cols = slice(j * GROUP, (j + 1) * GROUP)
@@ -333,11 +333,9 @@
     audio_counts,
 ):
     core = lax.axis_index("tp")
-    ring = ("yh", "aud")
     x_count = lax.axis_size("x")
-    zq_count = lax.axis_size("zq")
-    z_parity = lax.axis_index("zp")
-    y_index = lax.axis_index(ring)
+    z_index = lax.axis_index("z")
+    parity = lax.axis_index("al")
     packed = pl.pallas_call(
         pack_kernel,
         grid=(1,),
@@ -356,7 +354,7 @@
     packed = lax.all_gather(packed, "tp", axis=0)
     blocks = pl.pallas_call(
         norm_kernel,
-        out_shape=jax.ShapeDtypeStruct((NY, 2 * BLOCK, GROUP), jnp.bfloat16),
+        out_shape=jax.ShapeDtypeStruct((RING, 2 * BLOCK, GROUP), jnp.bfloat16),
         in_specs=[whole(pltpu.SMEM)] + [whole()] * 5,
         out_specs=whole(),
         compiler_params=params(),
@@ -364,60 +362,57 @@
     )(core[None], video_proj, audio_proj, video_gains, audio_gains, packed)
 
     x_index = lax.axis_index("x")
-    aud_first = np.arange(NY // YH)
-    parities = jnp.stack([z_parity, 1 - z_parity])
     halves = jnp.stack([core, 1 - core])
 
     def allowed(counts):
-        here = counts.reshape(YH, x_count, zq_count, ZP)
-        here = lax.dynamic_index_in_dim(here, x_index, 1, keepdims=False)
-        here = here.transpose(2, 1, 0)
-        return jnp.where(z_parity == 0, here, here[::-1])
+        here = counts.reshape(YH, x_count, RING)
+        return lax.dynamic_index_in_dim(here, x_index, 1, keepdims=False)
 
     def bias(live):
         return jnp.where(live, 0.0, MASKED).astype(jnp.float32).reshape(1, -1)
 
-    video_first = (
-        aud_first[None, :, None] * (2 * VROWS)
-        + halves[:, None, None] * VROWS
-        + np.arange(VROWS)[None, None, :]
-    )
-    audio_first = aud_first[:, None] * 8 + np.arange(8)[None, :]
     allowed_video, allowed_audio = allowed(video_counts), allowed(audio_counts)
-    biases = [
-        (
-            bias(video_first[:, None, None] < allowed_video[parity][None, :, :, None, None]),
-            bias(audio_first < allowed_audio[parity][..., None, None]),
-        )
-        for parity in range(ZP)
-    ]
-    places = jnp.stack([core, y_index % 2])
+    biases = []
+    for al in (parity, 1 - parity):
+        aud = np.arange(AH) * AL + al
+        video_first = (
+            aud[None, :, None] * (2 * VROWS)
+            + halves[:, None, None] * VROWS
+            + np.arange(VROWS)[None, None, :]
+        )
+        audio_first = aud[:, None] * 8 + np.arange(8)[None, :]
+        biases.append(
+            (
+                bias(video_first[:, None, :, None, :] < allowed_video[None, :, None, :, None]),
+                bias(audio_first[None, :, None, :] < allowed_audio[:, None, :, None]),
+            )
+        )
+    places = jnp.stack([core, z_index % 2])
     gates = lax.dynamic_index_in_dim(cross_gates, timestep[0], 1, keepdims=False)
     gates, packed = lax.optimization_barrier((gates, packed))
     gates = lax.all_gather(gates, "tp", axis=0)
     gates = lax.dynamic_slice(
         gates,
-        (y_index // (NY // 2), 0, (y_index % (NY // 2)) * GROUP),
+        (z_index // (RING // 2), 0, (z_index % (RING // 2)) * GROUP),
         (1, 2, GROUP),
     )[0].astype(jnp.float32)
-    blocks = lax.all_to_all(blocks, ring, split_axis=0, concat_axis=0)
+    blocks = lax.all_to_all(blocks, "z", split_axis=0, concat_axis=0)
     keyval, queries = blocks[:, :BLOCK], blocks[:, BLOCK:]
     biases = [jnp.concatenate(part, axis=1) for part in zip(*biases)]
     keyval, queries, gates, biases, places = lax.optimization_barrier(
         (keyval, queries, gates, biases, places)
     )
-    keyval = lax.all_gather(keyval, "zq", axis=0, tiled=True)
+    keyval = lax.all_gather(keyval, ("yh", "ah"), axis=0, tiled=True)
     keyval, queries = lax.optimization_barrier((keyval, queries))
     queries = lax.all_gather(queries, "x", axis=0)
-    full_shape = (zq_count, YH, NY // YH, BLOCK, GROUP)
-
+    full_shape = (YH, AH, RING, BLOCK, GROUP)
+
+    y_count = YH * AH * AL
     ways = [
-        (z * 2 + c, (z + 1 - 2 * c) % (ZP * zq_count) * 2 + c)
-        for z in range(ZP * zq_count)
-        for c in range(2)
+        (y * 2 + c, (y + 1 - 2 * c) % y_count * 2 + c) for y in range(y_count) for c in range(2)
     ]
     swap = [(0, 1), (1, 0)]
-    far = lax.ppermute(keyval, ("zq", "zp", "tp"), ways)
+    far = lax.ppermute(keyval, ("yh", "ah", "al", "tp"), ways)
     keyval_other = lax.ppermute(keyval, "tp", swap)
     far, queries = lax.optimization_barrier((far, queries))
     far_other = lax.ppermute(far, "tp", swap)
@@ -433,7 +428,7 @@
         ),
         in_specs=[
             whole(pltpu.SMEM),
-            pl.BlockSpec((x_count, NY, BLOCK, HD), lambda h: (0, 0, 0, h)),
+            pl.BlockSpec((x_count, RING, BLOCK, HD), lambda h: (0, 0, 0, h)),
             *[keyval_spec] * 4,
             *[pl.BlockSpec(bias.shape, lambda h: (0, 0)) for bias in biases],
         ],
@@ -444,13 +439,13 @@
     partial = lax.all_to_all(partial, "x", split_axis=0, concat_axis=0)
     back = pl.pallas_call(
         combine_kernel,
-        out_shape=jax.ShapeDtypeStruct((NY, BACK_ROWS, GROUP), jnp.bfloat16),
+        out_shape=jax.ShapeDtypeStruct((RING, BACK_ROWS, GROUP), jnp.bfloat16),
         in_specs=[whole(), whole()],
         out_specs=whole(),
         compiler_params=params(),
         name="combine",
     )(partial, gates)
-    back = lax.all_to_all(back, ring, split_axis=0, concat_axis=0)
+    back = lax.all_to_all(back, "z", split_axis=0, concat_axis=0)
     back = lax.all_gather(back, "tp", axis=0)
     return pl.pallas_call(
         place_kernel,
@@ -467,9 +462,9 @@
 
 def solution(mesh):
     vid = mesh.devices.shape[0]
-    cut = (YH, vid // (YH * ZQ * ZP), ZQ, ZP)
-    axes = ("yh", "x", "zq", "zp", "aud", "tp")
-    fine = Mesh(mesh.devices.reshape(cut + mesh.devices.shape[1:]), axes)
+    cut = (YH, vid // (YH * RING), RING, AH, AL, 2)
+    axes = ("yh", "x", "z", "ah", "al", "tp")
+    fine = Mesh(mesh.devices.reshape(cut), axes)
     tokens = axes[:-1]
     in_specs = (
         P(None, tokens, "tp"),

time: 128 us -> 127 us (level)
  local copies, waits for them, and re-layouts: 3.05 us -> 1.76 us
    ppermute x1, starting transfers between devices: 5.32 us -> 2.16 us  [shards(): far = lax.ppermute(keyval, ('yh', 'ah', 'al', 'tp'), ways)]
    ppermute x1, starting transfers between devices: 2.34 us -> 4.53 us  [shards(): keyval_other = lax.ppermute(keyval, 'tp', swap)]
where the time goes in v6:
time: 127 us
  blocking collectives  80.2 us (63%)
  starting transfers between devices  14.7 us (12%)
  waiting for transfers between devices  14.2 us (11%)
  Pallas kernels  14 us (11%)
  local copies, waits for them, and re-layouts  1.76 us (1%)
  between operations  1.43 us (1%)
    all_gather x1, blocking collectives, shards(): keyval = lax.all_gather(keyval, ('yh', 'ah'), axis=0, tiled=True)  22.3 us
    all_to_all x1, blocking collectives, shards(): partial = lax.all_to_all(partial, 'x', split_axis=0, concat_axis=0)  17.9 us
    all_gather x1, blocking collectives, shards(): queries = lax.all_gather(queries, 'x', axis=0)  13.5 us
    all_to_all x1, waiting for transfers between devices, shards(): blocks = lax.all_to_all(blocks, 'z', split_axis=0, concat_axis=0)  12 us
    all_to_all x1, blocking collectives, shards(): back = lax.all_to_all(back, 'z', split_axis=0, concat_axis=0)  10.5 us
    all_gather x1, blocking collectives, shards(): packed = lax.all_gather(packed, 'tp', axis=0)  9.22 us
    pallas_call x1, Pallas kernels, shards(): pl.pallas_call(attend_kernel, grid=(HEADS_HERE,), out_shape=jax.ShapeDtyp...  8.66 us
    all_to_all x1, starting transfers between devices, shards(): blocks = lax.all_to_all(blocks, 'z', split_axis=0, concat_axis=0)  4.66 us
  transfers between devices with their start and end apart: 4, of which 2 were waited for; matrix products, arithmetic and copies ran while one was open for 1% of the time, Pallas kernels for 0%

profile of v6, /device:TPU:1, one launch (start us, length us, event | category | flops | bytes accessed | tf_op | source)
XLA Modules:
  0.0 126.9 jit_solution(5923783742966269809)
XLA Ops:
  0.6 1.9 %pack.1 = bf16[128,1536]{1,0:T(8,128)(2,1)} custom-call(s32[1]{0:T(128)} %bitcast.core_ref, bf16[4,32,1536]{2,1,0:T(8,128)(2,1)} %video_ref.3, bf16[4,8,1536]{2,1,0:T(8,128)(2,1)} %audio_ref.3, f32[3,1536]{1,0:T(4,128)} %video_gains_ref.3, f32[3,1536]{1,0:T(4,128)} %audio_gains_ref.3), custom_call_target="tpu_custom_call" | custom-call | tf_op jit(solution)/shard_map/pack/pallas_call | solution.py:339
  2.5 9.2 %all-gather = bf16[256,1536]{1,0:T(8,128)(2,1)S(1)} all-gather(bf16[128,1536]{1,0:T(8,128)(2,1)} %pack.1), channel_id=2, replica_groups=mesh['yh'=2,'x'=4,'z'=8,'ah'=2,'al'=2,'tp'=2] {'tp'}, dimensions={0}, use_global_device_ids=true | all-gather | bytes 1179648 | tf_op jit(solution)/shard_map/all_gather | solution.py:354
  11.8 1.2 norm.1
  12.9 4.7 %all-to-all-start = ((bf16[8,80,384]{2,1,0:T(8,128)(2,1)}), bf16[8,80,384]{2,1,0:T(8,128)(2,1)S(1)}, u32[]{:S(2)}, u32[]{:S(2)}) async-start(bf16[8,80,384]{2,1,0:T(8,128)(2,1)} %norm.1), calls=%async_computation | async-start | bytes 983040 | tf_op jit(solution)/shard_map/all_to_all | solution.py:399
  17.6 0.1 add_multiply_fusion
  17.8 0.1 iota_add_fusion.2
  17.9 0.1 iota_add_fusion.1
  18.1 0.6 copy-done.5
  18.7 0.1 reshape.282
  18.7 0.6 copy-done.6
  19.3 0.1 reshape.283
  19.4 0.1 compare_select_fusion.1
  19.5 0.1 compare_select_fusion.3
  20.2 0.1 select_n.95
  20.3 0.1 select_n.97
  20.4 0.1 select_n.91
  20.5 0.1 select_n.93
  20.6 2.1 %all-gather.4 = bf16[2,2,1536]{2,1,0:T(2,128)(2,1)S(1)} all-gather(bf16[1,2,1536]{2,1,0:T(2,128)(2,1)S(1)} %bitcast.37), channel_id=3, replica_groups=mesh['yh'=2,'x'=4,'z'=8,'ah'=2,'al'=2,'tp'=2] {'tp'}, dimensions={0}, use_global_device_ids=true | all-gather | bytes 18432 | tf_op jit(solution)/shard_map/all_gather | solution.py:393
  22.8 0.1 pad_add_fusion.place_ref
  22.8 12.0 %all-to-all-done = bf16[8,80,384]{2,1,0:T(8,128)(2,1)S(1)} async-done(((bf16[8,80,384]{2,1,0:T(8,128)(2,1)}), bf16[8,80,384]{2,1,0:T(8,128)(2,1)S(1)}, u32[]{:S(2)}, u32[]{:S(2)}) %all-to-all-start) | async-done | bytes 491552 | tf_op jit(solution)/shard_map/all_to_all | solution.py:399
  34.9 22.3 %all_gather.31 = bf16[32,40,384]{2,1,0:T(8,128)(2,1)S(1)} all-gather(bf16[8,40,384]{2,1,0:T(8,128)(2,1)S(1)} %get-tuple-element.15), channel_id=1, replica_groups=mesh['yh'=2,'x'=4,'z'=8,'ah'=2,'al'=2,'tp'=2] {'yh','ah'}, dimensions={0}, use_global_device_ids=true | all-gather | bytes 1228800 | tf_op jit(solution)/shard_map/all_gather | solution.py:405
  57.2 2.2 %collective-permute-start = (bf16[32,40,384]{2,1,0:T(8,128)(2,1)S(1)}, bf16[32,40,384]{2,1,0:T(8,128)(2,1)S(1)}, u32[]{:S(2)}, u32[]{:S(2)}) collective-permute-start(bf16[32,40,384]{2,1,0:T(8,128)(2,1)S(1)} %all_gather.31), channel_id=1, source_target_pairs={{0,2},{1,263},{2,4},{3,1},{4,6},{5,3},{6,256},{7,5},{256,258},{257... | collective-permute-start | bytes 2949128 | tf_op jit(solution)/shard_map/ppermute | solution.py:415
  59.4 4.5 %collective-permute-start.1 = (bf16[32,40,384]{2,1,0:T(8,128)(2,1)S(1)}, bf16[32,40,384]{2,1,0:T(8,128)(2,1)S(1)}, u32[]{:S(2)}, u32[]{:S(2)}) collective-permute-start(bf16[32,40,384]{2,1,0:T(8,128)(2,1)S(1)} %all_gather.31), channel_id=1, source_target_pairs={{0,1},{1,0},{2,3},{3,2},{4,5},{5,4},{6,7},{7,6},{8,9},{9,8},{10,11... | collective-permute-start | bytes 2949128 | tf_op jit(solution)/shard_map/ppermute | solution.py:416
  63.9 13.5 %all-gather.2 = bf16[32,40,384]{2,1,0:T(8,128)(2,1)S(1)} all-gather(bf16[8,40,384]{2,1,0:T(8,128)(2,1)S(1)} %get-tuple-element.18), channel_id=4, replica_groups=mesh['yh'=2,'x'=4,'z'=8,'ah'=2,'al'=2,'tp'=2] {'x'}, dimensions={0}, use_global_device_ids=true | all-gather | bytes 1228800 | tf_op jit(solution)/shard_map/all_gather | solution.py:407
  77.4 3.3 %collective-permute-start.2 = (bf16[32,40,384]{2,1,0:T(8,128)(2,1)S(1)}, bf16[32,40,384]{2,1,0:T(8,128)(2,1)S(1)}, u32[]{:S(2)}, u32[]{:S(2)}) collective-permute-start(bf16[32,40,384]{2,1,0:T(8,128)(2,1)S(1)} %collective-permute-done), channel_id=1, source_target_pairs={{0,1},{1,0},{2,3},{3,2},{4,5},{5,4},{6,7},{7,6},{8,9},{9,8},{10,11... | collective-permute-start | bytes 2949128 | tf_op jit(solution)/shard_map/ppermute | solution.py:418
  80.8 2.2 %collective-permute-done.2 = bf16[32,40,384]{2,1,0:T(8,128)(2,1)S(1)} collective-permute-done((bf16[32,40,384]{2,1,0:T(8,128)(2,1)S(1)}, bf16[32,40,384]{2,1,0:T(8,128)(2,1)S(1)}, u32[]{:S(2)}, u32[]{:S(2)}) %collective-permute-start.2) | collective-permute-done | bytes 983072 | tf_op jit(solution)/shard_map/ppermute | solution.py:418
  82.9 8.7 %attend.1 = bf16[4,336,384]{2,1,0:T(8,128)(2,1)S(1)} custom-call(s32[1]{0:T(128)} %bitcast.core_ref, bf16[4,8,40,384]{3,2,1,0:T(8,128)(2,1)S(1)} %bitcast.31, bf16[2,2,8,40,384]{4,3,2,1,0:T(8,128)(2,1)S(1)} %bitcast.30, bf16[2,2,8,40,384]{4,3,2,1,0:T(8,128)(2,1)S(1)} %bitcast.35, bf16[2,2,8,40,384]{4,3,2,1,0:T(8,128)(2,1)S(1)} %bitcast.34, ...), custom_call_target="tpu_custom_call" | custom-call | tf_op jit(solution)/shard_map/attend/pallas_call | solution.py:423
  91.6 17.9 %all_to_all.15.part_ref = bf16[4,336,384]{2,1,0:T(8,128)(2,1)S(1)} all-to-all(bf16[4,336,384]{2,1,0:T(8,128)(2,1)S(1)} %attend.1), channel_id=1, replica_groups=mesh['yh'=2,'x'=4,'z'=8,'ah'=2,'al'=2,'tp'=2] {'x'}, dimensions={0} | all-to-all | bytes 2064384 | tf_op jit(solution)/shard_map/all_to_all | solution.py:439
  109.5 1.1 combine.1
  110.6 10.5 %all_to_all.16 = bf16[8,24,384]{2,1,0:T(8,128)(2,1)S(1)} all-to-all(bf16[8,24,384]{2,1,0:T(8,128)(2,1)S(1)} %combine.1), channel_id=1, replica_groups=mesh['yh'=2,'x'=4,'z'=8,'ah'=2,'al'=2,'tp'=2] {'z'}, dimensions={0} | all-to-all | bytes 294912 | tf_op jit(solution)/shard_map/all_to_all | solution.py:448
  121.1 4.6 %all-gather.3 = bf16[16,24,384]{2,1,0:T(8,128)(2,1)S(1)} all-gather(bf16[8,24,384]{2,1,0:T(8,128)(2,1)S(1)} %all_to_all.16), channel_id=5, replica_groups=mesh['yh'=2,'x'=4,'z'=8,'ah'=2,'al'=2,'tp'=2] {'tp'}, dimensions={0}, use_global_device_ids=true | all-gather | bytes 442368 | tf_op jit(solution)/shard_map/all_gather | solution.py:449
  125.7 1.2 place.1
  (25 shorter events, 0.3 us)
Async XLA Ops:
  0.6 19.9 %copy-start = (bf16[2,50,1536]{2,0,1:T(2,128)(2,1)S(1)}, bf16[2,50,1536]{2,0,1:T(2,128)(2,1)}, u32[]{:S(2)}) copy-start(bf16[2,50,1536]{2,0,1:T(2,128)(2,1)} %param.18) | copy-start | bytes 921604
  2.5 9.2 %copy-start.1 = (bf16[4,32,1536]{2,1,0:T(8,128)(2,1)S(1)}, bf16[4,32,1536]{2,1,0:T(8,128)(2,1)}, u32[]{:S(2)}) copy-start(bf16[4,32,1536]{2,1,0:T(8,128)(2,1)} %video_ref.3) | copy-start | bytes 1179652
  2.5 9.2 %copy-start.2 = (bf16[4,8,1536]{2,1,0:T(8,128)(2,1)S(1)}, bf16[4,8,1536]{2,1,0:T(8,128)(2,1)}, u32[]{:S(2)}) copy-start(bf16[4,8,1536]{2,1,0:T(8,128)(2,1)} %audio_ref.3) | copy-start | bytes 294916
  2.5 9.2 %copy-start.3 = (f32[3,1536]{1,0:T(4,128)S(1)}, f32[3,1536]{1,0:T(4,128)}, u32[]{:S(2)}) copy-start(f32[3,1536]{1,0:T(4,128)} %video_gains_ref.3) | copy-start | bytes 55300
  2.5 9.2 %copy-start.4 = (f32[3,1536]{1,0:T(4,128)S(1)}, f32[3,1536]{1,0:T(4,128)}, u32[]{:S(2)}) copy-start(f32[3,1536]{1,0:T(4,128)} %audio_gains_ref.3) | copy-start | bytes 55300
  12.9 21.9 %all-to-all-start = ((bf16[8,80,384]{2,1,0:T(8,128)(2,1)}), bf16[8,80,384]{2,1,0:T(8,128)(2,1)S(1)}, u32[]{:S(2)}, u32[]{:S(2)}) async-start(bf16[8,80,384]{2,1,0:T(8,128)(2,1)} %norm.1), calls=%async_computation | async-start | bytes 983040 | tf_op jit(solution)/shard_map/all_to_all | solution.py:399
  18.0 0.7 copy-start.5
  18.7 0.7 copy-start.6
  57.2 20.2 %collective-permute-start = (bf16[32,40,384]{2,1,0:T(8,128)(2,1)S(1)}, bf16[32,40,384]{2,1,0:T(8,128)(2,1)S(1)}, u32[]{:S(2)}, u32[]{:S(2)}) collective-permute-start(bf16[32,40,384]{2,1,0:T(8,128)(2,1)S(1)} %all_gather.31), channel_id=1, source_target_pairs={{0,2},{1,263},{2,4},{3,1},{4,6},{5,3},{6,256},{7,5},{256,258},{257... | collective-permute-start | bytes 2949128 | tf_op jit(solution)/shard_map/ppermute | solution.py:415
  59.4 21.4 %collective-permute-start.1 = (bf16[32,40,384]{2,1,0:T(8,128)(2,1)S(1)}, bf16[32,40,384]{2,1,0:T(8,128)(2,1)S(1)}, u32[]{:S(2)}, u32[]{:S(2)}) collective-permute-start(bf16[32,40,384]{2,1,0:T(8,128)(2,1)S(1)} %all_gather.31), channel_id=1, source_target_pairs={{0,1},{1,0},{2,3},{3,2},{4,5},{5,4},{6,7},{7,6},{8,9},{9,8},{10,11... | collective-permute-start | bytes 2949128 | tf_op jit(solution)/shard_map/ppermute | solution.py:416
  77.4 5.5 %collective-permute-start.2 = (bf16[32,40,384]{2,1,0:T(8,128)(2,1)S(1)}, bf16[32,40,384]{2,1,0:T(8,128)(2,1)S(1)}, u32[]{:S(2)}, u32[]{:S(2)}) collective-permute-start(bf16[32,40,384]{2,1,0:T(8,128)(2,1)S(1)} %collective-permute-done), channel_id=1, source_target_pairs={{0,1},{1,0},{2,3},{3,2},{4,5},{5,4},{6,7},{7,6},{8,9},{9,8},{10,11... | collective-permute-start | bytes 2949128 | tf_op jit(solution)/shard_map/ppermute | solution.py:418

commit v7 on v6

--- a/solution.py
+++ b/solution.py
@@ -413,7 +413,8 @@
     ]
     swap = [(0, 1), (1, 0)]
     far = lax.ppermute(keyval, ("yh", "ah", "al", "tp"), ways)
-    keyval_other = lax.ppermute(keyval, "tp", swap)
+    near, queries = lax.optimization_barrier((keyval, queries))
+    keyval_other = lax.ppermute(near, "tp", swap)
     far, queries = lax.optimization_barrier((far, queries))
     far_other = lax.ppermute(far, "tp", swap)
     near = [keyval.reshape(full_shape), keyval_other.reshape(full_shape)]

time: 127 us -> 127 us (level)
  blocking collectives: 80.2 us -> 77.3 us
  starting transfers between devices: 14.7 us -> 16.6 us
    ppermute x1, starting transfers between devices: 4.53 us -> 7.84 us  [shards(): keyval_other = lax.ppermute(near, 'tp', swap)]
    all_gather x1, blocking collectives: 13.5 us -> 12 us  [shards(): queries = lax.all_gather(queries, 'x', axis=0)]
    ppermute x1, starting transfers between devices: 3.31 us -> 1.92 us  [shards(): far_other = lax.ppermute(far, 'tp', swap)]
  transfers between devices with their start and end apart: 4 -> 4, of which waited for: 2 -> 3; matrix products, arithmetic and copies ran while one was open for 1% -> 1% of each run, Pallas kernels for 0% -> 0%
where the time goes in v7:
time: 127 us; the launch traced here: 126 us
  blocking collectives  77.3 us (61%)
  starting transfers between devices  16.6 us (13%)
  waiting for transfers between devices  14.5 us (11%)
  Pallas kernels  14 us (11%)
  local copies, waits for them, and re-layouts  1.76 us (1%)
  between operations  1.43 us (1%)
    all_gather x1, blocking collectives, shards(): keyval = lax.all_gather(keyval, ('yh', 'ah'), axis=0, tiled=True)  22.3 us
    all_to_all x1, blocking collectives, shards(): partial = lax.all_to_all(partial, 'x', split_axis=0, concat_axis=0)  17.2 us
    all_gather x1, blocking collectives, shards(): queries = lax.all_gather(queries, 'x', axis=0)  12 us
    all_to_all x1, waiting for transfers between devices, shards(): blocks = lax.all_to_all(blocks, 'z', split_axis=0, concat_axis=0)  12 us
    all_to_all x1, blocking collectives, shards(): back = lax.all_to_all(back, 'z', split_axis=0, concat_axis=0)  10.3 us
    all_gather x1, blocking collectives, shards(): packed = lax.all_gather(packed, 'tp', axis=0)  9.22 us
    pallas_call x1, Pallas kernels, shards(): pl.pallas_call(attend_kernel, grid=(HEADS_HERE,), out_shape=jax.ShapeDtyp...  8.66 us
    ppermute x1, starting transfers between devices, shards(): keyval_other = lax.ppermute(near, 'tp', swap)  7.84 us
  transfers between devices with their start and end apart: 4, of which 3 were waited for; matrix products, arithmetic and copies ran while one was open for 1% of the time, Pallas kernels for 0%

profile of v7, /device:TPU:1, one launch (start us, length us, event | category | flops | bytes accessed | tf_op | source)
XLA Modules:
  0.0 126.3 jit_solution(15288003177618829701)
XLA Ops:
  0.6 1.9 %pack.1 = bf16[128,1536]{1,0:T(8,128)(2,1)} custom-call(s32[1]{0:T(128)} %bitcast.core_ref, bf16[4,32,1536]{2,1,0:T(8,128)(2,1)} %video_ref.3, bf16[4,8,1536]{2,1,0:T(8,128)(2,1)} %audio_ref.3, f32[3,1536]{1,0:T(4,128)} %video_gains_ref.3, f32[3,1536]{1,0:T(4,128)} %audio_gains_ref.3), custom_call_target="tpu_custom_call" | custom-call | tf_op jit(solution)/shard_map/pack/pallas_call | solution.py:339
  2.5 9.2 %all-gather = bf16[256,1536]{1,0:T(8,128)(2,1)S(1)} all-gather(bf16[128,1536]{1,0:T(8,128)(2,1)} %pack.1), channel_id=2, replica_groups=mesh['yh'=2,'x'=4,'z'=8,'ah'=2,'al'=2,'tp'=2] {'tp'}, dimensions={0}, use_global_device_ids=true | all-gather | bytes 1179648 | tf_op jit(solution)/shard_map/all_gather | solution.py:354
  11.8 1.2 norm.1
  12.9 4.7 %all-to-all-start = ((bf16[8,80,384]{2,1,0:T(8,128)(2,1)}), bf16[8,80,384]{2,1,0:T(8,128)(2,1)S(1)}, u32[]{:S(2)}, u32[]{:S(2)}) async-start(bf16[8,80,384]{2,1,0:T(8,128)(2,1)} %norm.1), calls=%async_computation | async-start | bytes 983040 | tf_op jit(solution)/shard_map/all_to_all | solution.py:399
  17.6 0.1 add_multiply_fusion
  17.8 0.1 iota_add_fusion.2
  17.9 0.1 iota_add_fusion.1
  18.1 0.6 copy-done.5
  18.7 0.1 reshape.282
  18.7 0.6 copy-done.6
  19.3 0.1 reshape.283
  19.4 0.1 compare_select_fusion.1
  20.2 0.1 select_n.95
  20.3 0.1 select_n.97
  20.4 0.1 select_n.91
  20.5 0.1 select_n.93
  20.6 2.1 %all-gather.4 = bf16[2,2,1536]{2,1,0:T(2,128)(2,1)S(1)} all-gather(bf16[1,2,1536]{2,1,0:T(2,128)(2,1)S(1)} %bitcast.37), channel_id=3, replica_groups=mesh['yh'=2,'x'=4,'z'=8,'ah'=2,'al'=2,'tp'=2] {'tp'}, dimensions={0}, use_global_device_ids=true | all-gather | bytes 18432 | tf_op jit(solution)/shard_map/all_gather | solution.py:393
  22.8 0.1 pad_add_fusion.place_ref
  22.8 12.0 %all-to-all-done = bf16[8,80,384]{2,1,0:T(8,128)(2,1)S(1)} async-done(((bf16[8,80,384]{2,1,0:T(8,128)(2,1)}), bf16[8,80,384]{2,1,0:T(8,128)(2,1)S(1)}, u32[]{:S(2)}, u32[]{:S(2)}) %all-to-all-start) | async-done | bytes 491552 | tf_op jit(solution)/shard_map/all_to_all | solution.py:399
  34.9 22.3 %all_gather.31 = bf16[32,40,384]{2,1,0:T(8,128)(2,1)S(1)} all-gather(bf16[8,40,384]{2,1,0:T(8,128)(2,1)S(1)} %get-tuple-element.17), channel_id=1, replica_groups=mesh['yh'=2,'x'=4,'z'=8,'ah'=2,'al'=2,'tp'=2] {'yh','ah'}, dimensions={0}, use_global_device_ids=true | all-gather | bytes 1228800 | tf_op jit(solution)/shard_map/all_gather | solution.py:405
  57.2 2.2 %collective-permute-start = (bf16[32,40,384]{2,1,0:T(8,128)(2,1)S(1)}, bf16[32,40,384]{2,1,0:T(8,128)(2,1)S(1)}, u32[]{:S(2)}, u32[]{:S(2)}) collective-permute-start(bf16[32,40,384]{2,1,0:T(8,128)(2,1)S(1)} %all_gather.31), channel_id=1, source_target_pairs={{0,2},{1,263},{2,4},{3,1},{4,6},{5,3},{6,256},{7,5},{256,258},{257... | collective-permute-start | bytes 2949128 | tf_op jit(solution)/shard_map/ppermute | solution.py:415
  59.4 12.0 %all-gather.2 = bf16[32,40,384]{2,1,0:T(8,128)(2,1)S(1)} all-gather(bf16[8,40,384]{2,1,0:T(8,128)(2,1)S(1)} %get-tuple-element.20), channel_id=4, replica_groups=mesh['yh'=2,'x'=4,'z'=8,'ah'=2,'al'=2,'tp'=2] {'x'}, dimensions={0}, use_global_device_ids=true | all-gather | bytes 1228800 | tf_op jit(solution)/shard_map/all_gather | solution.py:407
  71.4 7.8 %collective-permute-start.1 = (bf16[32,40,384]{2,1,0:T(8,128)(2,1)S(1)}, bf16[32,40,384]{2,1,0:T(8,128)(2,1)S(1)}, u32[]{:S(2)}, u32[]{:S(2)}) collective-permute-start(bf16[32,40,384]{2,1,0:T(8,128)(2,1)S(1)} %all_gather.31), channel_id=1, source_target_pairs={{0,1},{1,0},{2,3},{3,2},{4,5},{5,4},{6,7},{7,6},{8,9},{9,8},{10,11... | collective-permute-start | bytes 2949128 | tf_op jit(solution)/shard_map/ppermute | solution.py:417
  79.3 1.9 %collective-permute-start.2 = (bf16[32,40,384]{2,1,0:T(8,128)(2,1)S(1)}, bf16[32,40,384]{2,1,0:T(8,128)(2,1)S(1)}, u32[]{:S(2)}, u32[]{:S(2)}) collective-permute-start(bf16[32,40,384]{2,1,0:T(8,128)(2,1)S(1)} %collective-permute-done), channel_id=1, source_target_pairs={{0,1},{1,0},{2,3},{3,2},{4,5},{5,4},{6,7},{7,6},{8,9},{9,8},{10,11... | collective-permute-start | bytes 2949128 | tf_op jit(solution)/shard_map/ppermute | solution.py:419
  81.2 0.2 collective-permute-done.1
  81.5 2.3 %collective-permute-done.2 = bf16[32,40,384]{2,1,0:T(8,128)(2,1)S(1)} collective-permute-done((bf16[32,40,384]{2,1,0:T(8,128)(2,1)S(1)}, bf16[32,40,384]{2,1,0:T(8,128)(2,1)S(1)}, u32[]{:S(2)}, u32[]{:S(2)}) %collective-permute-start.2) | collective-permute-done | bytes 983072 | tf_op jit(solution)/shard_map/ppermute | solution.py:419
  83.8 8.7 %attend.1 = bf16[4,336,384]{2,1,0:T(8,128)(2,1)S(1)} custom-call(s32[1]{0:T(128)} %bitcast.core_ref, bf16[4,8,40,384]{3,2,1,0:T(8,128)(2,1)S(1)} %bitcast.31, bf16[2,2,8,40,384]{4,3,2,1,0:T(8,128)(2,1)S(1)} %bitcast.30, bf16[2,2,8,40,384]{4,3,2,1,0:T(8,128)(2,1)S(1)} %bitcast.35, bf16[2,2,8,40,384]{4,3,2,1,0:T(8,128)(2,1)S(1)} %bitcast.34, ...), custom_call_target="tpu_custom_call" | custom-call | tf_op jit(solution)/shard_map/attend/pallas_call | solution.py:424
  92.4 17.2 %all_to_all.15.part_ref = bf16[4,336,384]{2,1,0:T(8,128)(2,1)S(1)} all-to-all(bf16[4,336,384]{2,1,0:T(8,128)(2,1)S(1)} %attend.1), channel_id=1, replica_groups=mesh['yh'=2,'x'=4,'z'=8,'ah'=2,'al'=2,'tp'=2] {'x'}, dimensions={0} | all-to-all | bytes 2064384 | tf_op jit(solution)/shard_map/all_to_all | solution.py:440
  109.6 1.1 combine.1
  110.7 10.3 %all_to_all.16 = bf16[8,24,384]{2,1,0:T(8,128)(2,1)S(1)} all-to-all(bf16[8,24,384]{2,1,0:T(8,128)(2,1)S(1)} %combine.1), channel_id=1, replica_groups=mesh['yh'=2,'x'=4,'z'=8,'ah'=2,'al'=2,'tp'=2] {'z'}, dimensions={0} | all-to-all | bytes 294912 | tf_op jit(solution)/shard_map/all_to_all | solution.py:449
  121.0 4.1 %all-gather.3 = bf16[16,24,384]{2,1,0:T(8,128)(2,1)S(1)} all-gather(bf16[8,24,384]{2,1,0:T(8,128)(2,1)S(1)} %all_to_all.16), channel_id=5, replica_groups=mesh['yh'=2,'x'=4,'z'=8,'ah'=2,'al'=2,'tp'=2] {'tp'}, dimensions={0}, use_global_device_ids=true | all-gather | bytes 442368 | tf_op jit(solution)/shard_map/all_gather | solution.py:450
  125.1 1.2 place.1
  (25 shorter events, 0.4 us)
Async XLA Ops:
  0.6 19.9 %copy-start = (bf16[2,50,1536]{2,0,1:T(2,128)(2,1)S(1)}, bf16[2,50,1536]{2,0,1:T(2,128)(2,1)}, u32[]{:S(2)}) copy-start(bf16[2,50,1536]{2,0,1:T(2,128)(2,1)} %param.18) | copy-start | bytes 921604
  2.5 9.2 %copy-start.1 = (bf16[4,32,1536]{2,1,0:T(8,128)(2,1)S(1)}, bf16[4,32,1536]{2,1,0:T(8,128)(2,1)}, u32[]{:S(2)}) copy-start(bf16[4,32,1536]{2,1,0:T(8,128)(2,1)} %video_ref.3) | copy-start | bytes 1179652
  2.5 9.2 %copy-start.2 = (bf16[4,8,1536]{2,1,0:T(8,128)(2,1)S(1)}, bf16[4,8,1536]{2,1,0:T(8,128)(2,1)}, u32[]{:S(2)}) copy-start(bf16[4,8,1536]{2,1,0:T(8,128)(2,1)} %audio_ref.3) | copy-start | bytes 294916
  2.5 9.2 %copy-start.3 = (f32[3,1536]{1,0:T(4,128)S(1)}, f32[3,1536]{1,0:T(4,128)}, u32[]{:S(2)}) copy-start(f32[3,1536]{1,0:T(4,128)} %video_gains_ref.3) | copy-start | bytes 55300
  2.5 9.2 %copy-start.4 = (f32[3,1536]{1,0:T(4,128)S(1)}, f32[3,1536]{1,0:T(4,128)}, u32[]{:S(2)}) copy-start(f32[3,1536]{1,0:T(4,128)} %audio_gains_ref.3) | copy-start | bytes 55300
  12.9 21.9 %all-to-all-start = ((bf16[8,80,384]{2,1,0:T(8,128)(2,1)}), bf16[8,80,384]{2,1,0:T(8,128)(2,1)S(1)}, u32[]{:S(2)}, u32[]{:S(2)}) async-start(bf16[8,80,384]{2,1,0:T(8,128)(2,1)} %norm.1), calls=%async_computation | async-start | bytes 983040 | tf_op jit(solution)/shard_map/all_to_all | solution.py:399
  18.0 0.7 copy-start.5
  18.7 0.7 copy-start.6
  57.2 22.1 %collective-permute-start = (bf16[32,40,384]{2,1,0:T(8,128)(2,1)S(1)}, bf16[32,40,384]{2,1,0:T(8,128)(2,1)S(1)}, u32[]{:S(2)}, u32[]{:S(2)}) collective-permute-start(bf16[32,40,384]{2,1,0:T(8,128)(2,1)S(1)} %all_gather.31), channel_id=1, source_target_pairs={{0,2},{1,263},{2,4},{3,1},{4,6},{5,3},{6,256},{7,5},{256,258},{257... | collective-permute-start | bytes 2949128 | tf_op jit(solution)/shard_map/ppermute | solution.py:415
  71.4 10.0 %collective-permute-start.1 = (bf16[32,40,384]{2,1,0:T(8,128)(2,1)S(1)}, bf16[32,40,384]{2,1,0:T(8,128)(2,1)S(1)}, u32[]{:S(2)}, u32[]{:S(2)}) collective-permute-start(bf16[32,40,384]{2,1,0:T(8,128)(2,1)S(1)} %all_gather.31), channel_id=1, source_target_pairs={{0,1},{1,0},{2,3},{3,2},{4,5},{5,4},{6,7},{7,6},{8,9},{9,8},{10,11... | collective-permute-start | bytes 2949128 | tf_op jit(solution)/shard_map/ppermute | solution.py:417
  79.3 4.5 %collective-permute-start.2 = (bf16[32,40,384]{2,1,0:T(8,128)(2,1)S(1)}, bf16[32,40,384]{2,1,0:T(8,128)(2,1)S(1)}, u32[]{:S(2)}, u32[]{:S(2)}) collective-permute-start(bf16[32,40,384]{2,1,0:T(8,128)(2,1)S(1)} %collective-permute-done), channel_id=1, source_target_pairs={{0,1},{1,0},{2,3},{3,2},{4,5},{5,4},{6,7},{7,6},{8,9},{9,8},{10,11... | collective-permute-start | bytes 2949128 | tf_op jit(solution)/shard_map/ppermute | solution.py:419

commit v8 on v7

--- a/solution.py
+++ b/solution.py
@@ -34,7 +34,7 @@
 AUDIO_ROW = 4 * VROWS
 SMALL_ROW = AUDIO_ROW + 4 * 2 * AROWS
 PACK_ROWS = SMALL_ROW + 32
-KEY_STEP = 256
+KEY_STEP = 512
 SCORE_SCALE = HD ** (-0.5) * math.log2(math.e)
 VMEM_LIMIT = 48 * 1024 * 1024
 PACK_VMEM = 60 * 1024 * 1024

time: 127 us -> 127 us (level)
  no operation moved by 1% of the time
where the time goes in v8:
time: 127 us; the launch traced here: 126 us
  blocking collectives  77.3 us (61%)
  starting transfers between devices  16.6 us (13%)
  waiting for transfers between devices  14.5 us (11%)
  Pallas kernels  13.7 us (11%)
  local copies, waits for them, and re-layouts  1.76 us (1%)
  between operations  1.43 us (1%)
    all_gather x1, blocking collectives, shards(): keyval = lax.all_gather(keyval, ('yh', 'ah'), axis=0, tiled=True)  22.3 us
    all_to_all x1, blocking collectives, shards(): partial = lax.all_to_all(partial, 'x', split_axis=0, concat_axis=0)  17.2 us
    all_gather x1, blocking collectives, shards(): queries = lax.all_gather(queries, 'x', axis=0)  12 us
    all_to_all x1, waiting for transfers between devices, shards(): blocks = lax.all_to_all(blocks, 'z', split_axis=0, concat_axis=0)  12 us
    all_to_all x1, blocking collectives, shards(): back = lax.all_to_all(back, 'z', split_axis=0, concat_axis=0)  10.3 us
    all_gather x1, blocking collectives, shards(): packed = lax.all_gather(packed, 'tp', axis=0)  9.22 us
    pallas_call x1, Pallas kernels, shards(): pl.pallas_call(attend_kernel, grid=(HEADS_HERE,), out_shape=jax.ShapeDtyp...  8.42 us
    ppermute x1, starting transfers between devices, shards(): keyval_other = lax.ppermute(near, 'tp', swap)  7.84 us
  transfers between devices with their start and end apart: 4, of which 3 were waited for; matrix products, arithmetic and copies ran while one was open for 1% of the time, Pallas kernels for 0%

profile of v8, /device:TPU:1, one launch (start us, length us, event | category | flops | bytes accessed | tf_op | source)
XLA Modules:
  0.0 126.1 jit_solution(14481243634237291554)
XLA Ops:
  0.6 1.9 %pack.1 = bf16[128,1536]{1,0:T(8,128)(2,1)} custom-call(s32[1]{0:T(128)} %bitcast.core_ref, bf16[4,32,1536]{2,1,0:T(8,128)(2,1)} %video_ref.3, bf16[4,8,1536]{2,1,0:T(8,128)(2,1)} %audio_ref.3, f32[3,1536]{1,0:T(4,128)} %video_gains_ref.3, f32[3,1536]{1,0:T(4,128)} %audio_gains_ref.3), custom_call_target="tpu_custom_call" | custom-call | tf_op jit(solution)/shard_map/pack/pallas_call | solution.py:339
  2.5 9.2 %all-gather = bf16[256,1536]{1,0:T(8,128)(2,1)S(1)} all-gather(bf16[128,1536]{1,0:T(8,128)(2,1)} %pack.1), channel_id=2, replica_groups=mesh['yh'=2,'x'=4,'z'=8,'ah'=2,'al'=2,'tp'=2] {'tp'}, dimensions={0}, use_global_device_ids=true | all-gather | bytes 1179648 | tf_op jit(solution)/shard_map/all_gather | solution.py:354
  11.8 1.2 norm.1
  12.9 4.7 %all-to-all-start = ((bf16[8,80,384]{2,1,0:T(8,128)(2,1)}), bf16[8,80,384]{2,1,0:T(8,128)(2,1)S(1)}, u32[]{:S(2)}, u32[]{:S(2)}) async-start(bf16[8,80,384]{2,1,0:T(8,128)(2,1)} %norm.1), calls=%async_computation | async-start | bytes 983040 | tf_op jit(solution)/shard_map/all_to_all | solution.py:399
  17.6 0.1 add_multiply_fusion
  17.8 0.1 iota_add_fusion.2
  17.9 0.1 iota_add_fusion.1
  18.1 0.6 copy-done.5
  18.7 0.1 reshape.282
  18.7 0.6 copy-done.6
  19.3 0.1 reshape.283
  19.4 0.1 compare_select_fusion.1
  20.2 0.1 select_n.95
  20.3 0.1 select_n.97
  20.4 0.1 select_n.91
  20.5 0.1 select_n.93
  20.6 2.1 %all-gather.4 = bf16[2,2,1536]{2,1,0:T(2,128)(2,1)S(1)} all-gather(bf16[1,2,1536]{2,1,0:T(2,128)(2,1)S(1)} %bitcast.37), channel_id=3, replica_groups=mesh['yh'=2,'x'=4,'z'=8,'ah'=2,'al'=2,'tp'=2] {'tp'}, dimensions={0}, use_global_device_ids=true | all-gather | bytes 18432 | tf_op jit(solution)/shard_map/all_gather | solution.py:393
  22.8 0.1 pad_add_fusion.place_ref
  22.8 12.0 %all-to-all-done = bf16[8,80,384]{2,1,0:T(8,128)(2,1)S(1)} async-done(((bf16[8,80,384]{2,1,0:T(8,128)(2,1)}), bf16[8,80,384]{2,1,0:T(8,128)(2,1)S(1)}, u32[]{:S(2)}, u32[]{:S(2)}) %all-to-all-start) | async-done | bytes 491552 | tf_op jit(solution)/shard_map/all_to_all | solution.py:399
  34.9 22.3 %all_gather.31 = bf16[32,40,384]{2,1,0:T(8,128)(2,1)S(1)} all-gather(bf16[8,40,384]{2,1,0:T(8,128)(2,1)S(1)} %get-tuple-element.17), channel_id=1, replica_groups=mesh['yh'=2,'x'=4,'z'=8,'ah'=2,'al'=2,'tp'=2] {'yh','ah'}, dimensions={0}, use_global_device_ids=true | all-gather | bytes 1228800 | tf_op jit(solution)/shard_map/all_gather | solution.py:405
  57.2 2.2 %collective-permute-start = (bf16[32,40,384]{2,1,0:T(8,128)(2,1)S(1)}, bf16[32,40,384]{2,1,0:T(8,128)(2,1)S(1)}, u32[]{:S(2)}, u32[]{:S(2)}) collective-permute-start(bf16[32,40,384]{2,1,0:T(8,128)(2,1)S(1)} %all_gather.31), channel_id=1, source_target_pairs={{0,2},{1,263},{2,4},{3,1},{4,6},{5,3},{6,256},{7,5},{256,258},{257... | collective-permute-start | bytes 2949128 | tf_op jit(solution)/shard_map/ppermute | solution.py:415
  59.4 12.0 %all-gather.2 = bf16[32,40,384]{2,1,0:T(8,128)(2,1)S(1)} all-gather(bf16[8,40,384]{2,1,0:T(8,128)(2,1)S(1)} %get-tuple-element.20), channel_id=4, replica_groups=mesh['yh'=2,'x'=4,'z'=8,'ah'=2,'al'=2,'tp'=2] {'x'}, dimensions={0}, use_global_device_ids=true | all-gather | bytes 1228800 | tf_op jit(solution)/shard_map/all_gather | solution.py:407
  71.4 7.8 %collective-permute-start.1 = (bf16[32,40,384]{2,1,0:T(8,128)(2,1)S(1)}, bf16[32,40,384]{2,1,0:T(8,128)(2,1)S(1)}, u32[]{:S(2)}, u32[]{:S(2)}) collective-permute-start(bf16[32,40,384]{2,1,0:T(8,128)(2,1)S(1)} %all_gather.31), channel_id=1, source_target_pairs={{0,1},{1,0},{2,3},{3,2},{4,5},{5,4},{6,7},{7,6},{8,9},{9,8},{10,11... | collective-permute-start | bytes 2949128 | tf_op jit(solution)/shard_map/ppermute | solution.py:417
  79.3 1.9 %collective-permute-start.2 = (bf16[32,40,384]{2,1,0:T(8,128)(2,1)S(1)}, bf16[32,40,384]{2,1,0:T(8,128)(2,1)S(1)}, u32[]{:S(2)}, u32[]{:S(2)}) collective-permute-start(bf16[32,40,384]{2,1,0:T(8,128)(2,1)S(1)} %collective-permute-done), channel_id=1, source_target_pairs={{0,1},{1,0},{2,3},{3,2},{4,5},{5,4},{6,7},{7,6},{8,9},{9,8},{10,11... | collective-permute-start | bytes 2949128 | tf_op jit(solution)/shard_map/ppermute | solution.py:419
  81.2 0.2 collective-permute-done.1
  81.5 2.3 %collective-permute-done.2 = bf16[32,40,384]{2,1,0:T(8,128)(2,1)S(1)} collective-permute-done((bf16[32,40,384]{2,1,0:T(8,128)(2,1)S(1)}, bf16[32,40,384]{2,1,0:T(8,128)(2,1)S(1)}, u32[]{:S(2)}, u32[]{:S(2)}) %collective-permute-start.2) | collective-permute-done | bytes 983072 | tf_op jit(solution)/shard_map/ppermute | solution.py:419
  83.8 8.4 %attend.1 = bf16[4,336,384]{2,1,0:T(8,128)(2,1)S(1)} custom-call(s32[1]{0:T(128)} %bitcast.core_ref, bf16[4,8,40,384]{3,2,1,0:T(8,128)(2,1)S(1)} %bitcast.31, bf16[2,2,8,40,384]{4,3,2,1,0:T(8,128)(2,1)S(1)} %bitcast.30, bf16[2,2,8,40,384]{4,3,2,1,0:T(8,128)(2,1)S(1)} %bitcast.35, bf16[2,2,8,40,384]{4,3,2,1,0:T(8,128)(2,1)S(1)} %bitcast.34, ...), custom_call_target="tpu_custom_call" | custom-call | tf_op jit(solution)/shard_map/attend/pallas_call | solution.py:424
  92.2 17.2 %all_to_all.15.part_ref = bf16[4,336,384]{2,1,0:T(8,128)(2,1)S(1)} all-to-all(bf16[4,336,384]{2,1,0:T(8,128)(2,1)S(1)} %attend.1), channel_id=1, replica_groups=mesh['yh'=2,'x'=4,'z'=8,'ah'=2,'al'=2,'tp'=2] {'x'}, dimensions={0} | all-to-all | bytes 2064384 | tf_op jit(solution)/shard_map/all_to_all | solution.py:440
  109.4 1.1 combine.1
  110.5 10.3 %all_to_all.16 = bf16[8,24,384]{2,1,0:T(8,128)(2,1)S(1)} all-to-all(bf16[8,24,384]{2,1,0:T(8,128)(2,1)S(1)} %combine.1), channel_id=1, replica_groups=mesh['yh'=2,'x'=4,'z'=8,'ah'=2,'al'=2,'tp'=2] {'z'}, dimensions={0} | all-to-all | bytes 294912 | tf_op jit(solution)/shard_map/all_to_all | solution.py:449
  120.8 4.1 %all-gather.3 = bf16[16,24,384]{2,1,0:T(8,128)(2,1)S(1)} all-gather(bf16[8,24,384]{2,1,0:T(8,128)(2,1)S(1)} %all_to_all.16), channel_id=5, replica_groups=mesh['yh'=2,'x'=4,'z'=8,'ah'=2,'al'=2,'tp'=2] {'tp'}, dimensions={0}, use_global_device_ids=true | all-gather | bytes 442368 | tf_op jit(solution)/shard_map/all_gather | solution.py:450
  124.9 1.2 place.1
  (25 shorter events, 0.4 us)
Async XLA Ops:
  0.6 19.9 %copy-start = (bf16[2,50,1536]{2,0,1:T(2,128)(2,1)S(1)}, bf16[2,50,1536]{2,0,1:T(2,128)(2,1)}, u32[]{:S(2)}) copy-start(bf16[2,50,1536]{2,0,1:T(2,128)(2,1)} %param.18) | copy-start | bytes 921604
  2.5 9.2 %copy-start.1 = (bf16[4,32,1536]{2,1,0:T(8,128)(2,1)S(1)}, bf16[4,32,1536]{2,1,0:T(8,128)(2,1)}, u32[]{:S(2)}) copy-start(bf16[4,32,1536]{2,1,0:T(8,128)(2,1)} %video_ref.3) | copy-start | bytes 1179652
  2.5 9.2 %copy-start.2 = (bf16[4,8,1536]{2,1,0:T(8,128)(2,1)S(1)}, bf16[4,8,1536]{2,1,0:T(8,128)(2,1)}, u32[]{:S(2)}) copy-start(bf16[4,8,1536]{2,1,0:T(8,128)(2,1)} %audio_ref.3) | copy-start | bytes 294916
  2.5 9.2 %copy-start.3 = (f32[3,1536]{1,0:T(4,128)S(1)}, f32[3,1536]{1,0:T(4,128)}, u32[]{:S(2)}) copy-start(f32[3,1536]{1,0:T(4,128)} %video_gains_ref.3) | copy-start | bytes 55300
  2.5 9.2 %copy-start.4 = (f32[3,1536]{1,0:T(4,128)S(1)}, f32[3,1536]{1,0:T(4,128)}, u32[]{:S(2)}) copy-start(f32[3,1536]{1,0:T(4,128)} %audio_gains_ref.3) | copy-start | bytes 55300
  12.9 21.9 %all-to-all-start = ((bf16[8,80,384]{2,1,0:T(8,128)(2,1)}), bf16[8,80,384]{2,1,0:T(8,128)(2,1)S(1)}, u32[]{:S(2)}, u32[]{:S(2)}) async-start(bf16[8,80,384]{2,1,0:T(8,128)(2,1)} %norm.1), calls=%async_computation | async-start | bytes 983040 | tf_op jit(solution)/shard_map/all_to_all | solution.py:399
  18.0 0.7 copy-start.5
  18.7 0.7 copy-start.6
  57.2 22.1 %collective-permute-start = (bf16[32,40,384]{2,1,0:T(8,128)(2,1)S(1)}, bf16[32,40,384]{2,1,0:T(8,128)(2,1)S(1)}, u32[]{:S(2)}, u32[]{:S(2)}) collective-permute-start(bf16[32,40,384]{2,1,0:T(8,128)(2,1)S(1)} %all_gather.31), channel_id=1, source_target_pairs={{0,2},{1,263},{2,4},{3,1},{4,6},{5,3},{6,256},{7,5},{256,258},{257... | collective-permute-start | bytes 2949128 | tf_op jit(solution)/shard_map/ppermute | solution.py:415
  71.4 10.0 %collective-permute-start.1 = (bf16[32,40,384]{2,1,0:T(8,128)(2,1)S(1)}, bf16[32,40,384]{2,1,0:T(8,128)(2,1)S(1)}, u32[]{:S(2)}, u32[]{:S(2)}) collective-permute-start(bf16[32,40,384]{2,1,0:T(8,128)(2,1)S(1)} %all_gather.31), channel_id=1, source_target_pairs={{0,1},{1,0},{2,3},{3,2},{4,5},{5,4},{6,7},{7,6},{8,9},{9,8},{10,11... | collective-permute-start | bytes 2949128 | tf_op jit(solution)/shard_map/ppermute | solution.py:417
  79.3 4.5 %collective-permute-start.2 = (bf16[32,40,384]{2,1,0:T(8,128)(2,1)S(1)}, bf16[32,40,384]{2,1,0:T(8,128)(2,1)S(1)}, u32[]{:S(2)}, u32[]{:S(2)}) collective-permute-start(bf16[32,40,384]{2,1,0:T(8,128)(2,1)S(1)} %collective-permute-done), channel_id=1, source_target_pairs={{0,1},{1,0},{2,3},{3,2},{4,5},{5,4},{6,7},{7,6},{8,9},{9,8},{10,11... | collective-permute-start | bytes 2949128 | tf_op jit(solution)/shard_map/ppermute | solution.py:419
